TPU v7x, 32 devices: a whole 2x2x4 slice. The times are simulated.
32 devices in a mesh: section: 2 (over core), dp: 4 (over y, x), mp: 4 (over z).
Axes of the slice: x: 2, y: 2, z: 4, core: 2. Of those that a mesh axis runs over, the one named last changes fastest.
Arguments:
- block_input: bfloat16 [2, 1536, 2048], P(None, 'dp', 'mp'), may hold values from -6 to 6
- image_sides: int32 [2, 4, 96], P(None, 'dp'), may hold values from 0 to 7, as said below
- w_reduce: float32 [2, 2048, 512], P('section', 'mp', 'dp'), may hold values from -0.125 to 0.125
- w_spatial: float32 [2, 9, 512, 512], P('section', None, 'dp', 'mp'), may hold values from -0.09375 to 0.09375
- w_expand: float32 [2, 512, 2048], P('section', 'dp', 'mp'), may hold values from -0.25 to 0.25
- gain_inner: float32 [2, 2, 512], P('section', None, 'mp'), may hold values from 0.5 to 1.5
- shift_inner: float32 [2, 2, 512], P('section', None, 'mp'), may hold values from -1.8 to 1.8
- gain_outer: float32 [2, 2048], P('section', 'mp'), may hold values from 0.5 to 1.5
- shift_outer: float32 [2, 2048], P('section', 'mp'), may hold values from -1.8 to 1.8
- head_weight: float32 [3, 2048, 128], P(None, 'mp', ('section', 'dp')), may hold values from -0.3 to 0.3
- labels: int32 [3, 2, 1536], P(None, None, 'dp'), may hold values from 0 to 127
- thresholds: float32 [2, 1536, 2048], P(None, 'dp', 'mp'), may hold values from 0 to 1
Outputs:
- activations: bfloat16 [2, 2, 1536, 2048], P('section', None, 'dp', 'mp')
- input_grads: float32 [2, 2, 1536, 2048], P('section', None, 'dp', 'mp')
- grad_reduce: float32 [2, 2048, 512], P('section', 'mp', 'dp')
- grad_spatial: float32 [2, 9, 512, 512], P('section', None, 'dp', 'mp')
- grad_expand: float32 [2, 512, 2048], P('section', 'dp', 'mp')
- grad_gain_inner: float32 [2, 2, 4, 128], P('section', None, 'mp', 'dp')
- grad_shift_inner: float32 [2, 2, 4, 128], P('section', None, 'mp', 'dp')
- grad_gain_outer: float32 [2, 4, 512], P('section', 'mp', 'dp')
- grad_shift_outer: float32 [2, 4, 512], P('section', 'mp', 'dp')
- grad_head: float32 [3, 2048, 128], P(None, 'mp', ('section', 'dp'))
Inputs may be any that keep to these rules, and one draw needn't show every extreme that they name: `image_sides`: each nonzero entry is 7 or 2. The live pixels (sum of squared sides) of one data group in one micro-batch number at most 384, and in every micro-batch some group has exactly 384.
All inputs are finite; a program needn't handle non-finite values.
Results may differ from a plain program's by a relative error of at most 0.02.
Values may be sent and summed in bfloat16 or wider, within the bound.
A program may use at most 192 MiB of HBM per device.

v0:
```python
import jax
import jax.numpy as jnp
from jax import lax
from jax.sharding import PartitionSpec as P

NORM_EPS = 1e-05
LOSS_WEIGHT = 20.0
SIGN_FLOOR = 0.1
KEEP_TEMPER = 0.2


def shifted(value, axis, steps):
    count = lax.axis_size(axis)
    leading, last = (max(0, -steps), min(count, count - steps))
    return lax.ppermute(value, axis, [(source, source + steps) for source in range(leading, last)])


def geometry(img_sides, row_count):
    img_sizes = img_sides * img_sides
    img_ends = jnp.cumsum(img_sizes)
    img_starts = img_ends - img_sizes
    row_pos = jnp.arange(row_count, dtype=jnp.int32)[:, None]
    inside = (row_pos >= img_starts[None, :]) & (row_pos < img_ends[None, :])
    first_row = jnp.sum(jnp.where(inside, img_starts[None, :], 0), axis=1)
    side_len = jnp.sum(jnp.where(inside, img_sides[None, :], 0), axis=1)
    live_rows = jnp.any(inside, axis=1)
    offset = row_pos[:, 0] - first_row
    safe_side = jnp.maximum(side_len, 1)
    row_in = offset // safe_side
    col_in = offset % safe_side
    index_list = []
    valid_list = []
    for row_step in (-1, 0, 1):
        for col_step in (-1, 0, 1):
            new_row = row_in + row_step
            new_col = col_in + col_step
            valid = (
                live_rows
                & (new_row >= 0)
                & (new_row < side_len)
                & (new_col >= 0)
                & (new_col < side_len)
            )
            index_list.append(jnp.where(valid, first_row + new_row * side_len + new_col, 0))
            valid_list.append(valid)
    return (
        jnp.stack(index_list),
        jnp.stack(valid_list).astype(jnp.float32),
        live_rows.astype(jnp.float32),
    )


def smooth_act(values):
    return jax.nn.gelu(values, approximate=True)


def take_block(store, micro_idx):
    return lax.dynamic_index_in_dim(store, micro_idx, 0, keepdims=False)


def put_block(store, update, micro_idx, active):
    previous = take_block(store, micro_idx)
    return lax.dynamic_update_index_in_dim(store, jnp.where(active, update, previous), micro_idx, 0)


def channel_gather(values):
    return lax.all_gather(values, "mp", axis=1, tiled=True)


def channel_sum(values):
    return lax.psum_scatter(values, "mp", scatter_dimension=1, tiled=True)


def norm_stats(values, live_rows):
    masked = values * live_rows[:, None]
    total_sum, live_total = lax.psum((jnp.sum(masked, axis=0), jnp.sum(live_rows)), "dp")
    mean_val = total_sum / live_total
    centered = (values - mean_val) * live_rows[:, None]
    var_val = lax.psum(jnp.sum(centered * centered, axis=0), "dp") / live_total
    return (mean_val, lax.rsqrt(var_val + NORM_EPS), live_total)


def normalize(values, stats, live_rows, gain_vec, shift_vec):
    mean_val, inv_std, live_total = stats
    return live_rows[:, None] * (gain_vec * (values - mean_val) * inv_std + shift_vec)


def norm_backward(values, stats, live_rows, gain_vec, grad_norm):
    mean_val, inv_std, live_total = stats
    normed = (values - mean_val) * inv_std
    grad_live = grad_norm * live_rows[:, None]
    local_shift = jnp.sum(grad_live, axis=0)
    local_gain = jnp.sum(grad_live * normed, axis=0)
    sum_shift, sum_gain = lax.psum((local_shift, local_gain), "dp")
    grad_values = (
        live_rows[:, None]
        * inv_std
        * gain_vec
        * (grad_live - sum_shift / live_total - normed * sum_gain / live_total)
    )
    return (grad_values, local_gain, local_shift)


def gather_taps(values, indices, valids, tap_idx):
    return values[indices[tap_idx]] * valids[tap_idx][:, None].astype(values.dtype)


def act_backward(pre_values, grad_values):
    return jax.vjp(smooth_act, pre_values)[1](grad_values)[0]


def block_forward(x_in, layout, weights):
    indices, valids, live_rows = layout
    w_red, w_spa, w_exp, g_in, s_in, g_out, s_out = weights
    first_pre = channel_sum(jnp.dot(x_in, w_red, preferred_element_type=jnp.float32))
    stats_a = norm_stats(first_pre, live_rows)
    full_a = channel_gather(
        smooth_act(normalize(first_pre, stats_a, live_rows, g_in[0], s_in[0])).astype(jnp.bfloat16)
    )
    second_pre = jnp.zeros((x_in.shape[0], w_spa.shape[2]), jnp.float32)
    for tap_idx in range(9):
        second_pre = second_pre + jnp.dot(
            gather_taps(full_a, indices, valids, tap_idx),
            w_spa[tap_idx],
            preferred_element_type=jnp.float32,
        )
    stats_b = norm_stats(second_pre, live_rows)
    full_b = channel_gather(
        smooth_act(normalize(second_pre, stats_b, live_rows, g_in[1], s_in[1])).astype(jnp.bfloat16)
    )
    third_pre = jnp.dot(full_b, w_exp, preferred_element_type=jnp.float32)
    stats_c = norm_stats(third_pre, live_rows)
    pre_out = normalize(third_pre, stats_c, live_rows, g_out, s_out) + x_in.astype(jnp.float32)
    result = smooth_act(pre_out) * live_rows[:, None]
    return (result, (first_pre, stats_a, full_a, second_pre, stats_b, full_b, third_pre, stats_c))


def block_backward(d_out, x_in, layout, weights, saved_state):
    indices, valids, live_rows = layout
    w_red, w_spa, w_exp, g_in, s_in, g_out, s_out = weights
    first_pre, stats_a, full_a, second_pre, stats_b, full_b, third_pre, stats_c = saved_state
    pre_out = normalize(third_pre, stats_c, live_rows, g_out, s_out) + x_in.astype(jnp.float32)
    d_pre = act_backward(pre_out, d_out * live_rows[:, None])
    d_third, gain_c, shift_c = norm_backward(third_pre, stats_c, live_rows, g_out, d_pre)
    d_third = d_third.astype(jnp.bfloat16)
    grad_exp = jnp.einsum("rc,ro->co", full_b, d_third, preferred_element_type=jnp.float32)
    d_full_b = channel_sum(
        jnp.einsum("ro,co->rc", d_third, w_exp, preferred_element_type=jnp.float32)
    )
    pre_b = normalize(second_pre, stats_b, live_rows, g_in[1], s_in[1])
    d_second, gain_b, shift_b = norm_backward(
        second_pre, stats_b, live_rows, g_in[1], act_backward(pre_b, d_full_b)
    )
    d_second = d_second.astype(jnp.bfloat16)
    grad_spa = []
    back_total = jnp.zeros((x_in.shape[0], w_spa.shape[1]), jnp.float32)
    for tap_idx in range(9):
        grad_spa.append(
            jnp.einsum(
                "rc,ro->co",
                gather_taps(full_a, indices, valids, tap_idx),
                d_second,
                preferred_element_type=jnp.float32,
            )
        )
        spread = jnp.einsum(
            "ro,co->rc", d_second, w_spa[8 - tap_idx], preferred_element_type=jnp.float32
        )
        back_total = back_total + spread[indices[tap_idx]] * valids[tap_idx][:, None]
    d_full_a = channel_sum(back_total)
    pre_a = normalize(first_pre, stats_a, live_rows, g_in[0], s_in[0])
    d_first, gain_a, shift_a = norm_backward(
        first_pre, stats_a, live_rows, g_in[0], act_backward(pre_a, d_full_a)
    )
    d_first_full = channel_gather(d_first.astype(jnp.bfloat16))
    grad_red = jnp.einsum("rc,ro->co", x_in, d_first_full, preferred_element_type=jnp.float32)
    d_in = jnp.einsum("ro,co->rc", d_first_full, w_red, preferred_element_type=jnp.float32) + d_pre
    return (
        d_in,
        (
            grad_red,
            jnp.stack(grad_spa),
            grad_exp,
            jnp.stack([gain_a, gain_b]),
            jnp.stack([shift_a, shift_b]),
            gain_c,
            shift_c,
        ),
    )


def sign_merge(task_grads, thresh):
    soft_abs = jnp.sqrt(task_grads * task_grads + SIGN_FLOOR * SIGN_FLOOR) - SIGN_FLOOR
    purity = 0.5 * (1.0 + jnp.sum(task_grads, axis=0) / (jnp.sum(soft_abs, axis=0) + SIGN_FLOOR))
    keep_frac = jax.nn.sigmoid((purity - thresh) / KEEP_TEMPER)
    upper = 0.5 * jnp.sum(task_grads + soft_abs, axis=0)
    lower = 0.5 * jnp.sum(task_grads - soft_abs, axis=0)
    return keep_frac * upper + (1.0 - keep_frac) * lower


def per_device(
    block_input,
    image_sides,
    w_reduce,
    w_spatial,
    w_expand,
    gain_inner,
    shift_inner,
    gain_outer,
    shift_outer,
    head_weight,
    labels,
    thresholds,
):
    section_idx = lax.axis_index("section")
    micro_count = block_input.shape[0]
    row_count = block_input.shape[1]
    w_red, w_spa, w_exp = (
        lax.all_gather(w_reduce[0].astype(jnp.bfloat16), "dp", axis=1, tiled=True),
        lax.all_gather(w_spatial[0].astype(jnp.bfloat16), "dp", axis=1, tiled=True),
        lax.all_gather(w_expand[0].astype(jnp.bfloat16), "dp", axis=0, tiled=True),
    )
    weights = (w_red, w_spa, w_exp, gain_inner[0], shift_inner[0], gain_outer[0], shift_outer[0])
    heads_all = lax.all_gather(
        head_weight.astype(jnp.bfloat16), ("section", "dp"), axis=2, tiled=True
    )
    class_total = heads_all.shape[2]
    class_ids = jnp.arange(class_total, dtype=jnp.int32)[None, None, :]

    def layout_for(micro_idx):
        return geometry(take_block(image_sides, micro_idx)[0], row_count)

    received = jnp.zeros(block_input.shape[1:], jnp.bfloat16)
    kept_inputs = jnp.zeros(block_input.shape, jnp.bfloat16)
    activ_store = jnp.zeros(block_input.shape, jnp.bfloat16)
    cotangents = jnp.zeros(block_input.shape, jnp.float32)
    head_grad = jnp.zeros(heads_all.shape, jnp.float32)
    for turn_idx in range(micro_count + 1):
        micro_idx = jnp.clip(turn_idx - section_idx, 0, micro_count - 1)
        active = (turn_idx - section_idx >= 0) & (turn_idx - section_idx < micro_count)
        x_in = jnp.where(section_idx == 0, block_input[min(turn_idx, micro_count - 1)], received)
        layout = layout_for(micro_idx)
        live_rows = layout[2]
        result, saved_state = block_forward(x_in, layout, weights)
        result_low = result.astype(jnp.bfloat16)
        kept_inputs = put_block(kept_inputs, x_in, micro_idx, active)
        activ_store = put_block(activ_store, result_low, micro_idx, active)
        labels_now = lax.dynamic_index_in_dim(labels, micro_idx, 1, keepdims=False)
        logits = lax.psum(
            jnp.einsum("rc,tco->tro", result_low, heads_all, preferred_element_type=jnp.float32),
            "mp",
        )
        peak_val = jnp.max(logits, axis=2, keepdims=True)
        expo = jnp.exp(logits - peak_val)
        soft_p = expo / jnp.sum(expo, axis=2, keepdims=True)
        picked = (class_ids == labels_now[:, :, None]).astype(jnp.float32)
        delta_low = (LOSS_WEIGHT * live_rows[None, :, None] * (soft_p - picked)).astype(
            jnp.bfloat16
        )
        task_grads = jnp.einsum(
            "tro,tco->trc", delta_low, heads_all, preferred_element_type=jnp.float32
        )
        merged = sign_merge(task_grads, take_block(thresholds, micro_idx))
        use_head = active & (section_idx == 1)
        head_grad = head_grad + jnp.where(
            use_head,
            jnp.einsum("rc,tro->tco", result_low, delta_low, preferred_element_type=jnp.float32),
            0.0,
        )
        cotangents = put_block(cotangents, merged, micro_idx, use_head)
        received = shifted(result_low, "section", 1)
    grad_recv = jnp.zeros(block_input.shape[1:], jnp.bfloat16)
    input_store = jnp.zeros(block_input.shape, jnp.float32)
    grad_total = None
    for turn_idx in range(micro_count + 1):
        micro_idx = jnp.clip(turn_idx - 1 + section_idx, 0, micro_count - 1)
        active = (turn_idx - 1 + section_idx >= 0) & (turn_idx - 1 + section_idx < micro_count)
        d_out = jnp.where(
            section_idx == 1, take_block(cotangents, micro_idx), grad_recv.astype(jnp.float32)
        )
        x_in = take_block(kept_inputs, micro_idx)
        layout = layout_for(micro_idx)
        saved_state = block_forward(x_in, layout, weights)[1]
        d_in, grad_set = block_backward(d_out, x_in, layout, weights, saved_state)
        masked = jax.tree.map(lambda leaf: jnp.where(active, leaf, 0.0), grad_set)
        grad_total = masked if grad_total is None else jax.tree.map(jnp.add, grad_total, masked)
        d_send = d_in.astype(jnp.bfloat16)
        input_store = put_block(
            input_store,
            jnp.where(section_idx == 1, d_send.astype(jnp.float32), d_in),
            micro_idx,
            active,
        )
        grad_recv = shifted(d_send, "section", -1)
    g_red, g_spa, g_exp, g_gain_in, g_shift_in, g_gain_out, g_shift_out = grad_total
    out_red, out_spa, out_exp, out_gain_in, out_shift_in, out_gain_out, out_shift_out = (
        lax.psum_scatter(g_red[None], "dp", scatter_dimension=2, tiled=True),
        lax.psum_scatter(g_spa[None], "dp", scatter_dimension=2, tiled=True),
        lax.psum_scatter(g_exp[None], "dp", scatter_dimension=1, tiled=True),
        lax.psum_scatter(g_gain_in[None, :, None, :], "dp", scatter_dimension=3, tiled=True),
        lax.psum_scatter(g_shift_in[None, :, None, :], "dp", scatter_dimension=3, tiled=True),
        lax.psum_scatter(g_gain_out[None, None, :], "dp", scatter_dimension=2, tiled=True),
        lax.psum_scatter(g_shift_out[None, None, :], "dp", scatter_dimension=2, tiled=True),
    )
    head_out = lax.psum_scatter(head_grad, ("section", "dp"), scatter_dimension=2, tiled=True)
    return (
        activ_store[None],
        input_store[None],
        out_red,
        out_spa,
        out_exp,
        out_gain_in,
        out_shift_in,
        out_gain_out,
        out_shift_out,
        head_out,
    )


def solution(mesh):
    return jax.shard_map(
        per_device,
        mesh=mesh,
        in_specs=(
            P(None, "dp", "mp"),
            P(None, "dp", None),
            P("section", "mp", "dp"),
            P("section", None, "dp", "mp"),
            P("section", "dp", "mp"),
            P("section", None, "mp"),
            P("section", None, "mp"),
            P("section", "mp"),
            P("section", "mp"),
            P(None, "mp", ("section", "dp")),
            P(None, None, "dp"),
            P(None, "dp", "mp"),
        ),
        out_specs=(
            P("section", None, "dp", "mp"),
            P("section", None, "dp", "mp"),
            P("section", "mp", "dp"),
            P("section", None, "dp", "mp"),
            P("section", "dp", "mp"),
            P("section", None, "mp", "dp"),
            P("section", None, "mp", "dp"),
            P("section", "mp", "dp"),
            P("section", "mp", "dp"),
            P(None, "mp", ("section", "dp")),
        ),
        check_vma=False,
    )
```

profile of v0, /device:TPU:0, one launch (start us, length us, event | category | flops | bytes accessed | tf_op | source)
XLA Modules:
  0.0 1431.0 jit_solution(2382502804449613298)
XLA Ops:
  9.0 11.5 all-gather
  42.6 13.7 all-gather.2
  58.6 9.6 all-reduce.17
  69.9 8.8 psum.479
  80.5 13.6 all_gather.58
  121.1 8.9 psum.480
  130.8 8.0 psum.481
  139.6 13.3 all_gather.60
  153.4 8.9 psum.482
  163.1 8.8 psum.483
  189.5 14.5 %reduce-scatter.31.cloned.1.call-done = f32[384,128]{1,0:T(8,128)} async-done(((f32[384,512]{1,0:T(8,128)}), f32[384,128]{1,0:T(8,128)}) %reduce-scatter.31.cloned.1.call-update) | async-done | bytes 196624 | tf_op jit(solution)/shard_map/reduce_scatter | solution.py:71
  205.0 10.5 all-reduce.16
  217.2 8.0 psum.486
  226.9 13.3 all_gather.62
  268.8 9.0 psum.487
  278.6 8.0 psum.488
  287.4 13.3 all_gather.63
  302.0 9.7 psum.489
  313.7 8.0 psum.490
  367.5 23.4 %all_gather.68 = bf16[3,512,128]{1,2,0:T(8,128)(2,1)S(1)} all-gather(bf16[3,512,16]{1,2,0:T(8,128)(2,1)S(1)} %convert_element_type.768), channel_id=1, replica_groups=mesh['section'=2,'dp'=4,'mp'=4] {'section','dp'}, dimensions={2}, use_global_device_ids=true | all-gather | bytes 442368 | tf_op jit(solution)/shard_map/all_gather | solution.py:224
  401.1 11.0 all-reduce.15
  415.5 7.5 all-reduce.14
  425.6 17.9 %all_gather.64 = bf16[384,512]{1,0:T(8,128)(2,1)S(1)} all-gather(bf16[384,128]{1,0:T(8,128)(2,1)S(1)} %get-tuple-element.459), channel_id=1, replica_groups=mesh['section'=2,'dp'=4,'mp'=4] {'mp'}, dimensions={1}, use_global_device_ids=true | all-gather | bytes 491520 | tf_op jit(solution)/shard_map/all_gather | solution.py:67
  467.9 13.6 all_gather.66
  513.3 10.9 all-reduce.13
  526.9 8.5 all-reduce.12
  537.7 13.6 all_gather.67
  552.5 13.8 all_gather.65
  568.4 9.6 all-reduce.11
  579.2 13.3 all_gather.70
  624.0 8.2 all-reduce.10
  642.4 69.8 %all-reduce.20.cloned.1.call-done = (f32[3,384,128]{2,1,0:T(8,128)}, f32[3,384,128]{2,1,0:T(8,128)}, f32[3,384,128]{2,1,0:T(8,128)}) async-done(((f32[3,384,128]{2,1,0:T(8,128)}, f32[3,384,128]{2,1,0:T(8,128)}, f32[3,384,128]{2,1,0:T(8,128)}), (f32[3,384,128]{2,1,0:T(8,128)}, f32[3,384,128]{2,1,0:T(8,128)}, f32[3,384,128]{2,1,0:T(8,128)})) %all-reduce.20.cloned.1.call-update) | async-done | bytes 1769488 | tf_op jit(solution)/shard_map/psum | solution.py:249
  712.2 5.8 fusion.8
  718.0 5.8 fusion.7
  723.9 5.9 fusion.6
  738.8 10.8 all-reduce.9
  762.5 13.0 reduce-scatter.37.cloned.1.call-done
  776.8 14.3 all_gather.71
  793.1 10.5 all-reduce.8
  846.3 5.9 reduce-scatter.39.cloned.1.call-done
  854.6 14.7 %all_gather.73 = bf16[384,512]{1,0:T(8,128)(2,1)S(1)} all-gather(bf16[384,128]{1,0:T(8,128)(2,1)S(1)} %get-tuple-element.438), channel_id=1, replica_groups=mesh['section'=2,'dp'=4,'mp'=4] {'mp'}, dimensions={1}, use_global_device_ids=true | all-gather | bytes 491520 | tf_op jit(solution)/shard_map/all_gather | solution.py:67
  898.5 10.6 all-reduce.7
  912.1 13.3 all_gather.69
  933.6 8.1 all-reduce.6
  947.0 20.3 %reduce-scatter.43.cloned.1.call-done = f32[384,128]{1,0:T(8,128)} async-done(((f32[384,512]{1,0:T(8,128)}), f32[384,128]{1,0:T(8,128)}) %reduce-scatter.43.cloned.1.call-update) | async-done | bytes 196624 | tf_op jit(solution)/shard_map/reduce_scatter | solution.py:71
  968.7 14.5 %all_gather.74 = bf16[384,512]{1,0:T(8,128)(2,1)S(1)} all-gather(bf16[384,128]{1,0:T(8,128)(2,1)S(1)} %get-tuple-element.437), channel_id=1, replica_groups=mesh['section'=2,'dp'=4,'mp'=4] {'mp'}, dimensions={1}, use_global_device_ids=true | all-gather | bytes 491520 | tf_op jit(solution)/shard_map/all_gather | solution.py:67
  985.3 9.8 all-reduce.5
  1026.6 17.0 %reduce-scatter.45.cloned.1.call-done = f32[384,128]{1,0:T(8,128)} async-done(((f32[384,512]{1,0:T(8,128)}), f32[384,128]{1,0:T(8,128)}) %reduce-scatter.45.cloned.1.call-update) | async-done | bytes 196624 | tf_op jit(solution)/shard_map/reduce_scatter | solution.py:71
  1045.5 10.5 all-reduce.4
  1058.2 14.0 all_gather.72
  1080.4 7.9 all-reduce.3
  1093.2 21.0 %reduce-scatter.49.cloned.1.call-done = f32[384,128]{1,0:T(8,128)} async-done(((f32[384,512]{1,0:T(8,128)}), f32[384,128]{1,0:T(8,128)}) %reduce-scatter.49.cloned.1.call-update) | async-done | bytes 196624 | tf_op jit(solution)/shard_map/reduce_scatter | solution.py:71
  1115.4 10.1 all-reduce.2
  1153.7 4.6 convolution_select_fusion.6
  1158.4 4.7 convolution_select_fusion.7
  1165.2 9.3 reduce-scatter.51.cloned.1.call-done
  1178.0 5.2 fusion.23
  1209.1 9.8 all-reduce.1
  1220.3 14.1 all_gather.75
  1259.0 21.3 %reduce-scatter.61.cloned.1.call-done = f32[32,2]{1,0:T(8,128)} async-done(((f32[128,2]{1,0:T(8,128)}), f32[32,2]{1,0:T(8,128)}) %reduce-scatter.61.cloned.1.call-update) | async-done | bytes 272
  1281.8 37.5 %reduce-scatter.59.cloned.1.call-done = f32[3,512,16]{1,2,0:T(8,128)} async-done(((f32[3,512,128]{1,2,0:T(8,128)}), f32[3,512,16]{1,2,0:T(8,128)}) %reduce-scatter.59.cloned.1.call-update) | async-done | bytes 98320 | tf_op jit(solution)/shard_map/reduce_scatter | solution.py:305
  1319.2 31.5 %reduce-scatter.57.cloned.1.call-done = f32[1,128,512]{2,1,0:T(8,128)} async-done(((f32[1,512,512]{2,1,0:T(8,128)}), f32[1,128,512]{2,1,0:T(8,128)}) %reduce-scatter.57.cloned.1.call-update) | async-done | bytes 262160 | tf_op jit(solution)/shard_map/reduce_scatter | solution.py:299
  1350.7 31.1 %reduce-scatter.53.cloned.1.call-done = f32[1,512,128]{2,1,0:T(8,128)} async-done(((f32[1,512,512]{2,1,0:T(8,128)}), f32[1,512,128]{2,1,0:T(8,128)}) %reduce-scatter.53.cloned.1.call-update) | async-done | bytes 262160 | tf_op jit(solution)/shard_map/reduce_scatter | solution.py:297
  1381.8 41.3 %reduce-scatter.55.cloned.1.call-done = f32[1,9,128,128]{3,2,1,0:T(8,128)} async-done(((f32[1,9,512,128]{3,2,1,0:T(8,128)}), f32[1,9,128,128]{3,2,1,0:T(8,128)}) %reduce-scatter.55.cloned.1.call-update) | async-done | bytes 589840 | tf_op jit(solution)/shard_map/reduce_scatter | solution.py:298
  (1471 shorter events, 534.7 us)
Async XLA Ops:
  8.0 49.5 %reduce-scatter.29.cloned.1.call-start = ((), (), s32[]{:S(2)}) async-start(), calls=%async_computation.20 | async-start | bytes 983040 | tf_op jit(solution)/shard_map/reduce_scatter | solution.py:71
  22.9 92.9 %all-gather.5.cloned.1.call-start = ((), (), s32[]{:S(2)}) async-start(), calls=%async_computation.36 | async-start | bytes 1474560 | tf_op jit(solution)/shard_map/all_gather | solution.py:220
  23.7 180.2 %reduce-scatter.31.cloned.1.call-start = ((), (), s32[]{:S(2)}) async-start(), calls=%async_computation.21 | async-start | bytes 983040 | tf_op jit(solution)/shard_map/reduce_scatter | solution.py:71
  26.1 43.7 %copy-start.284 = (pred[384]{0:T(512)(128)(4,1)}, pred[384]{0:T(512)(128)(4,1)S(1)}, u32[]{:S(2)}) copy-start(pred[384]{0:T(512)(128)(4,1)S(1)} %fusion.474) | copy-start | bytes 1156
  26.4 43.5 %copy-start.286 = (pred[384]{0:T(512)(128)(4,1)}, pred[384]{0:T(512)(128)(4,1)S(1)}, u32[]{:S(2)}) copy-start(pred[384]{0:T(512)(128)(4,1)S(1)} %fusion.475) | copy-start | bytes 1156
  30.1 156.4 %copy-start.249 = (pred[384]{0:T(512)(128)(4,1)}, pred[384]{0:T(512)(128)(4,1)S(1)}, u32[]{:S(2)}) copy-start(pred[384]{0:T(512)(128)(4,1)S(1)} %fusion.477) | copy-start | bytes 1156
  30.3 148.3 %copy-start.252 = (pred[384]{0:T(512)(128)(4,1)}, pred[384]{0:T(512)(128)(4,1)S(1)}, u32[]{:S(2)}) copy-start(pred[384]{0:T(512)(128)(4,1)S(1)} %fusion.478) | copy-start | bytes 1156
  41.7 286.3 %copy-start.153 = (f32[384]{0:T(512)}, f32[384]{0:T(512)S(1)}, u32[]{:S(2)}) copy-start(f32[384]{0:T(512)S(1)} %get-tuple-element.66) | copy-start | bytes 4612
  41.7 286.9 %copy-start.151 = (f32[384]{0:T(512)}, f32[384]{0:T(512)S(1)}, u32[]{:S(2)}) copy-start(f32[384]{0:T(512)S(1)} %get-tuple-element.65) | copy-start | bytes 4612
  41.7 287.5 %copy-start.149 = (f32[384]{0:T(512)}, f32[384]{0:T(512)S(1)}, u32[]{:S(2)}) copy-start(f32[384]{0:T(512)S(1)} %get-tuple-element.64) | copy-start | bytes 4612
  41.7 288.0 %copy-start.147 = (f32[384]{0:T(512)}, f32[384]{0:T(512)S(1)}, u32[]{:S(2)}) copy-start(f32[384]{0:T(512)S(1)} %get-tuple-element.63) | copy-start | bytes 4612
  41.7 288.6 %copy-start.145 = (f32[384]{0:T(512)}, f32[384]{0:T(512)S(1)}, u32[]{:S(2)}) copy-start(f32[384]{0:T(512)S(1)} %get-tuple-element.62) | copy-start | bytes 4612
  41.7 289.2 %copy-start.143 = (f32[384]{0:T(512)}, f32[384]{0:T(512)S(1)}, u32[]{:S(2)}) copy-start(f32[384]{0:T(512)S(1)} %get-tuple-element.61) | copy-start | bytes 4612
  41.7 289.8 %copy-start.141 = (f32[384]{0:T(512)}, f32[384]{0:T(512)S(1)}, u32[]{:S(2)}) copy-start(f32[384]{0:T(512)S(1)} %get-tuple-element.60) | copy-start | bytes 4612
  41.7 290.3 %copy-start.139 = (f32[384]{0:T(512)}, f32[384]{0:T(512)S(1)}, u32[]{:S(2)}) copy-start(f32[384]{0:T(512)S(1)} %get-tuple-element.59) | copy-start | bytes 4612
  175.9 4.8 collective-permute-start
  182.9 216.1 %reduce-scatter.35.cloned.1.call-start = ((), (), s32[]{:S(2)}) async-start(), calls=%async_computation.23 | async-start | bytes 983040 | tf_op jit(solution)/shard_map/reduce_scatter | solution.py:71
  184.2 151.9 %copy-start.161 = (f32[384]{0:T(512)}, f32[384]{0:T(512)S(1)}, u32[]{:S(2)}) copy-start(f32[384]{0:T(512)S(1)} %get-tuple-element.52) | copy-start | bytes 4612
  184.2 152.5 %copy-start.159 = (f32[384]{0:T(512)}, f32[384]{0:T(512)S(1)}, u32[]{:S(2)}) copy-start(f32[384]{0:T(512)S(1)} %get-tuple-element.51) | copy-start | bytes 4612
  184.2 153.1 %copy-start.157 = (f32[384]{0:T(512)}, f32[384]{0:T(512)S(1)}, u32[]{:S(2)}) copy-start(f32[384]{0:T(512)S(1)} %get-tuple-element.50) | copy-start | bytes 4612
  184.2 153.7 %copy-start.155 = (f32[384]{0:T(512)}, f32[384]{0:T(512)S(1)}, u32[]{:S(2)}) copy-start(f32[384]{0:T(512)S(1)} %get-tuple-element.49) | copy-start | bytes 4612
  325.1 18.2 %collective-permute-start.1 = (bf16[384,512]{1,0:T(8,128)(2,1)}, bf16[384,512]{1,0:T(8,128)(2,1)}, u32[]{:S(2)}, u32[]{:S(2)}) collective-permute-start(bf16[384,512]{1,0:T(8,128)(2,1)} %get-tuple-element.309), channel_id=1, source_target_pairs={{0,16},{1,17},{2,18},{3,19},{4,20},{5,21},{6,22},{7,23},{8,24},{9,... | collective-permute-start | bytes 1179656 | tf_op jit(solution)/shard_map/ppermute | solution.py:15
  344.5 391.9 %copy-start.1 = (bf16[2,384,512]{2,1,0:T(8,128)(2,1)}, bf16[2,384,512]{2,1,0:T(8,128)(2,1)S(1)}, u32[]{:S(2)}) copy-start(bf16[2,384,512]{2,1,0:T(8,128)(2,1)S(1)} %get-tuple-element.302) | copy-start | bytes 2359300
  346.0 54.1 %reduce-scatter.33.cloned.1.call-start = ((), (), s32[]{:S(2)}) async-start(), calls=%async_computation.22 | async-start | bytes 983040 | tf_op jit(solution)/shard_map/reduce_scatter | solution.py:71
  356.4 169.4 %reduce-scatter.41.cloned.1.call-start = ((), (), s32[]{:S(2)}) async-start(), calls=%async_computation.26 | async-start | bytes 983040 | tf_op jit(solution)/shard_map/reduce_scatter | solution.py:71
  364.9 26.0 %copy-start.251 = (pred[384]{0:T(512)(128)(4,1)S(1)}, pred[384]{0:T(512)(128)(4,1)}, u32[]{:S(2)}) copy-start(pred[384]{0:T(512)(128)(4,1)} %copy-done.249) | copy-start | bytes 1156
  364.9 27.2 %copy-start.111 = (bf16[384,512]{1,0:T(8,128)(2,1)S(1)}, bf16[384,512]{1,0:T(8,128)(2,1)}, u32[]{:S(2)}) copy-start(bf16[384,512]{1,0:T(8,128)(2,1)} %copy-done.110) | copy-start | bytes 1179652
  366.2 272.7 %reduce-scatter.47.cloned.1.call-start = ((), (), s32[]{:S(2)}) async-start(), calls=%async_computation.29 | async-start | bytes 983040 | tf_op jit(solution)/shard_map/reduce_scatter | solution.py:71
  398.9 313.3 %all-reduce.20.cloned.1.call-start = ((), (), s32[]{:S(2)}) async-start(), calls=%async_computation.41 | async-start | bytes 3538944 | tf_op jit(solution)/shard_map/psum | solution.py:249
  513.3 37.9 %copy-start.46 = (f32[384,128]{1,0:T(8,128)}, f32[384,128]{1,0:T(8,128)S(1)}, u32[]{:S(2)}) copy-start(f32[384,128]{1,0:T(8,128)S(1)} %get-tuple-element.481) | copy-start | bytes 589828
  637.6 74.6 %copy-start.409 = (f32[384]{0:T(512)S(1)}, f32[384]{0:T(512)}, u32[]{:S(2)}) copy-start(f32[384]{0:T(512)} %get-tuple-element.468) | copy-start | bytes 4612
  637.6 137.9 %reduce-scatter.37.cloned.1.call-start = ((), (), s32[]{:S(2)}) async-start(), calls=%async_computation.24 | async-start | bytes 983040 | tf_op jit(solution)/shard_map/reduce_scatter | solution.py:71
  638.3 79.7 %copy-start.311 = (s32[3,1,384]{2,0,1:T(4,128)}, s32[3,1,384]{2,0,1:T(4,128)S(1)}, u32[]{:S(2)}) copy-start(s32[3,1,384]{2,0,1:T(4,128)S(1)} %copy.75) | copy-start | bytes 13828
  638.9 79.1 %copy-start.313 = (s32[3,384]{1,0:T(4,128)}, s32[3,384]{1,0:T(4,128)S(1)}, u32[]{:S(2)}) copy-start(s32[3,384]{1,0:T(4,128)S(1)} %get-tuple-element.518) | copy-start | bytes 13828
  638.9 85.0 %copy-start.315 = (s32[3,384]{1,0:T(4,128)}, s32[3,384]{1,0:T(4,128)S(1)}, u32[]{:S(2)}) copy-start(s32[3,384]{1,0:T(4,128)S(1)} %get-tuple-element.517) | copy-start | bytes 13828
  640.6 134.9 %copy-start.262 = (f32[128]{0:T(128)}, f32[128]{0:T(128)S(1)}, u32[]{:S(2)}) copy-start(f32[128]{0:T(128)S(1)} %broadcast_divide_fusion.15) | copy-start | bytes 1540
  754.8 97.3 %reduce-scatter.39.cloned.1.call-start = ((), (), s32[]{:S(2)}) async-start(), calls=%async_computation.25 | async-start | bytes 983040 | tf_op jit(solution)/shard_map/reduce_scatter | solution.py:71
  761.7 31.4 %copy-start.264 = (f32[128]{0:T(128)}, f32[128]{0:T(128)S(1)}, u32[]{:S(2)}) copy-start(f32[128]{0:T(128)S(1)} %broadcast_divide_fusion.12) | copy-start | bytes 1540
  762.5 28.6 %copy-start.321 = (f32[128]{0:T(128)}, f32[128]{0:T(128)S(1)}, u32[]{:S(2)}) copy-start(f32[128]{0:T(128)S(1)} %add_rsqrt_fusion.8) | copy-start | bytes 1540
  776.8 28.2 %copy-start.323 = (f32[128]{0:T(128)}, f32[128]{0:T(128)S(1)}, u32[]{:S(2)}) copy-start(f32[128]{0:T(128)S(1)} %get-tuple-element.39) | copy-start | bytes 1540
  776.8 28.2 %copy-start.325 = (f32[128]{0:T(128)}, f32[128]{0:T(128)S(1)}, u32[]{:S(2)}) copy-start(f32[128]{0:T(128)S(1)} %get-tuple-element.38) | copy-start | bytes 1540
  832.0 135.3 %reduce-scatter.43.cloned.1.call-start = ((), (), s32[]{:S(2)}) async-start(), calls=%async_computation.27 | async-start | bytes 983040 | tf_op jit(solution)/shard_map/reduce_scatter | solution.py:71
  832.8 39.0 %copy-start.231 = (s32[1024]{0:T(1024)}, s32[1024]{0:T(1024)S(1)}, u32[]{:S(2)}) copy-start(s32[1024]{0:T(1024)S(1)} %pad_clamp_fusion) | copy-start | bytes 12292
  833.5 38.4 %copy-start.233 = (s32[1024]{0:T(1024)}, s32[1024]{0:T(1024)S(1)}, u32[]{:S(2)}) copy-start(s32[1024]{0:T(1024)S(1)} %pad_clamp_fusion.1) | copy-start | bytes 12292
  898.5 68.9 %copy-start.48 = (f32[384,128]{1,0:T(8,128)}, f32[384,128]{1,0:T(8,128)S(1)}, u32[]{:S(2)}) copy-start(f32[384,128]{1,0:T(8,128)S(1)} %get-tuple-element.491) | copy-start | bytes 589828
  928.1 3.6 collective-permute-start.2
  930.1 37.3 %copy-start.270 = (f32[128]{0:T(128)}, f32[128]{0:T(128)S(1)}, u32[]{:S(2)}) copy-start(f32[128]{0:T(128)S(1)} %broadcast_divide_fusion.11) | copy-start | bytes 1540
  944.9 22.4 %copy-start.263 = (f32[128]{0:T(128)S(1)}, f32[128]{0:T(128)}, u32[]{:S(2)}) copy-start(f32[128]{0:T(128)} %copy-done.262) | copy-start | bytes 1540
  944.9 22.4 %copy-start.322 = (f32[128]{0:T(128)S(1)}, f32[128]{0:T(128)}, u32[]{:S(2)}) copy-start(f32[128]{0:T(128)} %copy-done.321) | copy-start | bytes 1540
  946.3 97.3 %reduce-scatter.45.cloned.1.call-start = ((), (), s32[]{:S(2)}) async-start(), calls=%async_computation.28 | async-start | bytes 983040 | tf_op jit(solution)/shard_map/reduce_scatter | solution.py:71
  968.7 27.0 %copy-start.329 = (f32[128]{0:T(128)}, f32[128]{0:T(128)S(1)}, u32[]{:S(2)}) copy-start(f32[128]{0:T(128)S(1)} %get-tuple-element.35) | copy-start | bytes 1540
  968.7 27.0 %copy-start.331 = (f32[128]{0:T(128)}, f32[128]{0:T(128)S(1)}, u32[]{:S(2)}) copy-start(f32[128]{0:T(128)S(1)} %get-tuple-element.34) | copy-start | bytes 1540
  1023.5 90.7 %reduce-scatter.49.cloned.1.call-start = ((), (), s32[]{:S(2)}) async-start(), calls=%async_computation.30 | async-start | bytes 983040 | tf_op jit(solution)/shard_map/reduce_scatter | solution.py:71
  1074.9 3.6 collective-permute-start.3
  1093.1 34.1 %copy-start.247 = (s32[1024]{0:T(1024)S(1)}, s32[1024]{0:T(1024)}, u32[]{:S(2)}) copy-start(s32[1024]{0:T(1024)} %pad_clamp_fusion.8) | copy-start | bytes 12292
  1093.1 81.4 %reduce-scatter.51.cloned.1.call-start = ((), (), s32[]{:S(2)}) async-start(), calls=%async_computation.31 | async-start | bytes 983040 | tf_op jit(solution)/shard_map/reduce_scatter | solution.py:71
  1153.6 98.7 %reduce-scatter.67.cloned.1.call-start = ((), (), s32[]{:S(2)}) async-start(), calls=%async_computation.40 | async-start | bytes 327680
  1164.2 89.6 %reduce-scatter.65.cloned.1.call-start = ((), (), s32[]{:S(2)}) async-start(), calls=%async_computation.39 | async-start | bytes 327680
  1165.1 92.4 %reduce-scatter.63.cloned.1.call-start = ((), (), s32[]{:S(2)}) async-start(), calls=%async_computation.38 | async-start | bytes 81920
  1177.0 103.3 %reduce-scatter.61.cloned.1.call-start = ((), (), s32[]{:S(2)}) async-start(), calls=%async_computation.37 | async-start | bytes 81920
  1178.0 141.3 %reduce-scatter.59.cloned.1.call-start = ((), (), s32[]{:S(2)}) async-start(), calls=%async_computation.35 | async-start | bytes 884736 | tf_op jit(solution)/shard_map/reduce_scatter | solution.py:305
  1183.3 167.5 %reduce-scatter.57.cloned.1.call-start = ((), (), s32[]{:S(2)}) async-start(), calls=%async_computation.34 | async-start | bytes 1310720 | tf_op jit(solution)/shard_map/reduce_scatter | solution.py:299
  1204.0 177.8 %reduce-scatter.53.cloned.1.call-start = ((), (), s32[]{:S(2)}) async-start(), calls=%async_computation.32 | async-start | bytes 1310720 | tf_op jit(solution)/shard_map/reduce_scatter | solution.py:297
  1236.4 186.7 %reduce-scatter.55.cloned.1.call-start = ((), (), s32[]{:S(2)}) async-start(), calls=%async_computation.33 | async-start | bytes 2949120 | tf_op jit(solution)/shard_map/reduce_scatter | solution.py:298
  (402 other events, 1904.1 us)
Sparse Core Ops, SparseCore 0:
  23.0 23.6 reduce-scatter.28
  183.0 20.8 reduce-scatter.30
  346.1 20.8 reduce-scatter.34
  369.1 22.5 reduce-scatter.32
  393.8 22.5 reduce-scatter.40
  418.6 28.3 reduce-scatter.46
  637.7 74.4 all-reduce.19
  754.9 20.4 reduce-scatter.36
  832.2 19.9 reduce-scatter.38
  946.4 20.8 reduce-scatter.42
  1023.6 19.9 reduce-scatter.44
  1093.2 20.9 reduce-scatter.48
  1153.8 20.7 reduce-scatter.50
  1177.4 23.3 reduce-scatter.66
  1203.4 24.0 reduce-scatter.64
  1230.3 23.6 reduce-scatter.62
  1256.5 23.7 reduce-scatter.60
  1284.2 34.9 reduce-scatter.58
  1323.0 27.7 reduce-scatter.56
  1354.0 27.7 reduce-scatter.52
  1385.7 37.3 reduce-scatter.54
Sparse Core Ops, SparseCore 1:
  25.2 30.9 all-gather.4
where the time goes:
time: 1440 us; the launch traced here: 1430 us
  blocking collectives  509 us (35%)
  waiting for transfers between devices  336 us (23%)
  local copies, waits for them, and re-layouts  238 us (17%)
  other arithmetic  185 us (13%)
  matrix products  132 us (9%)
  between operations  21.8 us (2%)
    all_gather x15, blocking collectives, channel_gather(): return lax.all_gather(values, 'mp', axis=1, tiled=True)  211 us
    gather x54, local copies, waits for them, and re-layouts, gather_taps(): values[indices[tap_idx]] * valids[tap_idx][:, None].astype(values.dtype)  139 us
    reduce_scatter x12, waiting for transfers between devices, channel_sum(): return lax.psum_scatter(values, 'mp', scatter_dimension=1, tiled=True)  101 us
    psum x9, blocking collectives, norm_stats(): lax.psum((jnp.sum(masked, axis=0), jnp.sum(live_rows)), 'dp')  88 us
    psum x9, blocking collectives, norm_backward(): sum_shift, sum_gain = lax.psum((local_shift, local_gain), 'dp')  87.9 us
    psum x9, blocking collectives, norm_stats(): var_val = lax.psum(jnp.sum(centered * centered, axis=0), 'dp') / live_total  73.8 us
    psum x1, waiting for transfers between devices, per_device(): lax.psum(jnp.einsum('rc,tco->tro', result_low, heads_all, preferred_eleme...  69.8 us
    gather x27, local copies, waits for them, and re-layouts, block_backward(): spread[indices[tap_idx]] * valids[tap_idx][:, None]  60.7 us
  transfers between devices with their start and end apart: 26, of which 15 were waited for; matrix products, arithmetic and copies ran while one was open for 22% of the time, Pallas kernels for 0%

commit v1 on v0

--- a/solution.py
+++ b/solution.py
@@ -1,6 +1,10 @@
+import math
+
 import jax
 import jax.numpy as jnp
 from jax import lax
+from jax.experimental import pallas as pl
+from jax.experimental.pallas import tpu as pltpu
 from jax.sharding import PartitionSpec as P
 
 NORM_EPS = 1e-05
@@ -198,7 +202,7 @@
     return keep_frac * upper + (1.0 - keep_frac) * lower
 
 
-def per_device(
+def plain_device(
     block_input,
     image_sides,
     w_reduce,
@@ -317,6 +321,938 @@
     )
 
 
+K0 = math.sqrt(2.0 / math.pi)
+K1 = 0.044715
+MESH = pl.DeviceIdType.MESH
+F32 = jnp.float32
+BF16 = jnp.bfloat16
+SIDES = (2, 7)
+TAPS = [(a, b) for a in (-1, 0, 1) for b in (-1, 0, 1)]
+PAD = 8
+NN = (((1,), (0,)), ((), ()))
+NT = (((1,), (1,)), ((), ()))
+TN = (((0,), (0,)), ((), ()))
+
+
+def tap_masks():
+    found = []
+    for tap_idx, (a, b) in enumerate(TAPS):
+        for side in SIDES:
+            found.append((tap_idx, a, b, side, a * side + b))
+    return found
+
+
+MASKS = tap_masks()
+
+
+def dot(left, right, dims):
+    return lax.dot_general(left, right, dims, preferred_element_type=F32)
+
+
+def gelu(v):
+    return 0.5 * v * (1.0 + jnp.tanh(K0 * v * (1.0 + K1 * v * v)))
+
+
+def gelu_grad(v):
+    sq = v * v
+    t = jnp.tanh(K0 * v * (1.0 + K1 * sq))
+    return 0.5 * (1.0 + t) + (0.5 * K0) * v * (1.0 - t * t) * (1.0 + 3.0 * K1 * sq)
+
+
+def fold(x):
+    return jnp.sum(x.reshape(x.shape[0] // 8, 8, x.shape[1]), axis=0)
+
+
+def wide(x, width):
+    times = width // x.shape[1]
+    return x if times == 1 else jnp.concatenate([x] * times, axis=1)
+
+
+def loop(total, chunk, body, init=None):
+    def one(i, carry):
+        return body(pl.ds(pl.multiple_of(i * chunk, chunk), chunk), carry)
+
+    return lax.fori_loop(0, total // chunk, one, 0 if init is None else init)
+
+
+def rows_tile(first, second, third):
+    width = first.shape[1]
+    place = lax.broadcasted_iota(jnp.int32, (8, width), 0)
+    wide_of = lambda v: jnp.broadcast_to(v, (8, width))
+    return jnp.where(
+        place == 0, wide_of(first), jnp.where(place == 1, wide_of(second), wide_of(third))
+    )
+
+
+class Sems:
+    def __init__(self, ref):
+        self.ref, self.used, self.size = ref, 0, ref.shape[0]
+
+    def take(self, count=1):
+        first = self.used
+        self.used += count
+        assert self.used <= self.size, self.used
+        return first
+
+
+def make_kernel(sizes):
+    n_dp, n_mp, R, Wd, M, C, Cd, classes, tasks, piece = sizes
+    n_sec = 2
+    W9 = 9 * C
+
+    def kernel(*refs):
+        (
+            x_hbm, sides_ref, wred_hbm, wspa_hbm, wexp_hbm, gin_ref, sin_ref, gout_ref, sout_ref,
+            head_hbm, lab_ref, thr_hbm,
+            act_hbm, ig_hbm, ored, ospa, oexp, ovec, ohead,
+            ssems, rsems, lsems,
+            sred, sspa, sexp, shead, thr, xin, wr, wsp, we, hd, par,
+            live, geo, masks, labc,
+            rs_s, rs_r, ag_a, ag_b, ag_d, st, keep, first, second, third, ppad, dpad, dbuf,
+            lg_s, lg_r, dl, act1, tg, dpre, evec, dth, hbuf, ig,
+            gred, gspa, gexp, sibred, sibspa, sibexp, rred, rspa, rexp, ghead, rhead, vec, vsib,
+        ) = refs
+        s = lax.axis_index("section")
+        d = lax.axis_index("dp")
+        m = lax.axis_index("mp")
+        o = 1 - s
+        send, recv, local = Sems(ssems), Sems(rsems), Sems(lsems)
+        pending = {None: [], 0: [], 1: []}
+        rem = lax.rem
+        dp_dev = lambda t: (s, t, m)
+        mp_dev = lambda t: (s, d, t)
+        sib_dev = (o, d, m)
+
+        def rcopy(src, dst, rsem, dev, when=None):
+            ssem = send.take()
+            pltpu.make_async_remote_copy(
+                src_ref=src(),
+                dst_ref=dst(),
+                send_sem=ssems.at[ssem],
+                recv_sem=rsems.at[rsem],
+                device_id=dev,
+                device_id_type=MESH,
+            ).start()
+
+            def sent():
+                pltpu.make_async_remote_copy(
+                    src_ref=src(),
+                    dst_ref=src(),
+                    send_sem=ssems.at[ssem],
+                    recv_sem=rsems.at[0],
+                    device_id=sib_dev,
+                    device_id_type=MESH,
+                ).wait_send()
+
+            pending[when].append(sent)
+
+        def arrive(dst, rsem):
+            pltpu.make_async_remote_copy(
+                src_ref=dst,
+                dst_ref=dst,
+                send_sem=ssems.at[0],
+                recv_sem=rsems.at[rsem],
+                device_id=sib_dev,
+                device_id_type=MESH,
+            ).wait_recv()
+
+        def load(src, dst):
+            cp = pltpu.make_async_copy(src, dst, lsems.at[local.take()])
+            cp.start()
+            return cp
+
+        axes = {"dp": (n_dp, d, dp_dev), "mp": (n_mp, m, mp_dev)}
+
+        def spread(axis, src_of, dst, when=None, base=None):
+            n, me, dev = axes[axis]
+            base = recv.take(n) if base is None else base
+            for k in range(1, n):
+                rcopy(lambda k=k: src_of(rem(me + k, n)), dst, base + me, dev(rem(me + k, n)), when)
+            return base
+
+        def gathered(axis, slot_of, base):
+            n, me, _ = axes[axis]
+            for k in range(1, n):
+                src = rem(me + n - k, n)
+                arrive(slot_of(src), base + src)
+
+        l_red = load(wred_hbm.at[0], sred)
+        l_x = load(x_hbm.at[s], xin.at[0])
+        l_spa = load(wspa_hbm.at[0], sspa)
+        l_exp = load(wexp_hbm.at[0], sexp)
+        l_head = load(head_hbm, shead)
+        l_thr = load(thr_hbm.at[s], thr)
+
+        barrier = pltpu.get_barrier_semaphore()
+        greeted = 0
+        for ds_ in range(n_sec):
+            for k in range(n_dp):
+                if ds_ == 0 and k == 0:
+                    continue
+                pl.semaphore_signal(
+                    barrier, inc=1,
+                    device_id=(rem(s + ds_, n_sec), rem(d + k, n_dp), m),
+                    device_id_type=MESH,
+                )
+                greeted += 1
+        for k in range(1, n_mp):
+            pl.semaphore_signal(
+                barrier, inc=1, device_id=(s, d, rem(m + k, n_mp)), device_id_type=MESH
+            )
+            greeted += 1
+
+        l_red.wait()
+        wr[s, d] = sred[...].astype(BF16)
+        par[s] = jnp.zeros(par.shape[1:], F32)
+        for i in range(2):
+            par[s, i:i + 1, :C] = gin_ref[0, i:i + 1, :]
+            par[s, 2 + i:3 + i, :C] = sin_ref[0, i:i + 1, :]
+        par[s, 4:5, :] = gout_ref[...]
+        par[s, 5:6, :] = sout_ref[...]
+        pl.semaphore_wait(barrier, greeted)
+
+        b_red, b_spa, b_exp = [[recv.take(n_dp) for _ in range(2)] for _ in range(3)]
+        f_red, f_spa, f_exp = [[recv.take() for _ in range(2)] for _ in range(3)]
+
+        def send_own(buf, bases, j):
+            spread("dp", lambda t: buf.at[j, d], lambda: buf.at[j, d], when=j, base=bases[j])
+
+        def pass_on(buf, bases, fsems, j):
+            @pl.when(s == j)
+            def _():
+                gathered("dp", lambda src: buf.at[j, src], bases[j])
+                rcopy(lambda: buf.at[j], lambda: buf.at[j], fsems[j], sib_dev, when=j)
+
+        def from_sib(buf, fsems, j):
+            @pl.when(s != j)
+            def _():
+                arrive(buf.at[j], fsems[j])
+
+        par_sem = recv.take()
+        rcopy(lambda: par.at[s], lambda: par.at[s], par_sem, sib_dev)
+
+        @pl.when(s == 0)
+        def _():
+            send_own(wr, b_red, 0)
+
+        l_spa.wait()
+        for k in range(9):
+            wsp[s, d, :, k * C:(k + 1) * C] = sspa[k].astype(BF16)
+
+        @pl.when(s == 0)
+        def _():
+            send_own(wsp, b_spa, 0)
+
+        l_exp.wait()
+        we[s, d] = sexp[...].astype(BF16)
+
+        @pl.when(s == 0)
+        def _():
+            send_own(we, b_exp, 0)
+
+        sides = jnp.where(s == 0, sides_ref[0], sides_ref[1]).astype(F32)
+        slots = sides.shape[1]
+        sq = jnp.broadcast_to(sides * sides, (8, slots)).astype(BF16)
+        upper = (
+            lax.broadcasted_iota(jnp.int32, (slots, slots), 0)
+            <= lax.broadcasted_iota(jnp.int32, (slots, slots), 1)
+        ).astype(BF16)
+        ends = dot(sq, upper, NN)[0:1]
+        starts = ends - sides * sides
+        nloc = jnp.broadcast_to(jnp.max(ends, axis=1, keepdims=True), (1, 128))
+        shape = (R, 128)
+        pos = lax.broadcasted_iota(jnp.int32, (R, slots), 0).astype(F32)
+        inside = (pos >= starts) & (pos < ends)
+        origin = jnp.sum(jnp.where(inside, starts, 0.0), axis=1, keepdims=True)
+        side = jnp.sum(jnp.where(inside, sides, 0.0), axis=1, keepdims=True)
+        geo[0] = jnp.broadcast_to(origin, shape)
+        geo[1] = jnp.broadcast_to(side, shape)
+
+        def make_masks(rows, carry):
+            side_b = geo[1, rows]
+            here = lax.broadcasted_iota(jnp.int32, side_b.shape, 0) + rows.start
+            offset = here.astype(F32) - geo[0, rows]
+            row_in = jnp.floor((offset + 0.5) / jnp.maximum(side_b, 1.0))
+            col_in = offset - row_in * side_b
+            live[rows] = (side_b > 0.0).astype(F32)
+            for idx, (_, a, b, q, _) in enumerate(MASKS):
+                ra, cb = row_in + a, col_in + b
+                ok = (side_b == q) & (ra >= 0.0) & (ra < q) & (cb >= 0.0) & (cb < q)
+                masks[idx, rows] = ok.astype(F32)
+            return carry
+
+        loop(R, 64, make_masks)
+        for buf in (ppad, dpad):
+            edge = jnp.zeros((PAD, buf.shape[1]), F32)
+            buf[0:PAD] = edge
+            buf[PAD + R:PAD + R + PAD] = edge
+        lab2 = lab_ref[...]
+        lab = jnp.where(s == 0, lab2[:, 0], lab2[:, 1]).astype(F32)
+        lab = jnp.concatenate([lab, jnp.zeros((8 - tasks, R), F32)], axis=0)
+        labc[...] = jnp.transpose(lab)
+
+        l_head.wait()
+        eye = (
+            lax.broadcasted_iota(jnp.int32, (piece, piece), 0)
+            == lax.broadcasted_iota(jnp.int32, (piece, piece), 1)
+        ).astype(BF16)
+        mine = s * n_dp + d
+        for t in range(tasks):
+            hd[mine, t] = dot(eye, shead[t].astype(BF16), NT).astype(BF16)
+        b_head = recv.take(n_sec * n_dp)
+
+        def to_all(src_of, dst, base):
+            for ds_ in range(n_sec):
+                for k in range(n_dp):
+                    if ds_ == 0 and k == 0:
+                        continue
+                    place = lambda ds_=ds_, k=k: (rem(s + ds_, n_sec), rem(d + k, n_dp))
+
+                    def src(place=place):
+                        ts, td = place()
+                        return src_of(ts * n_dp + td)
+
+                    rcopy(src, dst, base + mine, place() + (m,))
+
+        def from_all(slot_of, base):
+            for ds_ in range(n_sec):
+                for k in range(n_dp):
+                    if ds_ == 0 and k == 0:
+                        continue
+                    src = rem(s + ds_, n_sec) * n_dp + rem(d + k, n_dp)
+                    arrive(slot_of(src), base + src)
+
+        def cat(buf, n):
+            return jnp.concatenate([buf[i] for i in range(n)], axis=1)
+
+        phase = {"rs": 0, "st": 0}
+
+        def rs_start():
+            p = phase["rs"]
+            phase["rs"] += 1
+            base = spread("mp", lambda t: rs_s.at[p, t], lambda: rs_r.at[p, m])
+            return p, base
+
+        def rs_finish(handle, dst):
+            p, base = handle
+            gathered("mp", lambda src: rs_r.at[p, src], base)
+
+            def add(rows, carry):
+                total = rs_s[p, m, rows].astype(F32)
+                for k in range(1, n_mp):
+                    total = total + rs_r[p, rem(m + k, n_mp), rows].astype(F32)
+                dst[rows] = total
+                return carry
+
+            loop(R, 128, add)
+
+        def product_to_rs(left, right_of, dims):
+            p = phase["rs"]
+
+            def part(rows, carry):
+                out = dot(left[rows], right_of(), dims)
+                for c in range(n_mp):
+                    rs_s[p, c, rows] = out[:, c * C:(c + 1) * C].astype(BF16)
+                return carry
+
+            loop(R, 128, part)
+            return rs_start()
+
+        def exchange(tile):
+            p = phase["st"]
+            phase["st"] += 1
+            width = tile.shape[1]
+            view = st.at[p, :, :, 0:width]
+            st[p, d, :, 0:width] = tile
+            slot = lambda src: st.at[p, src, :, 0:width]
+            base = spread("dp", lambda t: slot(d), lambda: slot(d))
+            return p, width, base
+
+        def collect(handle):
+            p, width, base = handle
+            gathered("dp", lambda src: st.at[p, src, :, 0:width], base)
+            return [st[p, i, :, 0:width] for i in range(n_dp)]
+
+        def stats_start(buf, width):
+            chunk = 128 if width <= 128 else 32
+            zero = jnp.zeros((8, width), F32)
+
+            def sum_up(rows, carry):
+                return carry + fold(buf[rows] * wide(live[rows], width))
+
+            total = jnp.sum(loop(R, chunk, sum_up, zero), axis=0, keepdims=True)
+            count = wide(nloc, width)
+            mean = total / jnp.maximum(count, 1.0)
+
+            def squares(rows, carry):
+                off = (buf[rows] - mean) * wide(live[rows], width)
+                return carry + fold(off * off)
+
+            sqs = jnp.sum(loop(R, chunk, squares, zero), axis=0, keepdims=True)
+            return exchange(rows_tile(total, sqs, count))
+
+        def stats_finish(handle, j, i):
+            tiles = collect(handle)
+            width = handle[1]
+            count = sum(t[2:3] for t in tiles)
+            mean = sum(t[0:1] for t in tiles) / count
+            sqs = 0.0
+            for t in tiles:
+                local_mean = t[0:1] / jnp.maximum(t[2:3], 1.0)
+                sqs = sqs + t[1:2] + t[2:3] * (local_mean - mean) * (local_mean - mean)
+            inv = lax.rsqrt(sqs / count + NORM_EPS)
+            keep[j, i, :, 0:width] = rows_tile(mean, inv, count)
+
+        def norm_of(j, i, width):
+            tile = keep[j, i, :, 0:width]
+            if i < 2:
+                gain, shift = par[j, i:i + 1, 0:width], par[j, 2 + i:3 + i, 0:width]
+            else:
+                gain, shift = par[j, 4:5, 0:width], par[j, 5:6, 0:width]
+            return tile[0:1], tile[1:2], tile[2:3], gain, shift
+
+        def taps_sum(src, flip, put):
+            for r0 in range(0, R, 128):
+                put(r0, lambda idx_list, lanes: sum(
+                    masks[(len(MASKS) - 2 - (idx // 2) * 2 + idx % 2) if flip else idx, r0:r0 + 128]
+                    * src[
+                        PAD + r0 + (-1 if flip else 1) * MASKS[idx][4]:
+                        PAD + r0 + (-1 if flip else 1) * MASKS[idx][4] + 128,
+                        lanes,
+                    ]
+                    for idx in idx_list
+                ))
+
+        nothing = lambda: None
+        vec[...] = jnp.zeros(vec.shape, F32)
+
+        def forward(j, hooks):
+            x = xin.at[j]
+            h = product_to_rs(x, lambda: cat(wr.at[j], n_dp), NN)
+            hooks[0]()
+            rs_finish(h, first.at[j])
+            h = stats_start(first.at[j], C)
+            stats_finish(h, j, 0)
+            mu, inv, _, gain, shift = norm_of(j, 0, C)
+
+            def act_a(rows, carry):
+                y = live[rows] * (gain * ((first[j, rows] - mu) * inv) + shift)
+                ag_a[j, m, rows] = gelu(y).astype(BF16)
+                return carry
+
+            loop(R, 128, act_a)
+            base = spread("mp", lambda t: ag_a.at[j, m], lambda: ag_a.at[j, m])
+            hooks[1]()
+            gathered("mp", lambda src: ag_a.at[j, src], base)
+
+            def conv(rows, carry):
+                full = jnp.concatenate([ag_a[j, i, rows] for i in range(n_mp)], axis=1)
+                weights = wsp[j].reshape(M, W9)
+                start = pl.multiple_of(rows.start + PAD, 8)
+                ppad[pl.ds(start, 128)] = dot(full, weights, NN)
+                return carry
+
+            loop(R, 128, conv)
+
+            def put(r0, summed):
+                second[j, r0:r0 + 128] = sum(
+                    summed([2 * k, 2 * k + 1], slice(k * C, (k + 1) * C)) for k in range(9)
+                )
+
+            taps_sum(ppad, False, put)
+            h = stats_start(second.at[j], C)
+            stats_finish(h, j, 1)
+            mu, inv, _, gain, shift = norm_of(j, 1, C)
+
+            def act_b(rows, carry):
+                y = live[rows] * (gain * ((second[j, rows] - mu) * inv) + shift)
+                ag_b[j, m, rows] = gelu(y).astype(BF16)
+                return carry
+
+            loop(R, 128, act_b)
+            base = spread("mp", lambda t: ag_b.at[j, m], lambda: ag_b.at[j, m])
+            hooks[2]()
+            gathered("mp", lambda src: ag_b.at[j, src], base)
+
+            def expand(rows, carry):
+                full = jnp.concatenate([ag_b[j, i, rows] for i in range(n_mp)], axis=1)
+                third[j, rows] = dot(full, we[j].reshape(M, Wd), NN)
+                return carry
+
+            loop(R, 128, expand)
+            h = stats_start(third.at[j], Wd)
+            hooks[3]()
+            stats_finish(h, j, 2)
+            mu, inv, _, gain, shift = norm_of(j, 2, Wd)
+            out = xin.at[1] if j == 0 else act1
+
+            def act_c(rows, carry):
+                lv = wide(live[rows], Wd)
+                pre = lv * (gain * ((third[j, rows] - mu) * inv) + shift)
+                pre = pre + xin[j, rows].astype(F32)
+                out[rows] = (lv * gelu(pre)).astype(BF16)
+                return carry
+
+            loop(R, 32, act_c)
+
+        def to_section(src, hbm, j, sem):
+            @pl.when(s == j)
+            def _():
+                lsem = local.take()
+                made = lambda: pltpu.make_async_copy(src(), hbm.at[0, s], lsems.at[lsem])
+                made().start()
+                pending[j].append(lambda: made().wait())
+
+            @pl.when(s != j)
+            def _():
+                rcopy(src, lambda: hbm.at[0, s], sem, sib_dev, when=1 - j)
+
+        out_sems = [[recv.take() for _ in range(2)] for _ in range(2)]
+
+        g_sib = [recv.take() for _ in range(3)]
+        g_dp = [recv.take(n_dp) for _ in range(3)]
+        grads = ((gred, sibred, rred), (gspa, sibspa, rspa), (gexp, sibexp, rexp))
+
+        def grad_to_sib(which, j):
+            own, sib, _ = grads[which]
+
+            @pl.when(s != j)
+            def _():
+                rcopy(lambda: own.at[j], lambda: sib, g_sib[which], sib_dev, when=1 - j)
+
+        def grad_to_dp(which, j):
+            own, sib, got = grads[which]
+
+            @pl.when(s == j)
+            def _():
+                arrive(sib, g_sib[which])
+                depth = own.shape[2]
+
+                def add(rows, carry):
+                    for i in range(n_dp):
+                        own[j, i, rows] = (
+                            own[j, i, rows].astype(F32) + sib[i, rows].astype(F32)
+                        ).astype(BF16)
+                    return carry
+
+                loop(depth, 64, add)
+                spread("dp", lambda t: own.at[j, t], lambda: got.at[d], when=j, base=g_dp[which])
+
+        def backward(j, hooks):
+            mu, inv, count, gain, shift = norm_of(j, 2, Wd)
+            zero = (jnp.zeros((8, Wd), F32), jnp.zeros((8, Wd), F32))
+
+            def top(rows, carry):
+                sb, sg = carry
+                lv = wide(live[rows], Wd)
+                xhat = (third[j, rows] - mu) * inv
+                pre = lv * (gain * xhat + shift) + xin[j, rows].astype(F32)
+                dp_ = gelu_grad(pre) * lv * evec[rows]
+                dpre[rows] = dp_
+                return sb + fold(dp_), sg + fold(dp_ * xhat)
+
+            sb, sg = loop(R, 32, top, zero)
+            total = lambda v: jnp.sum(v, axis=0, keepdims=True)
+            sb, sg = total(sb), total(sg)
+            h = exchange(rows_tile(sb, sg, sg))
+            hooks[0]()
+            tile = sum(collect(h))
+            vec[j, 4:5, :] = tile[1:2]
+            vec[j, 5:6, :] = tile[0:1]
+            sb_n, sg_n = tile[0:1] / count, tile[1:2] / count
+            scale = gain * inv
+
+            def d_third(rows, carry):
+                lv = wide(live[rows], Wd)
+                xhat = (third[j, rows] - mu) * inv
+                dth[rows] = (lv * scale * (dpre[rows] - sb_n - xhat * sg_n)).astype(BF16)
+                return carry
+
+            loop(R, 32, d_third)
+            h = product_to_rs(dth, lambda: we[j].reshape(M, Wd), NT)
+            for i in range(n_dp):
+                full = cat(ag_b.at[j], n_mp)[:, i * Cd:(i + 1) * Cd]
+                gexp[j, i] = dot(full, dth[...], TN).astype(BF16)
+            grad_to_sib(2, j)
+            hooks[1]()
+            rs_finish(h, hbuf)
+
+            def inner(i, src):
+                mu, inv, count, gain, shift = norm_of(j, i, C)
+                zero = (jnp.zeros((8, C), F32), jnp.zeros((8, C), F32))
+
+                def up(rows, carry):
+                    sb, sg = carry
+                    xhat = (src[j, rows] - mu) * inv
+                    pre = live[rows] * (gain * xhat + shift)
+                    g = live[rows] * gelu_grad(pre) * hbuf[rows]
+                    hbuf[rows] = g
+                    return sb + fold(g), sg + fold(g * xhat)
+
+                sb, sg = loop(R, 128, up, zero)
+                sb, sg = total(sb), total(sg)
+                tile = sum(collect(exchange(rows_tile(sb, sg, sg))))
+                vec[j, i:i + 1, 0:C] = tile[1:2]
+                vec[j, 2 + i:3 + i, 0:C] = tile[0:1]
+                sb_n, sg_n = tile[0:1] / count, tile[1:2] / count
+                scale = gain * inv
+
+                def grad_of(rows):
+                    xhat = (src[j, rows] - mu) * inv
+                    return live[rows] * scale * (hbuf[rows] - sb_n - xhat * sg_n)
+
+                return grad_of
+
+            grad_of = inner(1, second)
+
+            def d_second(rows, carry):
+                start = pl.multiple_of(rows.start + PAD, 8)
+                dpad[pl.ds(start, 128)] = grad_of(rows).astype(BF16).astype(F32)
+                return carry
+
+            loop(R, 128, d_second)
+
+            def put(r0, summed):
+                for k in range(9):
+                    dbuf[r0:r0 + 128, k * C:(k + 1) * C] = summed(
+                        [2 * k, 2 * k + 1], slice(None)
+                    ).astype(BF16)
+
+            taps_sum(dpad, True, put)
+            h = product_to_rs(dbuf, lambda: wsp[j].reshape(M, W9), NT)
+            for i in range(n_dp):
+                full = cat(ag_a.at[j], n_mp)[:, i * Cd:(i + 1) * Cd]
+                gspa[j, i] = dot(full, dbuf[...], TN).astype(BF16)
+            grad_to_sib(1, j)
+            grad_to_dp(2, j)
+            hooks[2]()
+            rs_finish(h, hbuf)
+            grad_of = inner(0, first)
+
+            def d_first(rows, carry):
+                ag_d[j, m, rows] = grad_of(rows).astype(BF16)
+                return carry
+
+            loop(R, 128, d_first)
+            base = spread("mp", lambda t: ag_d.at[j, m], lambda: ag_d.at[j, m])
+            grad_to_dp(1, j)
+            hooks[3]()
+            gathered("mp", lambda src: ag_d.at[j, src], base)
+
+            def d_input():
+                def body(rows, carry):
+                    full = jnp.concatenate([ag_d[j, i, rows] for i in range(n_mp)], axis=1)
+                    out = dot(full, cat(wr.at[j], n_dp), NT) + dpre[rows]
+                    if j == 1:
+                        out = out.astype(BF16).astype(F32)
+                        evec[rows] = out
+                    ig[j, rows] = out
+                    return carry
+
+                loop(R, 128, body)
+                to_section(lambda: ig.at[j], ig_hbm, j, out_sems[1][j])
+
+            def g_reduce():
+                for i in range(n_dp):
+                    full = cat(ag_d.at[j], n_mp)[:, i * Cd:(i + 1) * Cd]
+                    gred[j, i] = dot(xin[j], full, TN).astype(BF16)
+                grad_to_sib(0, j)
+
+            return d_input, g_reduce
+
+        pass_on(wr, b_red, f_red, 0)
+        l_x.wait()
+        from_sib(wr, f_red, 0)
+
+        @pl.when(s == 1)
+        def _():
+            send_own(wr, b_red, 1)
+            send_own(wsp, b_spa, 1)
+            send_own(we, b_exp, 1)
+
+        arrive(par.at[o], par_sem)
+
+        def f00():
+            pass_on(wsp, b_spa, f_spa, 0)
+            to_all(lambda t: hd.at[mine], lambda: hd.at[mine], b_head)
+
+        def f01():
+            pass_on(we, b_exp, f_exp, 0)
+            from_sib(wsp, f_spa, 0)
+
+        def f02():
+            pass_on(wr, b_red, f_red, 1)
+            from_sib(we, f_exp, 0)
+
+        def f03():
+            pass_on(wsp, b_spa, f_spa, 1)
+            from_sib(wr, f_red, 1)
+
+        forward(0, (f00, f01, f02, f03))
+
+        def f10():
+            to_section(lambda: xin.at[1], act_hbm, 0, out_sems[0][0])
+            pass_on(we, b_exp, f_exp, 1)
+
+        def f11():
+            from_sib(wsp, f_spa, 1)
+
+        def f12():
+            from_sib(we, f_exp, 1)
+
+        forward(1, (f10, f11, f12, nothing))
+
+        from_all(lambda src: hd.at[src], b_head)
+        RM = R // n_mp
+        n_cls = n_sec * n_dp
+
+        def heads_of(t):
+            return hd[:, t].reshape(classes, Wd)
+
+        for c in range(n_mp):
+            rows = act1[c * RM:(c + 1) * RM]
+            for t in range(tasks):
+                lg_s[c, :, t * classes:(t + 1) * classes] = dot(rows, heads_of(t), NT).astype(
+                    lg_s.dtype
+                )
+        base = spread("mp", lambda t: lg_s.at[t], lambda: lg_r.at[m])
+        to_section(lambda: act1, act_hbm, 1, out_sems[0][1])
+        l_thr.wait()
+        gathered("mp", lambda src: lg_r.at[src], base)
+        here = pl.ds(pl.multiple_of(m * RM, RM), RM)
+        lv = wide(live[here], classes)
+        for t in range(tasks):
+            lanes = slice(t * classes, (t + 1) * classes)
+            logit = lg_s[m, :, lanes].astype(F32)
+            for k in range(1, n_mp):
+                logit = logit + lg_r[rem(m + k, n_mp), :, lanes].astype(F32)
+            expo = jnp.exp(logit - jnp.max(logit, axis=1, keepdims=True))
+            soft = expo / jnp.sum(expo, axis=1, keepdims=True)
+            ids = lax.broadcasted_iota(jnp.int32, (RM, classes), 1).astype(F32)
+            hot = (ids == labc[here, t:t + 1]).astype(F32)
+            dl[m, :, lanes] = (LOSS_WEIGHT * lv * (soft - hot)).astype(BF16)
+        base = spread("mp", lambda t: dl.at[m], lambda: dl.at[m])
+        gathered("mp", lambda src: dl.at[src], base)
+
+        def merge_block(c):
+            for t in range(tasks):
+                lanes = slice(t * classes, (t + 1) * classes)
+                tg[t] = dot(dl[c, :, lanes], heads_of(t), NN)
+
+            def merge(rows, carry):
+                total = soft_sum = None
+                for t in range(tasks):
+                    g = tg[t, rows]
+                    soft = jnp.sqrt(g * g + SIGN_FLOOR * SIGN_FLOOR) - SIGN_FLOOR
+                    total = g if t == 0 else total + g
+                    soft_sum = soft if t == 0 else soft_sum + soft
+                purity = 0.5 * (1.0 + total / (soft_sum + SIGN_FLOOR))
+                start = pl.multiple_of(rows.start + c * RM, 32)
+                there = pl.ds(start, 32)
+                frac = 1.0 / (1.0 + jnp.exp((thr[there] - purity) * (1.0 / KEEP_TEMPER)))
+                upper, lower = 0.5 * (total + soft_sum), 0.5 * (total - soft_sum)
+                evec[there] = frac * upper + (1.0 - frac) * lower
+                return carry
+
+            loop(RM, 32, merge)
+
+        for c in range(n_mp):
+            merge_block(c)
+
+        def b10():
+            b_gh = recv.take(n_cls)
+            for t in range(tasks):
+                lanes = slice(t * classes, (t + 1) * classes)
+                delta = dl[:, :, lanes].reshape(R, classes)
+                out = dot(delta, act1[...], TN).astype(BF16)
+                ghead[:, t] = out.reshape(n_cls, piece, Wd)
+            to_all(lambda t: ghead.at[t], lambda: rhead.at[mine], b_gh)
+            hold["b_gh"] = b_gh
+
+        hold = {}
+        late1 = backward(1, (b10, nothing, nothing, nothing))
+        late1[0]()
+
+        def b00():
+            late1[1]()
+
+        def b01():
+            grad_to_dp(0, 1)
+
+        late0 = backward(0, (b00, b01, nothing, nothing))
+        late0[1]()
+        late0[0]()
+        vec_sem = recv.take()
+        rcopy(lambda: vec.at[o], lambda: vsib, vec_sem, sib_dev)
+
+        from_all(lambda src: rhead.at[src], hold["b_gh"])
+        for t in range(tasks):
+            total = ghead[mine, t].astype(F32)
+            for k in range(1, n_cls):
+                total = total + rhead[rem(mine + k, n_cls), t].astype(F32)
+            ohead[t] = total
+        arrive(vsib, vec_sem)
+        ovec[...] = vec[s] + vsib[...]
+        grad_to_dp(0, 0)
+
+        def total_of(own, got, rows):
+            out = own[s, d, rows].astype(F32)
+            for k in range(1, n_dp):
+                out = out + got[rem(d + k, n_dp), rows].astype(F32)
+            return out
+
+        for which in (2, 1, 0):
+            own, _, got = grads[which]
+            gathered("dp", lambda src: got.at[src], g_dp[which])
+
+            def finish(rows, carry):
+                out = total_of(own, got, rows)
+                if which == 1:
+                    for k in range(9):
+                        ospa[0, k, rows] = out[:, k * C:(k + 1) * C]
+                else:
+                    (ored if which == 0 else oexp)[0, rows] = out
+                return carry
+
+            loop(own.shape[2], 64, finish)
+
+        for j in range(2):
+            @pl.when(s == j)
+            def _():
+                for i, hbm in enumerate((act_hbm, ig_hbm)):
+                    arrive(hbm.at[0, o], out_sems[i][j])
+
+        for key, waits in pending.items():
+            def finish_all(waits=waits):
+                for wait in waits:
+                    wait()
+
+            if key is None:
+                finish_all()
+            else:
+                pl.when(s == key)(finish_all)
+
+    return kernel
+
+
+def fused_device(sizes, *args):
+    n_dp, n_mp, R, Wd, M, C, Cd, classes, tasks, piece = sizes
+    W9, n_cls = 9 * C, 2 * n_dp
+    RM = R // n_mp
+    vmem = lambda shape, dtype: pltpu.VMEM(shape, dtype)
+    scratch = [
+        pltpu.SemaphoreType.DMA((300,)),
+        pltpu.SemaphoreType.DMA((300,)),
+        pltpu.SemaphoreType.DMA((16,)),
+        vmem((Wd, Cd), F32),
+        vmem((9, Cd, C), F32),
+        vmem((Cd, Wd), F32),
+        vmem((tasks, Wd, piece), F32),
+        vmem((R, Wd), F32),
+        vmem((2, R, Wd), BF16),
+        vmem((2, n_dp, Wd, Cd), BF16),
+        vmem((2, n_dp, Cd, W9), BF16),
+        vmem((2, n_dp, Cd, Wd), BF16),
+        vmem((n_cls, tasks, piece, Wd), BF16),
+        vmem((2, 8, Wd), F32),
+        vmem((R, 128), F32),
+        vmem((2, R, 128), F32),
+        vmem((len(MASKS), R, 128), F32),
+        vmem((R, 8), F32),
+        vmem((6, n_mp, R, C), BF16),
+        vmem((6, n_mp, R, C), BF16),
+        vmem((2, n_mp, R, C), BF16),
+        vmem((2, n_mp, R, C), BF16),
+        vmem((2, n_mp, R, C), BF16),
+        vmem((12, n_dp, 8, Wd), F32),
+        vmem((2, 3, 8, Wd), F32),
+        vmem((2, R, C), F32),
+        vmem((2, R, C), F32),
+        vmem((2, R, Wd), F32),
+        vmem((R + 2 * PAD, W9), F32),
+        vmem((R + 2 * PAD, C), F32),
+        vmem((R, W9), BF16),
+        vmem((n_mp, RM, tasks * classes), BF16),
+        vmem((n_mp, RM, tasks * classes), BF16),
+        vmem((n_mp, RM, tasks * classes), BF16),
+        vmem((R, Wd), BF16),
+        vmem((tasks, RM, Wd), F32),
+        vmem((R, Wd), F32),
+        vmem((R, Wd), F32),
+        vmem((R, Wd), BF16),
+        vmem((R, C), F32),
+        vmem((2, R, Wd), F32),
+        vmem((2, n_dp, Wd, Cd), BF16),
+        vmem((2, n_dp, Cd, W9), BF16),
+        vmem((2, n_dp, Cd, Wd), BF16),
+        vmem((n_dp, Wd, Cd), BF16),
+        vmem((n_dp, Cd, W9), BF16),
+        vmem((n_dp, Cd, Wd), BF16),
+        vmem((n_dp, Wd, Cd), BF16),
+        vmem((n_dp, Cd, W9), BF16),
+        vmem((n_dp, Cd, Wd), BF16),
+        vmem((n_cls, tasks, piece, Wd), BF16),
+        vmem((n_cls, tasks, piece, Wd), BF16),
+        vmem((2, 8, Wd), F32),
+        vmem((8, Wd), F32),
+    ]
+    in_vmem = pl.BlockSpec(memory_space=pltpu.VMEM)
+    in_any = pl.BlockSpec(memory_space=pl.ANY)
+    whole = lambda shape, dtype=F32: jax.ShapeDtypeStruct(shape, dtype)
+    out = pl.pallas_call(
+        make_kernel(sizes),
+        out_shape=(
+            whole((1, 2, R, Wd), BF16),
+            whole((1, 2, R, Wd)),
+            whole((1, Wd, Cd)),
+            whole((1, 9, Cd, C)),
+            whole((1, Cd, Wd)),
+            whole((8, Wd)),
+            whole((tasks, piece, Wd)),
+        ),
+        in_specs=[
+            in_any, in_vmem, in_any, in_any, in_any, in_vmem, in_vmem, in_vmem, in_vmem,
+            in_any, in_vmem, in_any,
+        ],
+        out_specs=(in_any, in_any, in_vmem, in_vmem, in_vmem, in_vmem, in_vmem),
+        scratch_shapes=scratch,
+        compiler_params=pltpu.CompilerParams(
+            collective_id=0, has_side_effects=True, vmem_limit_bytes=60 * 2**20
+        ),
+    )(*args)
+    act, grads_in, g_red, g_spa, g_exp, vec, head = out
+    d = lax.axis_index("dp")
+    part = C // n_dp
+    outer = Wd // n_dp
+    inner = lambda rows: lax.dynamic_slice_in_dim(vec[rows, :C], d * part, part, 1)[None, :, None]
+    outer_of = lambda row: lax.dynamic_slice_in_dim(vec[row, :], d * outer, outer, 0)[None, None]
+    return (
+        act,
+        grads_in,
+        g_red,
+        g_spa,
+        g_exp,
+        inner(slice(0, 2)),
+        inner(slice(2, 4)),
+        outer_of(4),
+        outer_of(5),
+        jnp.transpose(head, (0, 2, 1)),
+    )
+
+
+def per_device(*args):
+    block_input, _, w_reduce, w_spatial = args[:4]
+    n_dp, n_mp = lax.axis_size("dp"), lax.axis_size("mp")
+    R, Wd = block_input.shape[1:]
+    Cd, C = w_reduce.shape[2], w_spatial.shape[3]
+    tasks, _, piece = args[9].shape
+    sizes = (n_dp, n_mp, R, Wd, C * n_mp, C, Cd, piece * 2 * n_dp, tasks, piece)
+    whole_tiles = not (C % 128 or Cd % 128 or Wd % 128 or R % 128 or piece % 16 or (R // n_mp) % 32)
+    if whole_tiles and block_input.shape[0] == lax.axis_size("section") == 2:
+        return fused_device(sizes, *args)
+    return plain_device(*args)
+
+
 def solution(mesh):
     return jax.shard_map(
         per_device,

time: 1440 us -> 220 us (0.15)
  blocking collectives: 509 us -> 0 us
  waiting for transfers between devices: 336 us -> 0 us
  local copies, waits for them, and re-layouts: 238 us -> 10.9 us
  Pallas kernels: 0 us -> 208 us
  other arithmetic: 185 us -> 0 us
  matrix products: 132 us -> 0 us
  between operations: 21.8 us -> 0.67 us
    all_gather x18 -> x0, blocking collectives: 259 us -> none  [the longest x15 211 us: channel_gather(): return lax.all_gather(values, 'mp', axis=1, tiled=True)]
    psum x27 -> x0, blocking collectives: 250 us -> none  [the longest x9 88 us: norm_stats(): lax.psum((jnp.sum(masked, axis=0), jnp.sum(live_rows)), 'dp')]
    reduce_scatter x16 -> x0, waiting for transfers between devices: 242 us -> none  [the longest x12 101 us: channel_sum(): return lax.psum_scatter(values, 'mp', scatter_dimension=1, tiled=True)]
    pallas_call x0 -> x1, Pallas kernels: none -> 208 us  [fused_device(): pl.pallas_call(make_kernel(sizes), out_shape=(whole((1, 2, R, Wd), BF16),...]
    gather x81 -> x0, local copies, waits for them, and re-layouts: 200 us -> none  [the longest x54 139 us: gather_taps(): values[indices[tap_idx]] * valids[tap_idx][:, None].astype(values.dtype)]
    dot_general x141 -> x0, matrix products: 132 us -> none  [the longest x27 31 us: block_backward(): jnp.einsum('rc,ro->co', gather_taps(full_a, indices, valids, tap_idx), d_...]
    psum x1 -> x0, waiting for transfers between devices: 69.8 us -> none  [per_device(): lax.psum(jnp.einsum('rc,tco->tro', result_low, heads_all, preferred_eleme...]
    gather x54 -> x0, other arithmetic: 36.3 us -> none  [gather_taps(): values[indices[tap_idx]] * valids[tap_idx][:, None].astype(values.dtype)]
  transfers between devices with their start and end apart: 26 -> 0, of which waited for: 15 -> 0; matrix products, arithmetic and copies ran while one was open for 22% -> 0% of each run, Pallas kernels for 0% -> 0%
where the time goes in v1:
time: 220 us; the launch traced here: 219 us
  Pallas kernels  208 us (95%)
  local copies, waits for them, and re-layouts  10.9 us (5%)
    pallas_call x1, Pallas kernels, fused_device(): pl.pallas_call(make_kernel(sizes), out_shape=(whole((1, 2, R, Wd), BF16),...  208 us
    unnamed x17, local copies, waits for them, and re-layouts  8.13 us

profile of v1, /device:TPU:0, one launch (start us, length us, event | category | flops | bytes accessed | tf_op | source)
XLA Modules:
  0.0 219.4 jit_solution(43156896197876378)
XLA Ops:
  0.6 2.0 copy.22.refs_9_
  2.7 207.9 %shard_map.195 = (bf16[1,2,384,512]{3,2,1,0:T(8,128)(2,1)}, f32[1,2,384,512]{3,2,1,0:T(8,128)}, f32[1,512,128]{2,1,0:T(8,128)}, f32[1,9,128,128]{3,2,1,0:T(8,128...) custom-call(bf16[2,384,512]{2,1,0:T(8,128)(2,1)} %refs_0_.1, s32[2,1,96]{2,1,0:T(1,128)} %refs_1_.1, ...), custom_call_target="tpu_custom_call" | custom-call | tf_op jit(solution)/shard_map/pallas_call | solution.py:1202
  210.6 0.0 copy-start
  210.6 0.8 fusion.3
  211.4 0.8 fusion.2
  212.2 0.5 fusion
  212.7 0.6 constant_dynamic-slice_fusion.2
  213.3 2.1 copy.31
  215.4 0.0 copy-done
  215.4 0.0 copy-start.3
  215.4 0.0 copy-start.1
  215.4 1.1 copy.32
  216.6 0.0 copy-done.3
  216.6 0.0 copy-start.2
  216.6 0.0 copy-start.4
  216.6 0.7 copy.33
  217.3 0.0 copy-done.1
  217.3 0.8 copy.34
  218.1 0.0 copy-done.2
  218.1 0.7 copy.35
  218.8 0.0 copy-done.4
  218.8 0.6 copy.36
Async XLA Ops:
  210.6 4.8 %copy-start = (f32[1,2,384,512]{3,2,1,0:T(8,128)S(1)}, f32[1,2,384,512]{3,2,1,0:T(8,128)}, u32[]{:S(2)}) copy-start(f32[1,2,384,512]{3,2,1,0:T(8,128)} %get-tuple-element.53) | copy-start | bytes 4718596
  215.4 1.1 copy-start.3
  215.4 1.9 copy-start.1
  216.6 1.5 copy-start.2
  216.6 2.2 %copy-start.4 = (f32[3,16,512]{2,1,0:T(8,128)S(1)}, f32[3,16,512]{2,1,0:T(8,128)}, u32[]{:S(2)}) copy-start(f32[3,16,512]{2,1,0:T(8,128)} %get-tuple-element.23) | copy-start | bytes 294916

commit v2 on v1

--- a/solution.py
+++ b/solution.py
@@ -404,13 +404,14 @@
         (
             x_hbm, sides_ref, wred_hbm, wspa_hbm, wexp_hbm, gin_ref, sin_ref, gout_ref, sout_ref,
             head_hbm, lab_ref, thr_hbm,
-            act_hbm, ig_hbm, ored, ospa, oexp, ovec, ohead,
+            act_hbm, ig_hbm, red_hbm, spa_hbm, exp_hbm, vec_hbm, head_out,
             ssems, rsems, lsems,
             sred, sspa, sexp, shead, thr, xin, wr, wsp, we, hd, par,
             live, geo, masks, labc,
-            rs_s, rs_r, ag_a, ag_b, ag_d, st, keep, first, second, third, ppad, dpad, dbuf,
+            rs_s, rs_r, ag_a, ag_b, ag_d, fulla, fullb, dfull, co, st, keep, first, second, third, ppad, dpad, dbuf,
             lg_s, lg_r, dl, act1, tg, dpre, evec, dth, hbuf, ig,
             gred, gspa, gexp, sibred, sibspa, sibexp, rred, rspa, rexp, ghead, rhead, vec, vsib,
+            ored, ospa, oexp, ovec, ohead,
         ) = refs
         s = lax.axis_index("section")
         d = lax.axis_index("dp")
@@ -423,58 +424,72 @@
         mp_dev = lambda t: (s, d, t)
         sib_dev = (o, d, m)
 
-        def rcopy(src, dst, rsem, dev, when=None):
-            ssem = send.take()
+        def put_to(src, dst, ssem, rsem, dev):
             pltpu.make_async_remote_copy(
-                src_ref=src(),
-                dst_ref=dst(),
+                src_ref=src,
+                dst_ref=dst,
                 send_sem=ssems.at[ssem],
                 recv_sem=rsems.at[rsem],
                 device_id=dev,
                 device_id_type=MESH,
             ).start()
 
-            def sent():
-                pltpu.make_async_remote_copy(
-                    src_ref=src(),
-                    dst_ref=src(),
-                    send_sem=ssems.at[ssem],
-                    recv_sem=rsems.at[0],
-                    device_id=sib_dev,
-                    device_id_type=MESH,
-                ).wait_send()
-
-            pending[when].append(sent)
-
-        def arrive(dst, rsem):
-            pltpu.make_async_remote_copy(
-                src_ref=dst,
-                dst_ref=dst,
-                send_sem=ssems.at[0],
+        def waiter(ref, ssem, rsem):
+            return pltpu.make_async_remote_copy(
+                src_ref=ref,
+                dst_ref=ref,
+                send_sem=ssems.at[ssem],
                 recv_sem=rsems.at[rsem],
                 device_id=sib_dev,
                 device_id_type=MESH,
-            ).wait_recv()
+            )
+
+        def rcopy(src, dst, rsem, dev, when=None):
+            ssem = send.take()
+            put_to(src(), dst(), ssem, rsem, dev)
+            pending[when].append(lambda: waiter(src(), ssem, 0).wait_send())
+
+        def arrive(dst, rsem):
+            waiter(dst, 0, rsem).wait_recv()
+
+        axes = {"dp": (n_dp, d, dp_dev), "mp": (n_mp, m, mp_dev)}
+        expected = {}
+
+        def settle(key):
+            expected.pop(key)()
 
         def load(src, dst):
             cp = pltpu.make_async_copy(src, dst, lsems.at[local.take()])
             cp.start()
-            return cp
-
-        axes = {"dp": (n_dp, d, dp_dev), "mp": (n_mp, m, mp_dev)}
-
-        def spread(axis, src_of, dst, when=None, base=None):
-            n, me, dev = axes[axis]
-            base = recv.take(n) if base is None else base
-            for k in range(1, n):
-                rcopy(lambda k=k: src_of(rem(me + k, n)), dst, base + me, dev(rem(me + k, n)), when)
-            return base
-
-        def gathered(axis, slot_of, base):
-            n, me, _ = axes[axis]
-            for k in range(1, n):
-                src = rem(me + n - k, n)
-                arrive(slot_of(src), base + src)
+            key = ("load", local.used)
+            expected[key] = cp.wait
+            return key
+
+        def on(cond, what):
+            return lambda: pl.when(cond())(what)
+
+        class Group:
+            def __init__(self, axis, all_of, when=None):
+                self.n, self.me, self.dev = axes[axis]
+                self.ssem, self.rsem = send.take(), recv.take()
+                self.all_of, self.when = all_of, when
+
+            def put(self, src_of, slot_of):
+                for k in range(1, self.n):
+                    t = rem(self.me + k, self.n)
+                    put_to(src_of(t), slot_of(self.me), self.ssem, self.rsem, self.dev(t))
+
+            def close(self):
+                ssem, rsem, all_of, when = self.ssem, self.rsem, self.all_of, self.when
+                pending[when].append(lambda: waiter(all_of(), ssem, 0).wait_send())
+                wait = lambda: arrive(all_of(), rsem)
+                expected[rsem] = wait if when is None else on(lambda: s == when, wait)
+                return rsem
+
+        def spread(axis, src_of, slot_of, all_of, when=None):
+            group = Group(axis, all_of, when)
+            group.put(src_of, slot_of)
+            return group.close()
 
         l_red = load(wred_hbm.at[0], sred)
         l_x = load(x_hbm.at[s], xin.at[0])
@@ -501,7 +516,7 @@
             )
             greeted += 1
 
-        l_red.wait()
+        settle(l_red)
         wr[s, d] = sred[...].astype(BF16)
         par[s] = jnp.zeros(par.shape[1:], F32)
         for i in range(2):
@@ -511,44 +526,44 @@
         par[s, 5:6, :] = sout_ref[...]
         pl.semaphore_wait(barrier, greeted)
 
-        b_red, b_spa, b_exp = [[recv.take(n_dp) for _ in range(2)] for _ in range(3)]
-        f_red, f_spa, f_exp = [[recv.take() for _ in range(2)] for _ in range(3)]
-
-        def send_own(buf, bases, j):
-            spread("dp", lambda t: buf.at[j, d], lambda: buf.at[j, d], when=j, base=bases[j])
-
-        def pass_on(buf, bases, fsems, j):
+        by_dp, by_sib = {}, {}
+
+        def send_own(buf, j):
+            def go():
+                by_dp[id(buf), j] = spread(
+                    "dp",
+                    lambda t: buf.at[j, d],
+                    lambda src: buf.at[j, src],
+                    lambda: buf.at[j, pl.ds(0, n_dp - 1)],
+                    when=j,
+                )
+
+            pl.when(s == j)(go)
+
+        def pass_on(buf, j):
+            settle(by_dp[id(buf), j])
+            sem = by_sib[id(buf), j] = recv.take()
+
             @pl.when(s == j)
             def _():
-                gathered("dp", lambda src: buf.at[j, src], bases[j])
-                rcopy(lambda: buf.at[j], lambda: buf.at[j], fsems[j], sib_dev, when=j)
-
-        def from_sib(buf, fsems, j):
-            @pl.when(s != j)
-            def _():
-                arrive(buf.at[j], fsems[j])
+                rcopy(lambda: buf.at[j], lambda: buf.at[j], sem, sib_dev, when=j)
+
+            expected[sem] = on(lambda: s != j, lambda: arrive(buf.at[j], sem))
+
+        def from_sib(buf, j):
+            settle(by_sib[id(buf), j])
 
         par_sem = recv.take()
         rcopy(lambda: par.at[s], lambda: par.at[s], par_sem, sib_dev)
-
-        @pl.when(s == 0)
-        def _():
-            send_own(wr, b_red, 0)
-
-        l_spa.wait()
+        expected[par_sem] = lambda: arrive(par.at[o], par_sem)
+        send_own(wr, 0)
+
+        settle(l_spa)
         for k in range(9):
             wsp[s, d, :, k * C:(k + 1) * C] = sspa[k].astype(BF16)
 
-        @pl.when(s == 0)
-        def _():
-            send_own(wsp, b_spa, 0)
-
-        l_exp.wait()
+        settle(l_exp)
         we[s, d] = sexp[...].astype(BF16)
-
-        @pl.when(s == 0)
-        def _():
-            send_own(we, b_exp, 0)
 
         sides = jnp.where(s == 0, sides_ref[0], sides_ref[1]).astype(F32)
         slots = sides.shape[1]
@@ -591,51 +606,41 @@
         lab = jnp.concatenate([lab, jnp.zeros((8 - tasks, R), F32)], axis=0)
         labc[...] = jnp.transpose(lab)
 
-        l_head.wait()
-        eye = (
-            lax.broadcasted_iota(jnp.int32, (piece, piece), 0)
-            == lax.broadcasted_iota(jnp.int32, (piece, piece), 1)
-        ).astype(BF16)
+        settle(l_head)
         mine = s * n_dp + d
         for t in range(tasks):
-            hd[mine, t] = dot(eye, shead[t].astype(BF16), NT).astype(BF16)
-        b_head = recv.take(n_sec * n_dp)
-
-        def to_all(src_of, dst, base):
-            for ds_ in range(n_sec):
-                for k in range(n_dp):
-                    if ds_ == 0 and k == 0:
-                        continue
-                    place = lambda ds_=ds_, k=k: (rem(s + ds_, n_sec), rem(d + k, n_dp))
-
-                    def src(place=place):
-                        ts, td = place()
-                        return src_of(ts * n_dp + td)
-
-                    rcopy(src, dst, base + mine, place() + (m,))
-
-        def from_all(slot_of, base):
-            for ds_ in range(n_sec):
-                for k in range(n_dp):
-                    if ds_ == 0 and k == 0:
-                        continue
-                    src = rem(s + ds_, n_sec) * n_dp + rem(d + k, n_dp)
-                    arrive(slot_of(src), base + src)
+            hd[mine, t] = shead[t].astype(BF16)
+
+        def to_all(src_of, buf):
+            ssem, rsem = send.take(), recv.take()
+            others = [(a, k) for a in range(n_sec) for k in range(n_dp) if a or k]
+            for a, k in others:
+                ts, td = rem(s + a, n_sec), rem(d + k, n_dp)
+                put_to(src_of(ts * n_dp + td), buf.at[mine], ssem, rsem, (ts, td, m))
+            rest = lambda: buf.at[pl.ds(0, len(others))]
+            pending[None].append(lambda: waiter(rest(), ssem, 0).wait_send())
+            expected[rsem] = lambda: arrive(rest(), rsem)
+            return rsem
 
         def cat(buf, n):
             return jnp.concatenate([buf[i] for i in range(n)], axis=1)
 
         phase = {"rs": 0, "st": 0}
 
-        def rs_start():
+        def rs_open():
             p = phase["rs"]
             phase["rs"] += 1
-            base = spread("mp", lambda t: rs_s.at[p, t], lambda: rs_r.at[p, m])
-            return p, base
+            return p, Group("mp", lambda: rs_r.at[p, pl.ds(0, n_mp - 1)])
+
+        def rs_rows(handle, rows, out):
+            p, group = handle
+            for c in range(n_mp):
+                rs_s[p, c, rows] = out[:, c * C:(c + 1) * C].astype(BF16)
+            group.put(lambda t: rs_s.at[p, t, rows], lambda src: rs_r.at[p, src, rows])
 
         def rs_finish(handle, dst):
-            p, base = handle
-            gathered("mp", lambda src: rs_r.at[p, src], base)
+            p, group = handle
+            settle(group.rsem)
 
             def add(rows, carry):
                 total = rs_s[p, m, rows].astype(F32)
@@ -647,30 +652,28 @@
             loop(R, 128, add)
 
         def product_to_rs(left, right_of, dims):
-            p = phase["rs"]
+            handle = rs_open()
 
             def part(rows, carry):
-                out = dot(left[rows], right_of(), dims)
-                for c in range(n_mp):
-                    rs_s[p, c, rows] = out[:, c * C:(c + 1) * C].astype(BF16)
+                rs_rows(handle, rows, dot(left[rows], right_of(), dims))
                 return carry
 
             loop(R, 128, part)
-            return rs_start()
+            handle[1].close()
+            return handle
 
         def exchange(tile):
             p = phase["st"]
             phase["st"] += 1
             width = tile.shape[1]
-            view = st.at[p, :, :, 0:width]
             st[p, d, :, 0:width] = tile
             slot = lambda src: st.at[p, src, :, 0:width]
-            base = spread("dp", lambda t: slot(d), lambda: slot(d))
-            return p, width, base
+            rest = lambda: st.at[p, pl.ds(0, n_dp - 1), :, 0:width]
+            return p, width, spread("dp", lambda t: slot(d), slot, rest)
 
         def collect(handle):
             p, width, base = handle
-            gathered("dp", lambda src: st.at[p, src, :, 0:width], base)
+            settle(base)
             return [st[p, i, :, 0:width] for i in range(n_dp)]
 
         def stats_start(buf, width):
@@ -689,7 +692,7 @@
                 return carry + fold(off * off)
 
             sqs = jnp.sum(loop(R, chunk, squares, zero), axis=0, keepdims=True)
-            return exchange(rows_tile(total, sqs, count))
+            return exchange(rows_tile(total, sqs, count)), mean
 
         def stats_finish(handle, j, i):
             tiles = collect(handle)
@@ -703,6 +706,47 @@
             inv = lax.rsqrt(sqs / count + NORM_EPS)
             keep[j, i, :, 0:width] = rows_tile(mean, inv, count)
 
+        def slots_out(buf, at, values_of):
+            group = Group("mp", lambda: buf.at[at, pl.ds(0, n_mp - 1)])
+
+            def fill(rows, carry):
+                buf[at, m, rows] = values_of(rows).astype(BF16)
+                group.put(lambda t: buf.at[at, m, rows], lambda src: buf.at[at, src, rows])
+                return carry
+
+            loop(R, 128, fill)
+            return group.close()
+
+        def coeffs_out(at, *values):
+            place = lax.broadcasted_iota(jnp.int32, (8, C), 0)
+            tile = jnp.zeros((8, C), F32)
+            for i, v in enumerate(values):
+                tile = jnp.where(place == i, jnp.broadcast_to(v, (8, C)), tile)
+            co[at, m] = tile
+            slot = lambda src: co.at[at, src]
+            return spread("mp", lambda t: slot(m), slot, lambda: co.at[at, pl.ds(0, n_mp - 1)])
+
+        def inner_norm(j, i, src, raw, full, hook):
+            at = 2 * j + i
+            handle, mean_here = stats_start(src.at[j], C)
+            group = slots_out(raw, j, lambda rows: src[j, rows] - mean_here)
+            hook()
+            stats_finish(handle, j, i)
+            mu, inv, _, gain, shift = norm_of(j, i, C)
+            moved = (mean_here - mu) * inv
+            sent = coeffs_out(at, gain * inv, gain * moved + shift, inv, moved)
+            settle(group)
+            settle(sent)
+
+            def act(rows, carry):
+                for c in range(n_mp):
+                    tile = co[at, c]
+                    y = live[rows] * (raw[j, c, rows].astype(F32) * tile[0:1] + tile[1:2])
+                    full[j, rows, c * C:(c + 1) * C] = gelu(y).astype(BF16)
+                return carry
+
+            loop(R, 64, act)
+
         def norm_of(j, i, width):
             tile = keep[j, i, :, 0:width]
             if i < 2:
@@ -731,25 +775,11 @@
             h = product_to_rs(x, lambda: cat(wr.at[j], n_dp), NN)
             hooks[0]()
             rs_finish(h, first.at[j])
-            h = stats_start(first.at[j], C)
-            stats_finish(h, j, 0)
-            mu, inv, _, gain, shift = norm_of(j, 0, C)
-
-            def act_a(rows, carry):
-                y = live[rows] * (gain * ((first[j, rows] - mu) * inv) + shift)
-                ag_a[j, m, rows] = gelu(y).astype(BF16)
-                return carry
-
-            loop(R, 128, act_a)
-            base = spread("mp", lambda t: ag_a.at[j, m], lambda: ag_a.at[j, m])
-            hooks[1]()
-            gathered("mp", lambda src: ag_a.at[j, src], base)
+            inner_norm(j, 0, first, ag_a, fulla, hooks[1])
 
             def conv(rows, carry):
-                full = jnp.concatenate([ag_a[j, i, rows] for i in range(n_mp)], axis=1)
-                weights = wsp[j].reshape(M, W9)
                 start = pl.multiple_of(rows.start + PAD, 8)
-                ppad[pl.ds(start, 128)] = dot(full, weights, NN)
+                ppad[pl.ds(start, 128)] = dot(fulla[j, rows], wsp[j].reshape(M, W9), NN)
                 return carry
 
             loop(R, 128, conv)
@@ -760,27 +790,14 @@
                 )
 
             taps_sum(ppad, False, put)
-            h = stats_start(second.at[j], C)
-            stats_finish(h, j, 1)
-            mu, inv, _, gain, shift = norm_of(j, 1, C)
-
-            def act_b(rows, carry):
-                y = live[rows] * (gain * ((second[j, rows] - mu) * inv) + shift)
-                ag_b[j, m, rows] = gelu(y).astype(BF16)
+            inner_norm(j, 1, second, ag_b, fullb, hooks[2])
+
+            def expand(rows, carry):
+                third[j, rows] = dot(fullb[j, rows], we[j].reshape(M, Wd), NN)
                 return carry
 
-            loop(R, 128, act_b)
-            base = spread("mp", lambda t: ag_b.at[j, m], lambda: ag_b.at[j, m])
-            hooks[2]()
-            gathered("mp", lambda src: ag_b.at[j, src], base)
-
-            def expand(rows, carry):
-                full = jnp.concatenate([ag_b[j, i, rows] for i in range(n_mp)], axis=1)
-                third[j, rows] = dot(full, we[j].reshape(M, Wd), NN)
-                return carry
-
             loop(R, 128, expand)
-            h = stats_start(third.at[j], Wd)
+            h, _ = stats_start(third.at[j], Wd)
             hooks[3]()
             stats_finish(h, j, 2)
             mu, inv, _, gain, shift = norm_of(j, 2, Wd)
@@ -795,7 +812,9 @@
 
             loop(R, 32, act_c)
 
-        def to_section(src, hbm, j, sem):
+        def to_section(src, hbm, j):
+            sem = recv.take()
+
             @pl.when(s == j)
             def _():
                 lsem = local.take()
@@ -807,27 +826,26 @@
             def _():
                 rcopy(src, lambda: hbm.at[0, s], sem, sib_dev, when=1 - j)
 
-        out_sems = [[recv.take() for _ in range(2)] for _ in range(2)]
-
-        g_sib = [recv.take() for _ in range(3)]
-        g_dp = [recv.take(n_dp) for _ in range(3)]
+            expected[sem] = on(lambda: s == j, lambda: arrive(hbm.at[0, o], sem))
+
         grads = ((gred, sibred, rred), (gspa, sibspa, rspa), (gexp, sibexp, rexp))
+        at_sib, at_dp = {}, {}
 
         def grad_to_sib(which, j):
             own, sib, _ = grads[which]
+            sem = at_sib[which, j] = recv.take()
 
             @pl.when(s != j)
             def _():
-                rcopy(lambda: own.at[j], lambda: sib, g_sib[which], sib_dev, when=1 - j)
+                rcopy(lambda: own.at[j], lambda: sib, sem, sib_dev, when=1 - j)
+
+            expected[sem] = on(lambda: s == j, lambda: arrive(sib, sem))
 
         def grad_to_dp(which, j):
             own, sib, got = grads[which]
-
-            @pl.when(s == j)
-            def _():
-                arrive(sib, g_sib[which])
-                depth = own.shape[2]
-
+            settle(at_sib[which, j])
+
+            def go():
                 def add(rows, carry):
                     for i in range(n_dp):
                         own[j, i, rows] = (
@@ -835,8 +853,17 @@
                         ).astype(BF16)
                     return carry
 
-                loop(depth, 64, add)
-                spread("dp", lambda t: own.at[j, t], lambda: got.at[d], when=j, base=g_dp[which])
+                loop(own.shape[2], 64, add)
+                base = spread(
+                    "dp",
+                    lambda t: own.at[j, t],
+                    lambda src: got.at[src],
+                    lambda: got.at[pl.ds(0, n_dp - 1)],
+                    when=j,
+                )
+                at_dp.setdefault(which, []).append(base)
+
+            pl.when(s == j)(go)
 
         def backward(j, hooks):
             mu, inv, count, gain, shift = norm_of(j, 2, Wd)
@@ -871,13 +898,13 @@
             loop(R, 32, d_third)
             h = product_to_rs(dth, lambda: we[j].reshape(M, Wd), NT)
             for i in range(n_dp):
-                full = cat(ag_b.at[j], n_mp)[:, i * Cd:(i + 1) * Cd]
+                full = fullb[j, :, i * Cd:(i + 1) * Cd]
                 gexp[j, i] = dot(full, dth[...], TN).astype(BF16)
             grad_to_sib(2, j)
             hooks[1]()
             rs_finish(h, hbuf)
 
-            def inner(i, src):
+            def inner_sums(i, src):
                 mu, inv, count, gain, shift = norm_of(j, i, C)
                 zero = (jnp.zeros((8, C), F32), jnp.zeros((8, C), F32))
 
@@ -891,58 +918,78 @@
 
                 sb, sg = loop(R, 128, up, zero)
                 sb, sg = total(sb), total(sg)
-                tile = sum(collect(exchange(rows_tile(sb, sg, sg))))
+                return exchange(rows_tile(sb, sg, sg)), sb
+
+            def inner_coeffs(i, handle):
+                _, inv, count, gain, _ = norm_of(j, i, C)
+                tile = sum(collect(handle))
                 vec[j, i:i + 1, 0:C] = tile[1:2]
                 vec[j, 2 + i:3 + i, 0:C] = tile[0:1]
-                sb_n, sg_n = tile[0:1] / count, tile[1:2] / count
-                scale = gain * inv
-
-                def grad_of(rows):
-                    xhat = (src[j, rows] - mu) * inv
-                    return live[rows] * scale * (hbuf[rows] - sb_n - xhat * sg_n)
-
-                return grad_of
-
-            grad_of = inner(1, second)
+                return gain * inv, tile[0:1] / count, tile[1:2] / count
+
+            scale_b, sb_b, sg_b = inner_coeffs(1, inner_sums(1, second)[0])
+            mu_b, inv_b = norm_of(j, 1, C)[:2]
 
             def d_second(rows, carry):
                 start = pl.multiple_of(rows.start + PAD, 8)
-                dpad[pl.ds(start, 128)] = grad_of(rows).astype(BF16).astype(F32)
+                xhat = (second[j, rows] - mu_b) * inv_b
+                out = live[rows] * scale_b * (hbuf[rows] - sb_b - xhat * sg_b)
+                dpad[pl.ds(start, 128)] = out.astype(BF16).astype(F32)
                 return carry
 
             loop(R, 128, d_second)
+
+            h = rs_open()
 
             def put(r0, summed):
                 for k in range(9):
                     dbuf[r0:r0 + 128, k * C:(k + 1) * C] = summed(
                         [2 * k, 2 * k + 1], slice(None)
                     ).astype(BF16)
+                rows = slice(r0, r0 + 128)
+                rs_rows(h, rows, dot(dbuf[rows], wsp[j].reshape(M, W9), NT))
 
             taps_sum(dpad, True, put)
-            h = product_to_rs(dbuf, lambda: wsp[j].reshape(M, W9), NT)
+            h[1].close()
             for i in range(n_dp):
-                full = cat(ag_a.at[j], n_mp)[:, i * Cd:(i + 1) * Cd]
+                full = fulla[j, :, i * Cd:(i + 1) * Cd]
                 gspa[j, i] = dot(full, dbuf[...], TN).astype(BF16)
             grad_to_sib(1, j)
             grad_to_dp(2, j)
             hooks[2]()
             rs_finish(h, hbuf)
-            grad_of = inner(0, first)
-
-            def d_first(rows, carry):
-                ag_d[j, m, rows] = grad_of(rows).astype(BF16)
-                return carry
-
-            loop(R, 128, d_first)
-            base = spread("mp", lambda t: ag_d.at[j, m], lambda: ag_d.at[j, m])
+            handle, sb_here = inner_sums(0, first)
+            here = sb_here / jnp.maximum(nloc, 1.0)
+            group = slots_out(ag_d, j, lambda rows: hbuf[rows] - here)
+            scale, sb_a, sg_a = inner_coeffs(0, handle)
+            own = co[2 * j, m]
+            sent = coeffs_out(
+                4 + j,
+                scale,
+                -scale * sg_a * own[2:3],
+                scale * (here - sb_a - sg_a * own[3:4]),
+            )
             grad_to_dp(1, j)
             hooks[3]()
-            gathered("mp", lambda src: ag_d.at[j, src], base)
+            settle(group)
+            settle(sent)
+
+            def d_first(rows, carry):
+                for c in range(n_mp):
+                    tile = co[4 + j, c]
+                    out = live[rows] * (
+                        ag_d[j, c, rows].astype(F32) * tile[0:1]
+                        + ag_a[j, c, rows].astype(F32) * tile[1:2]
+                        + tile[2:3]
+                    )
+                    dfull[j, rows, c * C:(c + 1) * C] = out.astype(BF16)
+                return carry
+
+            loop(R, 64, d_first)
 
             def d_input():
                 def body(rows, carry):
-                    full = jnp.concatenate([ag_d[j, i, rows] for i in range(n_mp)], axis=1)
-                    out = dot(full, cat(wr.at[j], n_dp), NT) + dpre[rows]
+                    out = dot(dfull[j, rows], cat(wr.at[j], n_dp), NT) + dpre[rows]
                     if j == 1:
                         out = out.astype(BF16).astype(F32)
                         evec[rows] = out
@@ -950,59 +997,58 @@
                     return carry
 
                 loop(R, 128, body)
-                to_section(lambda: ig.at[j], ig_hbm, j, out_sems[1][j])
+                to_section(lambda: ig.at[j], ig_hbm, j)
 
             def g_reduce():
                 for i in range(n_dp):
-                    full = cat(ag_d.at[j], n_mp)[:, i * Cd:(i + 1) * Cd]
+                    full = dfull[j, :, i * Cd:(i + 1) * Cd]
                     gred[j, i] = dot(xin[j], full, TN).astype(BF16)
                 grad_to_sib(0, j)
 
             return d_input, g_reduce
 
-        pass_on(wr, b_red, f_red, 0)
-        l_x.wait()
-        from_sib(wr, f_red, 0)
-
-        @pl.when(s == 1)
-        def _():
-            send_own(wr, b_red, 1)
-            send_own(wsp, b_spa, 1)
-            send_own(we, b_exp, 1)
-
-        arrive(par.at[o], par_sem)
+        pass_on(wr, 0)
+        settle(l_x)
+        from_sib(wr, 0)
+        settle(par_sem)
 
         def f00():
-            pass_on(wsp, b_spa, f_spa, 0)
-            to_all(lambda t: hd.at[mine], lambda: hd.at[mine], b_head)
+            send_own(wsp, 0)
 
         def f01():
-            pass_on(we, b_exp, f_exp, 0)
-            from_sib(wsp, f_spa, 0)
+            pass_on(wsp, 0)
+            send_own(we, 0)
+            send_own(wr, 1)
+            from_sib(wsp, 0)
 
         def f02():
-            pass_on(wr, b_red, f_red, 1)
-            from_sib(we, f_exp, 0)
+            pass_on(we, 0)
+            pass_on(wr, 1)
+            send_own(wsp, 1)
+            from_sib(we, 0)
 
         def f03():
-            pass_on(wsp, b_spa, f_spa, 1)
-            from_sib(wr, f_red, 1)
-
+            from_sib(wr, 1)
+
+        hold = {}
         forward(0, (f00, f01, f02, f03))
 
         def f10():
-            to_section(lambda: xin.at[1], act_hbm, 0, out_sems[0][0])
-            pass_on(we, b_exp, f_exp, 1)
+            pass_on(wsp, 1)
+            send_own(we, 1)
+            hold["heads"] = to_all(lambda t: hd.at[mine], hd)
+            to_section(lambda: xin.at[1], act_hbm, 0)
 
         def f11():
-            from_sib(wsp, f_spa, 1)
+            pass_on(we, 1)
+            from_sib(wsp, 1)
 
         def f12():
-            from_sib(we, f_exp, 1)
+            from_sib(we, 1)
 
         forward(1, (f10, f11, f12, nothing))
 
-        from_all(lambda src: hd.at[src], b_head)
+        settle(hold["heads"])
         RM = R // n_mp
         n_cls = n_sec * n_dp
 
@@ -1015,10 +1061,12 @@
                 lg_s[c, :, t * classes:(t + 1) * classes] = dot(rows, heads_of(t), NT).astype(
                     lg_s.dtype
                 )
-        base = spread("mp", lambda t: lg_s.at[t], lambda: lg_r.at[m])
-        to_section(lambda: act1, act_hbm, 1, out_sems[0][1])
-        l_thr.wait()
-        gathered("mp", lambda src: lg_r.at[src], base)
+        base = spread(
+            "mp", lambda t: lg_s.at[t], lambda src: lg_r.at[src], lambda: lg_r.at[pl.ds(0, n_mp - 1)]
+        )
+        to_section(lambda: act1, act_hbm, 1)
+        settle(l_thr)
+        settle(base)
         here = pl.ds(pl.multiple_of(m * RM, RM), RM)
         lv = wide(live[here], classes)
         for t in range(tasks):
@@ -1031,8 +1079,9 @@
             ids = lax.broadcasted_iota(jnp.int32, (RM, classes), 1).astype(F32)
             hot = (ids == labc[here, t:t + 1]).astype(F32)
             dl[m, :, lanes] = (LOSS_WEIGHT * lv * (soft - hot)).astype(BF16)
-        base = spread("mp", lambda t: dl.at[m], lambda: dl.at[m])
-        gathered("mp", lambda src: dl.at[src], base)
+        settle(spread(
+            "mp", lambda t: dl.at[m], lambda src: dl.at[src], lambda: dl.at[pl.ds(0, n_mp - 1)]
+        ))
 
         def merge_block(c):
             for t in range(tasks):
@@ -1060,16 +1109,13 @@
             merge_block(c)
 
         def b10():
-            b_gh = recv.take(n_cls)
             for t in range(tasks):
                 lanes = slice(t * classes, (t + 1) * classes)
                 delta = dl[:, :, lanes].reshape(R, classes)
                 out = dot(delta, act1[...], TN).astype(BF16)
                 ghead[:, t] = out.reshape(n_cls, piece, Wd)
-            to_all(lambda t: ghead.at[t], lambda: rhead.at[mine], b_gh)
-            hold["b_gh"] = b_gh
-
-        hold = {}
+            hold["ghead"] = to_all(lambda t: ghead.at[t], rhead)
+
         late1 = backward(1, (b10, nothing, nothing, nothing))
         late1[0]()
 
@@ -1084,15 +1130,18 @@
         late0[0]()
         vec_sem = recv.take()
         rcopy(lambda: vec.at[o], lambda: vsib, vec_sem, sib_dev)
-
-        from_all(lambda src: rhead.at[src], hold["b_gh"])
+        expected[vec_sem] = lambda: arrive(vsib, vec_sem)
+
+        settle(hold["ghead"])
         for t in range(tasks):
             total = ghead[mine, t].astype(F32)
             for k in range(1, n_cls):
                 total = total + rhead[rem(mine + k, n_cls), t].astype(F32)
             ohead[t] = total
-        arrive(vsib, vec_sem)
+        load(ohead, head_out)
+        settle(vec_sem)
         ovec[...] = vec[s] + vsib[...]
+        load(ovec, vec_hbm)
         grad_to_dp(0, 0)
 
         def total_of(own, got, rows):
@@ -1101,9 +1150,10 @@
                 out = out + got[rem(d + k, n_dp), rows].astype(F32)
             return out
 
-        for which in (2, 1, 0):
+        def finish_grad(which):
             own, _, got = grads[which]
-            gathered("dp", lambda src: got.at[src], g_dp[which])
+            for key in at_dp[which]:
+                settle(key)
 
             def finish(rows, carry):
                 out = total_of(own, got, rows)
@@ -1115,12 +1165,13 @@
                 return carry
 
             loop(own.shape[2], 64, finish)
-
-        for j in range(2):
-            @pl.when(s == j)
-            def _():
-                for i, hbm in enumerate((act_hbm, ig_hbm)):
-                    arrive(hbm.at[0, o], out_sems[i][j])
+            load((ored, ospa, oexp)[which], (red_hbm, spa_hbm, exp_hbm)[which])
+
+        finish_grad(2)
+        finish_grad(1)
+        finish_grad(0)
+        for key in list(expected):
+            settle(key)
 
         for key, waits in pending.items():
             def finish_all(waits=waits):
@@ -1141,13 +1192,13 @@
     RM = R // n_mp
     vmem = lambda shape, dtype: pltpu.VMEM(shape, dtype)
     scratch = [
-        pltpu.SemaphoreType.DMA((300,)),
-        pltpu.SemaphoreType.DMA((300,)),
-        pltpu.SemaphoreType.DMA((16,)),
+        pltpu.SemaphoreType.DMA((64,)),
+        pltpu.SemaphoreType.DMA((64,)),
+        pltpu.SemaphoreType.DMA((15,)),
         vmem((Wd, Cd), F32),
         vmem((9, Cd, C), F32),
         vmem((Cd, Wd), F32),
-        vmem((tasks, Wd, piece), F32),
+        vmem((tasks, piece, Wd), F32),
         vmem((R, Wd), F32),
         vmem((2, R, Wd), BF16),
         vmem((2, n_dp, Wd, Cd), BF16),
@@ -1164,6 +1215,10 @@
         vmem((2, n_mp, R, C), BF16),
         vmem((2, n_mp, R, C), BF16),
         vmem((2, n_mp, R, C), BF16),
+        vmem((2, R, M), BF16),
+        vmem((2, R, M), BF16),
+        vmem((2, R, M), BF16),
+        vmem((6, n_mp, 8, C), F32),
         vmem((12, n_dp, 8, Wd), F32),
         vmem((2, 3, 8, Wd), F32),
         vmem((2, R, C), F32),
@@ -1195,6 +1250,11 @@
         vmem((n_cls, tasks, piece, Wd), BF16),
         vmem((2, 8, Wd), F32),
         vmem((8, Wd), F32),
+        vmem((1, Wd, Cd), F32),
+        vmem((1, 9, Cd, C), F32),
+        vmem((1, Cd, Wd), F32),
+        vmem((8, Wd), F32),
+        vmem((tasks, piece, Wd), F32),
     ]
     in_vmem = pl.BlockSpec(memory_space=pltpu.VMEM)
     in_any = pl.BlockSpec(memory_space=pl.ANY)
@@ -1214,30 +1274,65 @@
             in_any, in_vmem, in_any, in_any, in_any, in_vmem, in_vmem, in_vmem, in_vmem,
             in_any, in_vmem, in_any,
         ],
-        out_specs=(in_any, in_any, in_vmem, in_vmem, in_vmem, in_vmem, in_vmem),
+        out_specs=(in_any,) * 7,
         scratch_shapes=scratch,
         compiler_params=pltpu.CompilerParams(
             collective_id=0, has_side_effects=True, vmem_limit_bytes=60 * 2**20
         ),
-    )(*args)
-    act, grads_in, g_red, g_spa, g_exp, vec, head = out
+    )(*args[:9], jnp.transpose(args[9], (0, 2, 1)), *args[10:])
+    part, outer = C // n_dp, Wd // n_dp
+    shapes = (
+        whole((1, 2, R, Wd), BF16),
+        whole((1, 2, R, Wd)),
+        whole((1, Wd, Cd)),
+        whole((1, 9, Cd, C)),
+        whole((1, Cd, Wd)),
+        whole((1, 2, 1, part)),
+        whole((1, 2, 1, part)),
+        whole((1, 1, outer)),
+        whole((1, 1, outer)),
+        whole((tasks, piece, Wd)),
+    )
+    done = pl.pallas_call(
+        hand_out,
+        out_shape=shapes,
+        in_specs=[in_any] * 5 + [in_vmem, in_any],
+        out_specs=(in_any,) * 5 + (in_vmem,) * 4 + (in_any,),
+        scratch_shapes=[pltpu.VMEM(a.shape, a.dtype) for a in shapes[:5] + shapes[9:]]
+        + [pltpu.SemaphoreType.DMA((16,)), pltpu.SemaphoreType.DMA((16,))],
+    )(*out)
+    return done[:9] + (jnp.transpose(done[9], (0, 2, 1)),)
+
+
+def hand_out(*refs):
+    given, outs, held, came, left = refs[:7], refs[7:17], refs[17:23], refs[23], refs[24]
+    vec, gains, shifts, gain_out, shift_out = given[5], *outs[5:9]
+    pieces = []
+    for src, mid, dst in zip(given[:5] + given[6:], held, outs[:5] + outs[9:]):
+        for i in range(src.shape[1]) if len(src.shape) == 4 else (None,):
+            at = (lambda ref, i=i: ref) if i is None else (lambda ref, i=i: ref.at[0, i])
+            n = len(pieces)
+            pieces.append((
+                pltpu.make_async_copy(at(src), at(mid), came.at[n]),
+                pltpu.make_async_copy(at(mid), at(dst), left.at[n]),
+            ))
+    for fetch, _ in pieces:
+        fetch.start()
     d = lax.axis_index("dp")
-    part = C // n_dp
-    outer = Wd // n_dp
-    inner = lambda rows: lax.dynamic_slice_in_dim(vec[rows, :C], d * part, part, 1)[None, :, None]
-    outer_of = lambda row: lax.dynamic_slice_in_dim(vec[row, :], d * outer, outer, 0)[None, None]
-    return (
-        act,
-        grads_in,
-        g_red,
-        g_spa,
-        g_exp,
-        inner(slice(0, 2)),
-        inner(slice(2, 4)),
-        outer_of(4),
-        outer_of(5),
-        jnp.transpose(head, (0, 2, 1)),
-    )
+    part, outer = gains.shape[3], gain_out.shape[2]
+    lanes = part * lax.axis_size("dp")
+    rolled = pltpu.roll(vec[:, 0:lanes], lax.rem(lanes - d * part, lanes), 1)
+    for i in range(2):
+        gains[0, i] = rolled[i:i + 1, 0:part]
+        shifts[0, i] = rolled[2 + i:3 + i, 0:part]
+    mine = pl.ds(pl.multiple_of(d * outer, outer), outer)
+    gain_out[0] = vec[4:5, mine]
+    shift_out[0] = vec[5:6, mine]
+    for fetch, store in pieces:
+        fetch.wait()
+        store.start()
+    for _, store in pieces:
+        store.wait()
 
 
 def per_device(*args):

time: 220 us -> 187 us (0.85)
  Pallas kernels: 208 us -> 186 us
  local copies, waits for them, and re-layouts: 10.9 us -> 0 us
    pallas_call x1, Pallas kernels: 208 us -> 182 us  [fused_device(): pl.pallas_call(make_kernel(sizes), out_shape=(whole((1, 2, R, Wd), BF16),...]
    unnamed x17 -> x0, local copies, waits for them, and re-layouts: 8.13 us -> none
    pallas_call x0 -> x1, Pallas kernels: none -> 4.47 us  [fused_device(): pl.pallas_call(hand_out, out_shape=shapes, in_specs=[in_any] * 5 + [in_vm...]
where the time goes in v2:
time: 187 us
  Pallas kernels  186 us (99%)
    pallas_call x1, Pallas kernels, fused_device(): pl.pallas_call(make_kernel(sizes), out_shape=(whole((1, 2, R, Wd), BF16),...  182 us
    pallas_call x1, Pallas kernels, fused_device(): pl.pallas_call(hand_out, out_shape=shapes, in_specs=[in_any] * 5 + [in_vm...  4.47 us

profile of v2, /device:TPU:0, one launch (start us, length us, event | category | flops | bytes accessed | tf_op | source)
XLA Modules:
  0.0 186.8 jit_solution(9819116669220689373)
XLA Ops:
  0.6 181.7 %shard_map.195 = (bf16[1,2,384,512]{3,2,1,0:T(8,128)(2,1)}, f32[1,2,384,512]{3,2,1,0:T(8,128)}, f32[1,512,128]{2,1,0:T(8,128)}, f32[1,9,128,128]{3,2,1,0:T(8,128...) custom-call(bf16[2,384,512]{2,1,0:T(8,128)(2,1)} %refs_0_.1, s32[2,1,96]{2,1,0:T(1,128)} %refs_1_.1, ...), custom_call_target="tpu_custom_call" | custom-call | tf_op jit(solution)/shard_map/pallas_call | solution.py:1262
  182.3 4.5 %shard_map.196 = (bf16[1,2,384,512]{3,2,1,0:T(8,128)(2,1)}, f32[1,2,384,512]{3,2,1,0:T(8,128)}, f32[1,512,128]{2,1,0:T(8,128)}, f32[1,9,128,128]{3,2,1,0:T(8,128...) custom-call(bf16[1,2,384,512]{3,2,1,0:T(8,128)(2,1)} %get-tuple-elem, ...), custom_call_target="tpu_custom_call" | custom-call | tf_op jit(solution)/shard_map/pallas_call | solution.py:1296

commit v3 on v2

--- a/solution.py
+++ b/solution.py
@@ -405,11 +405,11 @@
             x_hbm, sides_ref, wred_hbm, wspa_hbm, wexp_hbm, gin_ref, sin_ref, gout_ref, sout_ref,
             head_hbm, lab_ref, thr_hbm,
             act_hbm, ig_hbm, red_hbm, spa_hbm, exp_hbm, vec_hbm, head_out,
-            ssems, rsems, lsems,
+            ssems, rsems, lsems, go,
             sred, sspa, sexp, shead, thr, xin, wr, wsp, we, hd, par,
             live, geo, masks, labc,
-            rs_s, rs_r, ag_a, ag_b, ag_d, fulla, fullb, dfull, co, st, keep, first, second, third, ppad, dpad, dbuf,
-            lg_s, lg_r, dl, act1, tg, dpre, evec, dth, hbuf, ig,
+            rs_s, rs_r, ag_a, ag_b, ag_d, fulla, fullb, co, sums_s, sums_r, st, keep, first, second, third, ppad, dpad, dbuf,
+            lg_s, lg_r, dl, act1, tg, dpre, evec, dth, ig, slope, steep,
             gred, gspa, gexp, sibred, sibspa, sibexp, rred, rspa, rexp, ghead, rhead, vec, vsib,
             ored, ospa, oexp, ovec, ohead,
         ) = refs
@@ -469,22 +469,36 @@
             return lambda: pl.when(cond())(what)
 
         class Group:
-            def __init__(self, axis, all_of, when=None):
+            def __init__(self, axis, all_of, when=None, slot_of=None):
                 self.n, self.me, self.dev = axes[axis]
-                self.ssem, self.rsem = send.take(), recv.take()
-                self.all_of, self.when = all_of, when
+                self.ssem = send.take()
+                self.rsem = recv.take(1 if slot_of is None else self.n - 1)
+                self.all_of, self.when, self.slot_of = all_of, when, slot_of
 
             def put(self, src_of, slot_of):
                 for k in range(1, self.n):
                     t = rem(self.me + k, self.n)
-                    put_to(src_of(t), slot_of(self.me), self.ssem, self.rsem, self.dev(t))
+                    rsem = self.rsem + (0 if self.slot_of is None else k - 1)
+                    put_to(src_of(t), slot_of(self.me), self.ssem, rsem, self.dev(t))
+
+            def came_from(self, k):
+                return rem(self.me + self.n - k, self.n)
 
             def close(self):
-                ssem, rsem, all_of, when = self.ssem, self.rsem, self.all_of, self.when
+                ssem, all_of, when = self.ssem, self.all_of, self.when
                 pending[when].append(lambda: waiter(all_of(), ssem, 0).wait_send())
-                wait = lambda: arrive(all_of(), rsem)
-                expected[rsem] = wait if when is None else on(lambda: s == when, wait)
-                return rsem
+                if self.slot_of is None:
+                    waits = {self.rsem: lambda: arrive(all_of(), self.rsem)}
+                else:
+                    waits = {
+                        self.rsem + k - 1: lambda k=k: arrive(
+                            self.slot_of(self.came_from(k)), self.rsem + k - 1
+                        )
+                        for k in range(1, self.n)
+                    }
+                for key, wait in waits.items():
+                    expected[key] = wait if when is None else on(lambda: s == when, wait)
+                return self.rsem
 
         def spread(axis, src_of, slot_of, all_of, when=None):
             group = Group(axis, all_of, when)
@@ -556,7 +570,18 @@
         par_sem = recv.take()
         rcopy(lambda: par.at[s], lambda: par.at[s], par_sem, sib_dev)
         expected[par_sem] = lambda: arrive(par.at[o], par_sem)
-        send_own(wr, 0)
+        early = Group(
+            "dp",
+            lambda: wr.at[0, pl.ds(0, n_dp - 1)],
+            when=0,
+            slot_of=lambda src: wr.at[0, src],
+        )
+
+        @pl.when(s == 0)
+        def _():
+            early.put(lambda t: wr.at[0, d], lambda src: wr.at[0, src])
+
+        early.close()
 
         settle(l_spa)
         for k in range(9):
@@ -643,10 +668,7 @@
             settle(group.rsem)
 
             def add(rows, carry):
-                total = rs_s[p, m, rows].astype(F32)
-                for k in range(1, n_mp):
-                    total = total + rs_r[p, rem(m + k, n_mp), rows].astype(F32)
-                dst[rows] = total
+                dst[rows] = rs_sum(handle, rows)
                 return carry
 
             loop(R, 128, add)
@@ -676,14 +698,16 @@
             settle(base)
             return [st[p, i, :, 0:width] for i in range(n_dp)]
 
-        def stats_start(buf, width):
+        def stats_start(buf, width, total=None):
             chunk = 128 if width <= 128 else 32
             zero = jnp.zeros((8, width), F32)
 
             def sum_up(rows, carry):
                 return carry + fold(buf[rows] * wide(live[rows], width))
 
-            total = jnp.sum(loop(R, chunk, sum_up, zero), axis=0, keepdims=True)
+            if total is None:
+                total = loop(R, chunk, sum_up, zero)
+            total = jnp.sum(total, axis=0, keepdims=True)
             count = wide(nloc, width)
             mean = total / jnp.maximum(count, 1.0)
 
@@ -706,16 +730,67 @@
             inv = lax.rsqrt(sqs / count + NORM_EPS)
             keep[j, i, :, 0:width] = rows_tile(mean, inv, count)
 
-        def slots_out(buf, at, values_of):
-            group = Group("mp", lambda: buf.at[at, pl.ds(0, n_mp - 1)])
-
-            def fill(rows, carry):
-                buf[at, m, rows] = values_of(rows).astype(BF16)
-                group.put(lambda t: buf.at[at, m, rows], lambda src: buf.at[at, src, rows])
-                return carry
-
-            loop(R, 128, fill)
-            return group.close()
+        spans = [slice(r0, r0 + 128) for r0 in range(0, R, 128)]
+
+        def rows_out(buf, at, rows, values):
+            buf[at, m, rows] = values.astype(BF16)
+            return spread(
+                "mp",
+                lambda t: buf.at[at, m, rows],
+                lambda src: buf.at[at, src, rows],
+                lambda: buf.at[at, pl.ds(0, n_mp - 1), rows],
+            )
+
+        def rs_rows_sums(handle, j, i, rows, out, carry):
+            p, group = handle
+            sb, sg = carry
+            raw = (ag_a, ag_b)[i]
+            for c in range(n_mp):
+                part = out[:, c * C:(c + 1) * C]
+                rs_s[p, c, rows] = part.astype(BF16)
+                tile = co[2 * j + i, c]
+                g = part * slope[j, i, c, rows]
+                xhat = raw[j, c, rows].astype(F32) * tile[2:3] + tile[3:4]
+                sb[c] = sb[c] + fold(g)
+                sg[c] = sg[c] + fold(g * xhat)
+            if rows is not spans[-1]:
+                group.put(lambda t: rs_s.at[p, t, rows], lambda src: rs_r.at[p, src, rows])
+
+        def rs_sums_out(handle, carry):
+            p, group = handle
+            sb, sg = carry
+            total = lambda v: jnp.sum(v, axis=0, keepdims=True)
+            for c in range(n_mp):
+                b, g = total(sb[c]), total(sg[c])
+                sums_s[p, c] = rows_tile(b, g, g)
+            ssem, rsem = send.take(), recv.take()
+            others = [(a, k) for a in range(n_mp) for k in range(n_dp) if a or k]
+            me = m * n_dp + d
+            for a, k in others:
+                tz, td = rem(m + a, n_mp), rem(d + k, n_dp)
+                put_to(sums_s.at[p, tz], sums_r.at[p, me], ssem, rsem, (s, td, tz))
+            rows = spans[-1]
+            group.put(lambda t: rs_s.at[p, t, rows], lambda src: rs_r.at[p, src, rows])
+            group.close()
+            rest = lambda: sums_r.at[p, pl.ds(0, len(others))]
+            pending[None].append(lambda: waiter(rest(), ssem, 0).wait_send())
+            expected[rsem] = lambda: arrive(rest(), rsem)
+
+            def collect_sums():
+                settle(rsem)
+                tile = sums_s[p, m]
+                for a, k in others:
+                    tile = tile + sums_r[p, rem(m + a, n_mp) * n_dp + rem(d + k, n_dp)]
+                return tile
+
+            return collect_sums
+
+        def rs_sum(handle, rows):
+            p, _ = handle
+            out = rs_s[p, m, rows].astype(F32)
+            for k in range(1, n_mp):
+                out = out + rs_r[p, rem(m + k, n_mp), rows].astype(F32)
+            return out
 
         def coeffs_out(at, *values):
             place = lax.broadcasted_iota(jnp.int32, (8, C), 0)
@@ -726,26 +801,26 @@
             slot = lambda src: co.at[at, src]
             return spread("mp", lambda t: slot(m), slot, lambda: co.at[at, pl.ds(0, n_mp - 1)])
 
-        def inner_norm(j, i, src, raw, full, hook):
+        def inner_norm(j, i, src, raw, full, hook, need, consume):
             at = 2 * j + i
             handle, mean_here = stats_start(src.at[j], C)
-            group = slots_out(raw, j, lambda rows: src[j, rows] - mean_here)
+            push = lambda rows: rows_out(raw, j, rows, src[j, rows] - mean_here)
+            groups = [push(rows) for rows in spans[:-1]]
             hook()
             stats_finish(handle, j, i)
             mu, inv, _, gain, shift = norm_of(j, i, C)
             moved = (mean_here - mu) * inv
             sent = coeffs_out(at, gain * inv, gain * moved + shift, inv, moved)
-            settle(group)
+            groups.append(push(spans[-1]))
+            need()
             settle(sent)
-
-            def act(rows, carry):
+            for rows, group in zip(spans, groups):
+                settle(group)
                 for c in range(n_mp):
                     tile = co[at, c]
                     y = live[rows] * (raw[j, c, rows].astype(F32) * tile[0:1] + tile[1:2])
                     full[j, rows, c * C:(c + 1) * C] = gelu(y).astype(BF16)
-                return carry
-
-            loop(R, 64, act)
+                consume(rows)
 
         def norm_of(j, i, width):
             tile = keep[j, i, :, 0:width]
@@ -770,19 +845,35 @@
         nothing = lambda: None
         vec[...] = jnp.zeros(vec.shape, F32)
 
-        def forward(j, hooks):
-            x = xin.at[j]
-            h = product_to_rs(x, lambda: cat(wr.at[j], n_dp), NN)
+        def prepare(j):
+            for i, raw in enumerate((ag_a, ag_b)):
+                def inner(rows, carry):
+                    for c in range(n_mp):
+                        tile = co[2 * j + i, c]
+                        y = live[rows] * (raw[j, c, rows].astype(F32) * tile[0:1] + tile[1:2])
+                        slope[j, i, c, rows] = live[rows] * gelu_grad(y)
+                    return carry
+
+                loop(R, 64, inner)
+            mu, inv, _, gain, shift = norm_of(j, 2, Wd)
+
+            def outer(rows, carry):
+                lv = wide(live[rows], Wd)
+                pre = lv * (gain * ((third[j, rows] - mu) * inv) + shift)
+                steep[j, rows] = lv * gelu_grad(pre + xin[j, rows].astype(F32))
+                return carry
+
+            loop(R, 32, outer)
+
+        def forward(j, h, hooks, needs):
             hooks[0]()
             rs_finish(h, first.at[j])
-            inner_norm(j, 0, first, ag_a, fulla, hooks[1])
-
-            def conv(rows, carry):
-                start = pl.multiple_of(rows.start + PAD, 8)
-                ppad[pl.ds(start, 128)] = dot(fulla[j, rows], wsp[j].reshape(M, W9), NN)
-                return carry
-
-            loop(R, 128, conv)
+
+            def conv(rows):
+                there = slice(PAD + rows.start, PAD + rows.stop)
+                ppad[there] = dot(fulla[j, rows], wsp[j].reshape(M, W9), NN)
+
+            inner_norm(j, 0, first, ag_a, fulla, hooks[1], needs[0], conv)
 
             def put(r0, summed):
                 second[j, r0:r0 + 128] = sum(
@@ -790,14 +881,17 @@
                 )
 
             taps_sum(ppad, False, put)
-            inner_norm(j, 1, second, ag_b, fullb, hooks[2])
-
-            def expand(rows, carry):
-                third[j, rows] = dot(fullb[j, rows], we[j].reshape(M, Wd), NN)
-                return carry
-
-            loop(R, 128, expand)
-            h, _ = stats_start(third.at[j], Wd)
+            if j == 0:
+                pass_on(wr, 1)
+            sums = []
+
+            def expand(rows):
+                out = dot(fullb[j, rows], we[j].reshape(M, Wd), NN)
+                third[j, rows] = out
+                sums.append(fold(out * wide(live[rows], Wd)))
+
+            inner_norm(j, 1, second, ag_b, fullb, hooks[2], needs[1], expand)
+            h, _ = stats_start(third.at[j], Wd, sum(sums))
             hooks[3]()
             stats_finish(h, j, 2)
             mu, inv, _, gain, shift = norm_of(j, 2, Wd)
@@ -865,20 +959,49 @@
 
             pl.when(s == j)(go)
 
-        def backward(j, hooks):
+        def reduce_to_sib(j):
+            for i in range(n_dp):
+                gred[j, i] = dot(xin[j], ag_d[j, i], TN).astype(BF16)
+                sem = at_sib[0, j, i] = recv.take()
+
+                @pl.when(s != j)
+                def _():
+                    rcopy(lambda: gred.at[j, i], lambda: sibred.at[i], sem, sib_dev, when=1 - j)
+
+                expected[sem] = on(
+                    lambda: s == j, lambda i=i, sem=sem: arrive(sibred.at[i], sem)
+                )
+
+        def reduce_to_dp(j):
+            group = Group("dp", lambda: rred.at[pl.ds(0, n_dp - 1)], when=j)
+            for i in range(n_dp):
+                settle(at_sib[0, j, i])
+
+                @pl.when(s == j)
+                def _():
+                    def add(rows, carry):
+                        gred[j, i, rows] = (
+                            gred[j, i, rows].astype(F32) + sibred[i, rows].astype(F32)
+                        ).astype(BF16)
+                        return carry
+
+                    loop(Wd, 128, add)
+
+                    @pl.when(d != i)
+                    def _():
+                        put_to(gred.at[j, i], rred.at[d], group.ssem, group.rsem, dp_dev(i))
+
+            at_dp.setdefault(0, []).append(group.close())
+
+        def steepest(j, rows, e, carry):
+            mu, inv, _, _, _ = norm_of(j, 2, Wd)
+            out = steep[j, rows] * e
+            dpre[rows] = out
+            return carry[0] + fold(out), carry[1] + fold(out * ((third[j, rows] - mu) * inv))
+
+        def backward(j, sums, hooks):
             mu, inv, count, gain, shift = norm_of(j, 2, Wd)
-            zero = (jnp.zeros((8, Wd), F32), jnp.zeros((8, Wd), F32))
-
-            def top(rows, carry):
-                sb, sg = carry
-                lv = wide(live[rows], Wd)
-                xhat = (third[j, rows] - mu) * inv
-                pre = lv * (gain * xhat + shift) + xin[j, rows].astype(F32)
-                dp_ = gelu_grad(pre) * lv * evec[rows]
-                dpre[rows] = dp_
-                return sb + fold(dp_), sg + fold(dp_ * xhat)
-
-            sb, sg = loop(R, 32, top, zero)
+            sb, sg = sums
             total = lambda v: jnp.sum(v, axis=0, keepdims=True)
             sb, sg = total(sb), total(sg)
             h = exchange(rows_tile(sb, sg, sg))
@@ -895,158 +1018,162 @@
                 dth[rows] = (lv * scale * (dpre[rows] - sb_n - xhat * sg_n)).astype(BF16)
                 return carry
 
-            loop(R, 32, d_third)
-            h = product_to_rs(dth, lambda: we[j].reshape(M, Wd), NT)
+            none = lambda: ([jnp.zeros((8, C), F32)] * n_mp, [jnp.zeros((8, C), F32)] * n_mp)
+            h, carry = rs_open(), none()
+            for rows in spans:
+                for r0 in range(rows.start, rows.stop, 32):
+                    d_third(slice(r0, r0 + 32), 0)
+                out = dot(dth[rows], we[j].reshape(M, Wd), NT)
+                rs_rows_sums(h, j, 1, rows, out, carry)
+            sums_of = rs_sums_out(h, carry)
             for i in range(n_dp):
                 full = fullb[j, :, i * Cd:(i + 1) * Cd]
                 gexp[j, i] = dot(full, dth[...], TN).astype(BF16)
             grad_to_sib(2, j)
             hooks[1]()
-            rs_finish(h, hbuf)
-
-            def inner_sums(i, src):
-                mu, inv, count, gain, shift = norm_of(j, i, C)
-                zero = (jnp.zeros((8, C), F32), jnp.zeros((8, C), F32))
-
-                def up(rows, carry):
-                    sb, sg = carry
-                    xhat = (src[j, rows] - mu) * inv
-                    pre = live[rows] * (gain * xhat + shift)
-                    g = live[rows] * gelu_grad(pre) * hbuf[rows]
-                    hbuf[rows] = g
-                    return sb + fold(g), sg + fold(g * xhat)
-
-                sb, sg = loop(R, 128, up, zero)
-                sb, sg = total(sb), total(sg)
-                return exchange(rows_tile(sb, sg, sg)), sb
-
-            def inner_coeffs(i, handle):
-                _, inv, count, gain, _ = norm_of(j, i, C)
-                tile = sum(collect(handle))
+            settle(h[1].rsem)
+
+            def norm_grad(i, src, tile):
+                mu, inv, count, gain, _ = norm_of(j, i, C)
                 vec[j, i:i + 1, 0:C] = tile[1:2]
                 vec[j, 2 + i:3 + i, 0:C] = tile[0:1]
-                return gain * inv, tile[0:1] / count, tile[1:2] / count
-
-            scale_b, sb_b, sg_b = inner_coeffs(1, inner_sums(1, second)[0])
-            mu_b, inv_b = norm_of(j, 1, C)[:2]
-
-            def d_second(rows, carry):
-                start = pl.multiple_of(rows.start + PAD, 8)
-                xhat = (second[j, rows] - mu_b) * inv_b
-                out = live[rows] * scale_b * (hbuf[rows] - sb_b - xhat * sg_b)
-                dpad[pl.ds(start, 128)] = out.astype(BF16).astype(F32)
-                return carry
-
-            loop(R, 128, d_second)
-
-            h = rs_open()
+                sb_n, sg_n, scale = tile[0:1] / count, tile[1:2] / count, gain * inv
+
+                def grad_of(rows, h):
+                    xhat = (src[j, rows] - mu) * inv
+                    g = slope[j, i, m, rows] * rs_sum(h, rows)
+                    return live[rows] * scale * (g - sb_n - xhat * sg_n)
+
+                return grad_of
+
+            grad_of = norm_grad(1, second, sums_of())
+            for rows in spans:
+                there = slice(PAD + rows.start, PAD + rows.stop)
+                dpad[there] = grad_of(rows, h).astype(BF16).astype(F32)
+
+            h, carry = rs_open(), none()
 
             def put(r0, summed):
                 for k in range(9):
                     dbuf[r0:r0 + 128, k * C:(k + 1) * C] = summed(
                         [2 * k, 2 * k + 1], slice(None)
                     ).astype(BF16)
-                rows = slice(r0, r0 + 128)
-                rs_rows(h, rows, dot(dbuf[rows], wsp[j].reshape(M, W9), NT))
+                rows = spans[r0 // 128]
+                out = dot(dbuf[rows], wsp[j].reshape(M, W9), NT)
+                rs_rows_sums(h, j, 0, rows, out, carry)
 
             taps_sum(dpad, True, put)
-            h[1].close()
+            sums_of = rs_sums_out(h, carry)
             for i in range(n_dp):
                 full = fulla[j, :, i * Cd:(i + 1) * Cd]
                 gspa[j, i] = dot(full, dbuf[...], TN).astype(BF16)
             grad_to_sib(1, j)
             grad_to_dp(2, j)
             hooks[2]()
-            rs_finish(h, hbuf)
-            handle, sb_here = inner_sums(0, first)
-            here = sb_here / jnp.maximum(nloc, 1.0)
-            group = slots_out(ag_d, j, lambda rows: hbuf[rows] - here)
-            scale, sb_a, sg_a = inner_coeffs(0, handle)
-            own = co[2 * j, m]
-            sent = coeffs_out(
-                4 + j,
-                scale,
-                -scale * sg_a * own[2:3],
-                scale * (here - sb_a - sg_a * own[3:4]),
-            )
+            settle(h[1].rsem)
+            grad_of = norm_grad(0, first, sums_of())
+            groups = [rows_out(ag_d, j, rows, grad_of(rows, h)) for rows in spans]
+            hooks[3]()
             grad_to_dp(1, j)
-            hooks[3]()
-            settle(group)
-            settle(sent)
-
-            def d_first(rows, carry):
-                for c in range(n_mp):
-                    tile = co[4 + j, c]
-                    out = live[rows] * (
-                        ag_d[j, c, rows].astype(F32) * tile[0:1]
-                        + ag_a[j, c, rows].astype(F32) * tile[1:2]
-                        + tile[2:3]
-                    )
-                    dfull[j, rows, c * C:(c + 1) * C] = out.astype(BF16)
-                return carry
-
-            loop(R, 64, d_first)
-
-            def d_input():
-                def body(rows, carry):
-                    out = dot(dfull[j, rows], cat(wr.at[j], n_dp), NT) + dpre[rows]
-                    if j == 1:
-                        out = out.astype(BF16).astype(F32)
-                        evec[rows] = out
-                    ig[j, rows] = out
+
+            def d_input(rows):
+                full = jnp.concatenate([ag_d[j, c, rows] for c in range(n_mp)], axis=1)
+                out = dot(full, cat(wr.at[j], n_dp), NT) + dpre[rows]
+                if j == 1:
+                    out = out.astype(BF16).astype(F32)
+                    evec[rows] = out
+                ig[j, rows] = out
+
+            for rows, group in zip(spans, groups):
+                settle(group)
+                if j == 1:
+                    d_input(rows)
+            if j == 0:
+                reduce_to_sib(j)
+                for rows in spans:
+                    d_input(rows)
+            to_section(lambda: ig.at[j], ig_hbm, j)
+
+        settle(l_x)
+        hold = {}
+
+        def first_product():
+            handle = rs_open()
+            p, group = handle
+            for k in range(n_dp):
+                src = early.came_from(k) if k else d
+                if k:
+                    settle(early.rsem + k - 1)
+                sem = recv.take()
+
+                @pl.when(s == 0)
+                def _():
+                    rcopy(lambda: wr.at[0, src], lambda: wr.at[0, src], sem, sib_dev, when=0)
+
+                expected[sem] = on(lambda: s != 0, lambda: arrive(wr.at[0, src], sem))
+                settle(sem)
+
+                def part(rows, carry):
+                    rs_s[p, src, rows] = dot(xin[0, rows], wr[0, src], NN).astype(BF16)
                     return carry
 
-                loop(R, 128, body)
-                to_section(lambda: ig.at[j], ig_hbm, j)
-
-            def g_reduce():
-                for i in range(n_dp):
-                    full = dfull[j, :, i * Cd:(i + 1) * Cd]
-                    gred[j, i] = dot(xin[j], full, TN).astype(BF16)
-                grad_to_sib(0, j)
-
-            return d_input, g_reduce
-
-        pass_on(wr, 0)
-        settle(l_x)
-        from_sib(wr, 0)
+                loop(R, 128, part)
+
+                @pl.when(src != m)
+                def _():
+                    put_to(rs_s.at[p, src], rs_r.at[p, m], group.ssem, group.rsem, mp_dev(src))
+
+            group.close()
+            return handle
+
+        @pl.when(s == 1)
+        def _():
+            pl.semaphore_wait(go, 1)
+
+        start = first_product()
         settle(par_sem)
+
+        def w_next():
+            send_own(we, 0)
+            send_own(wr, 1)
+
+        def w_head():
+            hold["heads"] = to_all(lambda t: hd.at[mine], hd)
 
         def f00():
             send_own(wsp, 0)
-
-        def f01():
+            pending[None].pop()()
+
+            @pl.when(s == 0)
+            def _():
+                pl.semaphore_signal(go, inc=1, device_id=sib_dev, device_id_type=MESH)
+
+        hooks = (f00, w_next, lambda: send_own(wsp, 1), nothing)
+
+        def n00():
             pass_on(wsp, 0)
-            send_own(we, 0)
-            send_own(wr, 1)
             from_sib(wsp, 0)
 
-        def f02():
+        def n01():
             pass_on(we, 0)
-            pass_on(wr, 1)
-            send_own(wsp, 1)
             from_sib(we, 0)
 
-        def f03():
-            from_sib(wr, 1)
-
-        hold = {}
-        forward(0, (f00, f01, f02, f03))
+        forward(0, start, hooks, (n00, n01))
+        from_sib(wr, 1)
+        start = product_to_rs(xin.at[1], lambda: cat(wr.at[1], n_dp), NN)
 
         def f10():
+            send_own(we, 1)
             pass_on(wsp, 1)
-            send_own(we, 1)
-            hold["heads"] = to_all(lambda t: hd.at[mine], hd)
             to_section(lambda: xin.at[1], act_hbm, 0)
-
-        def f11():
+            prepare(0)
+
+        def n10():
             pass_on(we, 1)
             from_sib(wsp, 1)
 
-        def f12():
-            from_sib(we, 1)
-
-        forward(1, (f10, f11, f12, nothing))
+        hooks = (f10, w_head, nothing, nothing)
+        forward(1, start, hooks, (n10, lambda: from_sib(we, 1)))
 
         settle(hold["heads"])
         RM = R // n_mp
@@ -1066,6 +1193,7 @@
         )
         to_section(lambda: act1, act_hbm, 1)
         settle(l_thr)
+        prepare(1)
         settle(base)
         here = pl.ds(pl.multiple_of(m * RM, RM), RM)
         lv = wide(live[here], classes)
@@ -1079,11 +1207,13 @@
             ids = lax.broadcasted_iota(jnp.int32, (RM, classes), 1).astype(F32)
             hot = (ids == labc[here, t:t + 1]).astype(F32)
             dl[m, :, lanes] = (LOSS_WEIGHT * lv * (soft - hot)).astype(BF16)
-        settle(spread(
-            "mp", lambda t: dl.at[m], lambda src: dl.at[src], lambda: dl.at[pl.ds(0, n_mp - 1)]
-        ))
-
-        def merge_block(c):
+        group = Group(
+            "mp", lambda: dl.at[pl.ds(0, n_mp - 1)], slot_of=lambda src: dl.at[src]
+        )
+        group.put(lambda t: dl.at[m], lambda src: dl.at[src])
+        group.close()
+
+        def merge_block(c, sums):
             for t in range(tasks):
                 lanes = slice(t * classes, (t + 1) * classes)
                 tg[t] = dot(dl[c, :, lanes], heads_of(t), NN)
@@ -1100,13 +1230,15 @@
                 there = pl.ds(start, 32)
                 frac = 1.0 / (1.0 + jnp.exp((thr[there] - purity) * (1.0 / KEEP_TEMPER)))
                 upper, lower = 0.5 * (total + soft_sum), 0.5 * (total - soft_sum)
-                evec[there] = frac * upper + (1.0 - frac) * lower
-                return carry
-
-            loop(RM, 32, merge)
-
-        for c in range(n_mp):
-            merge_block(c)
+                return steepest(1, there, frac * upper + (1.0 - frac) * lower, carry)
+
+            return loop(RM, 32, merge, sums)
+
+        zero = (jnp.zeros((8, Wd), F32), jnp.zeros((8, Wd), F32))
+        sums = merge_block(m, zero)
+        for k in [1] + list(range(n_mp - 1, 1, -1)):
+            settle(group.rsem + k - 1)
+            sums = merge_block(group.came_from(k), sums)
 
         def b10():
             for t in range(tasks):
@@ -1116,21 +1248,16 @@
                 ghead[:, t] = out.reshape(n_cls, piece, Wd)
             hold["ghead"] = to_all(lambda t: ghead.at[t], rhead)
 
-        late1 = backward(1, (b10, nothing, nothing, nothing))
-        late1[0]()
-
-        def b00():
-            late1[1]()
-
-        def b01():
-            grad_to_dp(0, 1)
-
-        late0 = backward(0, (b00, b01, nothing, nothing))
-        late0[1]()
-        late0[0]()
-        vec_sem = recv.take()
-        rcopy(lambda: vec.at[o], lambda: vsib, vec_sem, sib_dev)
-        expected[vec_sem] = lambda: arrive(vsib, vec_sem)
+        backward(1, sums, (nothing, b10, nothing, nothing))
+        sums = loop(R, 32, lambda rows, carry: steepest(0, rows, evec[rows], carry), zero)
+
+        def b03():
+            hold["vec"] = recv.take()
+            rcopy(lambda: vec.at[o], lambda: vsib, hold["vec"], sib_dev)
+            expected[hold["vec"]] = lambda: arrive(vsib, hold["vec"])
+
+        backward(0, sums, (lambda: reduce_to_sib(1), lambda: reduce_to_dp(1), nothing, b03))
+        reduce_to_dp(0)
 
         settle(hold["ghead"])
         for t in range(tasks):
@@ -1139,10 +1266,9 @@
                 total = total + rhead[rem(mine + k, n_cls), t].astype(F32)
             ohead[t] = total
         load(ohead, head_out)
-        settle(vec_sem)
+        settle(hold["vec"])
         ovec[...] = vec[s] + vsib[...]
         load(ovec, vec_hbm)
-        grad_to_dp(0, 0)
 
         def total_of(own, got, rows):
             out = own[s, d, rows].astype(F32)
@@ -1192,9 +1318,10 @@
     RM = R // n_mp
     vmem = lambda shape, dtype: pltpu.VMEM(shape, dtype)
     scratch = [
-        pltpu.SemaphoreType.DMA((64,)),
-        pltpu.SemaphoreType.DMA((64,)),
+        pltpu.SemaphoreType.DMA((83,)),
+        pltpu.SemaphoreType.DMA((87,)),
         pltpu.SemaphoreType.DMA((15,)),
+        pltpu.SemaphoreType.REGULAR,
         vmem((Wd, Cd), F32),
         vmem((9, Cd, C), F32),
         vmem((Cd, Wd), F32),
@@ -1217,8 +1344,9 @@
         vmem((2, n_mp, R, C), BF16),
         vmem((2, R, M), BF16),
         vmem((2, R, M), BF16),
-        vmem((2, R, M), BF16),
+        vmem((4, n_mp, 8, C), F32),
         vmem((6, n_mp, 8, C), F32),
+        vmem((6, n_mp * n_dp, 8, C), F32),
         vmem((12, n_dp, 8, Wd), F32),
         vmem((2, 3, 8, Wd), F32),
         vmem((2, R, C), F32),
@@ -1235,7 +1363,8 @@
         vmem((R, Wd), F32),
         vmem((R, Wd), F32),
         vmem((R, Wd), BF16),
-        vmem((R, C), F32),
+        vmem((2, R, Wd), F32),
+        vmem((2, 2, n_mp, R, C), F32),
         vmem((2, R, Wd), F32),
         vmem((2, n_dp, Wd, Cd), BF16),
         vmem((2, n_dp, Cd, W9), BF16),
@@ -1343,7 +1472,7 @@
     tasks, _, piece = args[9].shape
     sizes = (n_dp, n_mp, R, Wd, C * n_mp, C, Cd, piece * 2 * n_dp, tasks, piece)
     whole_tiles = not (C % 128 or Cd % 128 or Wd % 128 or R % 128 or piece % 16 or (R // n_mp) % 32)
-    if whole_tiles and block_input.shape[0] == lax.axis_size("section") == 2:
+    if whole_tiles and C == Cd and block_input.shape[0] == lax.axis_size("section") == 2:
         return fused_device(sizes, *args)
     return plain_device(*args)
 

time: 187 us -> 179 us (0.957)
  Pallas kernels: 186 us -> 177 us
    pallas_call x1, Pallas kernels: 182 us -> 173 us  [fused_device(): pl.pallas_call(make_kernel(sizes), out_shape=(whole((1, 2, R, Wd), BF16),...]
where the time goes in v3:
time: 179 us; the launch traced here: 178 us
  Pallas kernels  177 us (99%)
    pallas_call x1, Pallas kernels, fused_device(): pl.pallas_call(make_kernel(sizes), out_shape=(whole((1, 2, R, Wd), BF16),...  173 us
    pallas_call x1, Pallas kernels, fused_device(): pl.pallas_call(hand_out, out_shape=shapes, in_specs=[in_any] * 5 + [in_vm...  4.47 us

profile of v3, /device:TPU:0, one launch (start us, length us, event | category | flops | bytes accessed | tf_op | source)
XLA Modules:
  0.0 178.3 jit_solution(3468816705416117814)
XLA Ops:
  0.6 173.0 %shard_map.195 = (bf16[1,2,384,512]{3,2,1,0:T(8,128)(2,1)}, f32[1,2,384,512]{3,2,1,0:T(8,128)}, f32[1,512,128]{2,1,0:T(8,128)}, f32[1,9,128,128]{3,2,1,0:T(8,128...) custom-call(bf16[2,384,512]{2,1,0:T(8,128)(2,1)} %refs_0_.1, s32[2,1,96]{2,1,0:T(1,128)} %refs_1_.1, ...), custom_call_target="tpu_custom_call" | custom-call | tf_op jit(solution)/shard_map/pallas_call | solution.py:1391
  173.7 4.5 %shard_map.196 = (bf16[1,2,384,512]{3,2,1,0:T(8,128)(2,1)}, f32[1,2,384,512]{3,2,1,0:T(8,128)}, f32[1,512,128]{2,1,0:T(8,128)}, f32[1,9,128,128]{3,2,1,0:T(8,128...) custom-call(bf16[1,2,384,512]{3,2,1,0:T(8,128)(2,1)} %get-tuple-elem, ...), custom_call_target="tpu_custom_call" | custom-call | tf_op jit(solution)/shard_map/pallas_call | solution.py:1425

commit v4 on v3

--- a/solution.py
+++ b/solution.py
@@ -402,23 +402,25 @@
 
     def kernel(*refs):
         (
-            x_hbm, sides_ref, wred_hbm, wspa_hbm, wexp_hbm, gin_ref, sin_ref, gout_ref, sout_ref,
-            head_hbm, lab_ref, thr_hbm,
+            x_hbm, sides_hbm, wred_hbm, wspa_hbm, wexp_hbm, gin_hbm, sin_hbm, gout_hbm, sout_hbm,
+            head_hbm, lab_hbm, thr_hbm,
             act_hbm, ig_hbm, red_hbm, spa_hbm, exp_hbm, vec_hbm, head_out,
             ssems, rsems, lsems, go,
             sred, sspa, sexp, shead, thr, xin, wr, wsp, we, hd, par,
             live, geo, masks, labc,
-            rs_s, rs_r, ag_a, ag_b, ag_d, fulla, fullb, co, sums_s, sums_r, st, keep, first, second, third, ppad, dpad, dbuf,
+            rs_s, rs_r, ag_a, ag_b, ag_d, fulla, fullb, dfull, co, sums_s, sums_r, sums_t, st, keep, first, second, third, ppad, dpad, dbuf,
             lg_s, lg_r, dl, act1, tg, dpre, evec, dth, ig, slope, steep,
             gred, gspa, gexp, sibred, sibspa, sibexp, rred, rspa, rexp, ghead, rhead, vec, vsib,
             ored, ospa, oexp, ovec, ohead,
+            sides_ref, gin_ref, sin_ref, gout_ref, sout_ref, lab_ref,
         ) = refs
         s = lax.axis_index("section")
         d = lax.axis_index("dp")
         m = lax.axis_index("mp")
         o = 1 - s
-        send, recv, local = Sems(ssems), Sems(rsems), Sems(lsems)
+        recv, local = Sems(rsems), Sems(lsems)
         pending = {None: [], 0: [], 1: []}
+        sends = {None: 0, 0: 1, 1: 2}
         rem = lax.rem
         dp_dev = lambda t: (s, t, m)
         mp_dev = lambda t: (s, d, t)
@@ -445,7 +447,7 @@
             )
 
         def rcopy(src, dst, rsem, dev, when=None):
-            ssem = send.take()
+            ssem = sends[when]
             put_to(src(), dst(), ssem, rsem, dev)
             pending[when].append(lambda: waiter(src(), ssem, 0).wait_send())
 
@@ -453,7 +455,7 @@
             waiter(dst, 0, rsem).wait_recv()
 
         axes = {"dp": (n_dp, d, dp_dev), "mp": (n_mp, m, mp_dev)}
-        expected = {}
+        expected, hold = {}, {}
 
         def settle(key):
             expected.pop(key)()
@@ -471,7 +473,7 @@
         class Group:
             def __init__(self, axis, all_of, when=None, slot_of=None):
                 self.n, self.me, self.dev = axes[axis]
-                self.ssem = send.take()
+                self.ssem = sends[when]
                 self.rsem = recv.take(1 if slot_of is None else self.n - 1)
                 self.all_of, self.when, self.slot_of = all_of, when, slot_of
 
@@ -504,13 +506,6 @@
             group = Group(axis, all_of, when)
             group.put(src_of, slot_of)
             return group.close()
-
-        l_red = load(wred_hbm.at[0], sred)
-        l_x = load(x_hbm.at[s], xin.at[0])
-        l_spa = load(wspa_hbm.at[0], sspa)
-        l_exp = load(wexp_hbm.at[0], sexp)
-        l_head = load(head_hbm, shead)
-        l_thr = load(thr_hbm.at[s], thr)
 
         barrier = pltpu.get_barrier_semaphore()
         greeted = 0
@@ -530,8 +525,25 @@
             )
             greeted += 1
 
+
+        l_red = load(wred_hbm.at[0], sred)
+        l_par = [
+            load(src, dst)
+            for src, dst in (
+                (gin_hbm, gin_ref), (sin_hbm, sin_ref), (gout_hbm, gout_ref), (sout_hbm, sout_ref)
+            )
+        ]
+        l_x = load(x_hbm.at[s], xin.at[0])
+        l_spa = load(wspa_hbm.at[0], sspa)
+        l_exp = load(wexp_hbm.at[0], sexp)
+        l_small = [load(sides_hbm, sides_ref), load(lab_hbm, lab_ref)]
+        l_head = load(head_hbm, shead)
+        l_thr = load(thr_hbm.at[s], thr)
+
         settle(l_red)
         wr[s, d] = sred[...].astype(BF16)
+        for key in l_par:
+            settle(key)
         par[s] = jnp.zeros(par.shape[1:], F32)
         for i in range(2):
             par[s, i:i + 1, :C] = gin_ref[0, i:i + 1, :]
@@ -590,6 +602,8 @@
         settle(l_exp)
         we[s, d] = sexp[...].astype(BF16)
 
+        for key in l_small:
+            settle(key)
         sides = jnp.where(s == 0, sides_ref[0], sides_ref[1]).astype(F32)
         slots = sides.shape[1]
         sq = jnp.broadcast_to(sides * sides, (8, slots)).astype(BF16)
@@ -637,7 +651,7 @@
             hd[mine, t] = shead[t].astype(BF16)
 
         def to_all(src_of, buf):
-            ssem, rsem = send.take(), recv.take()
+            ssem, rsem = sends[None], recv.take()
             others = [(a, k) for a in range(n_sec) for k in range(n_dp) if a or k]
             for a, k in others:
                 ts, td = rem(s + a, n_sec), rem(d + k, n_dp)
@@ -672,17 +686,6 @@
                 return carry
 
             loop(R, 128, add)
-
-        def product_to_rs(left, right_of, dims):
-            handle = rs_open()
-
-            def part(rows, carry):
-                rs_rows(handle, rows, dot(left[rows], right_of(), dims))
-                return carry
-
-            loop(R, 128, part)
-            handle[1].close()
-            return handle
 
         def exchange(tile):
             p = phase["st"]
@@ -742,7 +745,7 @@
             )
 
         def rs_rows_sums(handle, j, i, rows, out, carry):
-            p, group = handle
+            p, groups = handle
             sb, sg = carry
             raw = (ag_a, ag_b)[i]
             for c in range(n_mp):
@@ -753,37 +756,43 @@
                 xhat = raw[j, c, rows].astype(F32) * tile[2:3] + tile[3:4]
                 sb[c] = sb[c] + fold(g)
                 sg[c] = sg[c] + fold(g * xhat)
-            if rows is not spans[-1]:
-                group.put(lambda t: rs_s.at[p, t, rows], lambda src: rs_r.at[p, src, rows])
-
-        def rs_sums_out(handle, carry):
-            p, group = handle
-            sb, sg = carry
-            total = lambda v: jnp.sum(v, axis=0, keepdims=True)
-            for c in range(n_mp):
-                b, g = total(sb[c]), total(sg[c])
-                sums_s[p, c] = rows_tile(b, g, g)
-            ssem, rsem = send.take(), recv.take()
+            if rows is spans[-1]:
+                sums = sums_out(p, sb + sg)
+            group = Group("mp", lambda: rs_r.at[p, pl.ds(0, n_mp - 1), rows])
+            group.put(lambda t: rs_s.at[p, t, rows], lambda src: rs_r.at[p, src, rows])
+            groups.append(group.close())
+            return sums if rows is spans[-1] else None
+
+        def sums_out(p, parts):
+            place = lax.broadcasted_iota(jnp.int32, (2 * n_mp, C), 0)
+            tile = jnp.zeros((2 * n_mp, C), F32)
+            for i, part in enumerate(parts):
+                tile = jnp.where(place == i, jnp.sum(part, axis=0, keepdims=True), tile)
+            sums_s[p] = tile
+            ssem, rsem = sends[None], recv.take()
             others = [(a, k) for a in range(n_mp) for k in range(n_dp) if a or k]
             me = m * n_dp + d
             for a, k in others:
                 tz, td = rem(m + a, n_mp), rem(d + k, n_dp)
-                put_to(sums_s.at[p, tz], sums_r.at[p, me], ssem, rsem, (s, td, tz))
-            rows = spans[-1]
-            group.put(lambda t: rs_s.at[p, t, rows], lambda src: rs_r.at[p, src, rows])
-            group.close()
+                put_to(sums_s.at[p], sums_r.at[p, me], ssem, rsem, (s, td, tz))
             rest = lambda: sums_r.at[p, pl.ds(0, len(others))]
             pending[None].append(lambda: waiter(rest(), ssem, 0).wait_send())
             expected[rsem] = lambda: arrive(rest(), rsem)
 
             def collect_sums():
                 settle(rsem)
-                tile = sums_s[p, m]
+                total = sums_s[p]
                 for a, k in others:
-                    tile = tile + sums_r[p, rem(m + a, n_mp) * n_dp + rem(d + k, n_dp)]
-                return tile
+                    total = total + sums_r[p, rem(m + a, n_mp) * n_dp + rem(d + k, n_dp)]
+                sums_t[p] = total
+                return total
 
             return collect_sums
+
+        def rs_parts():
+            p = phase["rs"]
+            phase["rs"] += 1
+            return p, []
 
         def rs_sum(handle, rows):
             p, _ = handle
@@ -897,14 +906,15 @@
             mu, inv, _, gain, shift = norm_of(j, 2, Wd)
             out = xin.at[1] if j == 0 else act1
 
-            def act_c(rows, carry):
-                lv = wide(live[rows], Wd)
-                pre = lv * (gain * ((third[j, rows] - mu) * inv) + shift)
-                pre = pre + xin[j, rows].astype(F32)
-                out[rows] = (lv * gelu(pre)).astype(BF16)
-                return carry
-
-            loop(R, 32, act_c)
+            def act_c(rows):
+                for r0 in range(rows.start, rows.stop, 32):
+                    there = slice(r0, r0 + 32)
+                    lv = wide(live[there], Wd)
+                    pre = lv * (gain * ((third[j, there] - mu) * inv) + shift)
+                    pre = pre + xin[j, there].astype(F32)
+                    out[there] = (lv * gelu(pre)).astype(BF16)
+
+            return act_c
 
         def to_section(src, hbm, j):
             sem = recv.take()
@@ -961,7 +971,8 @@
 
         def reduce_to_sib(j):
             for i in range(n_dp):
-                gred[j, i] = dot(xin[j], ag_d[j, i], TN).astype(BF16)
+                full = dfull[j, :, i * Cd:(i + 1) * Cd]
+                gred[j, i] = dot(xin[j], full, TN).astype(BF16)
                 sem = at_sib[0, j, i] = recv.take()
 
                 @pl.when(s != j)
@@ -1019,39 +1030,44 @@
                 return carry
 
             none = lambda: ([jnp.zeros((8, C), F32)] * n_mp, [jnp.zeros((8, C), F32)] * n_mp)
-            h, carry = rs_open(), none()
+            h, carry = rs_parts(), none()
             for rows in spans:
                 for r0 in range(rows.start, rows.stop, 32):
                     d_third(slice(r0, r0 + 32), 0)
                 out = dot(dth[rows], we[j].reshape(M, Wd), NT)
-                rs_rows_sums(h, j, 1, rows, out, carry)
-            sums_of = rs_sums_out(h, carry)
+                sums_of = rs_rows_sums(h, j, 1, rows, out, carry)
             for i in range(n_dp):
                 full = fullb[j, :, i * Cd:(i + 1) * Cd]
                 gexp[j, i] = dot(full, dth[...], TN).astype(BF16)
             grad_to_sib(2, j)
             hooks[1]()
-            settle(h[1].rsem)
-
-            def norm_grad(i, src, tile):
-                mu, inv, count, gain, _ = norm_of(j, i, C)
-                vec[j, i:i + 1, 0:C] = tile[1:2]
-                vec[j, 2 + i:3 + i, 0:C] = tile[0:1]
-                sb_n, sg_n, scale = tile[0:1] / count, tile[1:2] / count, gain * inv
-
-                def grad_of(rows, h):
-                    xhat = (src[j, rows] - mu) * inv
-                    g = slope[j, i, m, rows] * rs_sum(h, rows)
-                    return live[rows] * scale * (g - sb_n - xhat * sg_n)
-
-                return grad_of
-
-            grad_of = norm_grad(1, second, sums_of())
+            for group in h[1]:
+                settle(group)
+
+            def norm_sums(i, sums):
+                p = sums[0]
+                place = lax.broadcasted_iota(jnp.int32, (2 * n_mp, C), 0)
+                row = lambda i: jnp.sum(
+                    jnp.where(place == i, sums_t[p], 0.0), axis=0, keepdims=True
+                )
+                sb, sg = row(m), row(n_mp + m)
+                vec[j, i:i + 1, 0:C] = sg
+                vec[j, 2 + i:3 + i, 0:C] = sb
+                return sb, sg
+
+            sums_of()
+            sb_b, sg_b = norm_sums(1, h)
+            mu_b, inv_b, count_b, gain_b, _ = norm_of(j, 1, C)
+            scale_b, sb_b, sg_b = gain_b * inv_b, sb_b / count_b, sg_b / count_b
             for rows in spans:
                 there = slice(PAD + rows.start, PAD + rows.stop)
-                dpad[there] = grad_of(rows, h).astype(BF16).astype(F32)
-
-            h, carry = rs_open(), none()
+                xhat = (second[j, rows] - mu_b) * inv_b
+                g = slope[j, 1, m, rows] * rs_sum(h, rows)
+                out = live[rows] * scale_b * (g - sb_b - xhat * sg_b)
+                dpad[there] = out.astype(BF16).astype(F32)
+
+            h, carry = rs_parts(), none()
+            sums_a = []
 
             def put(r0, summed):
                 for k in range(9):
@@ -1060,42 +1076,71 @@
                     ).astype(BF16)
                 rows = spans[r0 // 128]
                 out = dot(dbuf[rows], wsp[j].reshape(M, W9), NT)
-                rs_rows_sums(h, j, 0, rows, out, carry)
+                sums_a.append(rs_rows_sums(h, j, 0, rows, out, carry))
 
             taps_sum(dpad, True, put)
-            sums_of = rs_sums_out(h, carry)
             for i in range(n_dp):
                 full = fulla[j, :, i * Cd:(i + 1) * Cd]
                 gspa[j, i] = dot(full, dbuf[...], TN).astype(BF16)
             grad_to_sib(1, j)
             grad_to_dp(2, j)
             hooks[2]()
-            settle(h[1].rsem)
-            grad_of = norm_grad(0, first, sums_of())
-            groups = [rows_out(ag_d, j, rows, grad_of(rows, h)) for rows in spans]
+            groups = []
+            for rows, part in zip(spans, h[1]):
+                settle(part)
+                g = slope[j, 0, m, rows] * rs_sum(h, rows)
+                if not groups:
+                    pivot = jnp.sum(g, axis=0, keepdims=True) / jnp.maximum(
+                        jnp.sum(live[rows], axis=0, keepdims=True), 1.0
+                    )
+                    sent = coeffs_out(4 + j, pivot)
+                groups.append(rows_out(ag_d, j, rows, g - pivot))
             hooks[3]()
             grad_to_dp(1, j)
 
             def d_input(rows):
-                full = jnp.concatenate([ag_d[j, c, rows] for c in range(n_mp)], axis=1)
-                out = dot(full, cat(wr.at[j], n_dp), NT) + dpre[rows]
+                out = dot(dfull[j, rows], cat(wr.at[j], n_dp), NT) + dpre[rows]
                 if j == 1:
                     out = out.astype(BF16).astype(F32)
                     evec[rows] = out
                 ig[j, rows] = out
 
+            sums = sums_a[-1]()
+            norm_sums(0, h)
+            if j == 0:
+                hold["vec"] = recv.take()
+                rcopy(lambda: vec.at[o], lambda: vsib, hold["vec"], sib_dev)
+                expected[hold["vec"]] = lambda: arrive(vsib, hold["vec"])
+            settle(sent)
+            count = keep[j, 0, 2:3, 0:C]
+            terms = []
+            for c in range(n_mp):
+                tile = co[2 * j, c]
+                sb_n, sg_n = sums[c:c + 1] / count, sums[n_mp + c:n_mp + c + 1] / count
+                scale, inv, moved = tile[0:1], tile[2:3], tile[3:4]
+                offset = scale * (co[4 + j, c, 0:1] - sb_n - moved * sg_n)
+                terms.append((scale, -scale * sg_n * inv, offset))
             for rows, group in zip(spans, groups):
                 settle(group)
+                for c, (scale, slant, offset) in enumerate(terms):
+                    out = live[rows] * (
+                        ag_d[j, c, rows].astype(F32) * scale
+                        + ag_a[j, c, rows].astype(F32) * slant
+                        + offset
+                    )
+                    dfull[j, rows, c * C:(c + 1) * C] = out.astype(BF16)
                 if j == 1:
                     d_input(rows)
             if j == 0:
                 reduce_to_sib(j)
-                for rows in spans:
+                d_input(spans[0])
+                d_input(spans[1])
+                reduce_to_dp(j)
+                for rows in spans[2:]:
                     d_input(rows)
             to_section(lambda: ig.at[j], ig_hbm, j)
 
         settle(l_x)
-        hold = {}
 
         def first_product():
             handle = rs_open()
@@ -1142,7 +1187,6 @@
 
         def f00():
             send_own(wsp, 0)
-            pending[None].pop()()
 
             @pl.when(s == 0)
             def _():
@@ -1158,9 +1202,13 @@
             pass_on(we, 0)
             from_sib(we, 0)
 
-        forward(0, start, hooks, (n00, n01))
+        act_c = forward(0, start, hooks, (n00, n01))
         from_sib(wr, 1)
-        start = product_to_rs(xin.at[1], lambda: cat(wr.at[1], n_dp), NN)
+        start = rs_open()
+        for rows in spans:
+            act_c(rows)
+            rs_rows(start, rows, dot(xin[1, rows], cat(wr.at[1], n_dp), NN))
+        start[1].close()
 
         def f10():
             send_own(we, 1)
@@ -1173,7 +1221,7 @@
             from_sib(wsp, 1)
 
         hooks = (f10, w_head, nothing, nothing)
-        forward(1, start, hooks, (n10, lambda: from_sib(we, 1)))
+        act_c = forward(1, start, hooks, (n10, lambda: from_sib(we, 1)))
 
         settle(hold["heads"])
         RM = R // n_mp
@@ -1183,6 +1231,7 @@
             return hd[:, t].reshape(classes, Wd)
 
         for c in range(n_mp):
+            act_c(slice(c * RM, (c + 1) * RM))
             rows = act1[c * RM:(c + 1) * RM]
             for t in range(tasks):
                 lg_s[c, :, t * classes:(t + 1) * classes] = dot(rows, heads_of(t), NT).astype(
@@ -1251,13 +1300,7 @@
         backward(1, sums, (nothing, b10, nothing, nothing))
         sums = loop(R, 32, lambda rows, carry: steepest(0, rows, evec[rows], carry), zero)
 
-        def b03():
-            hold["vec"] = recv.take()
-            rcopy(lambda: vec.at[o], lambda: vsib, hold["vec"], sib_dev)
-            expected[hold["vec"]] = lambda: arrive(vsib, hold["vec"])
-
-        backward(0, sums, (lambda: reduce_to_sib(1), lambda: reduce_to_dp(1), nothing, b03))
-        reduce_to_dp(0)
+        backward(0, sums, (lambda: reduce_to_sib(1), lambda: reduce_to_dp(1), nothing, nothing))
 
         settle(hold["ghead"])
         for t in range(tasks):
@@ -1318,9 +1361,9 @@
     RM = R // n_mp
     vmem = lambda shape, dtype: pltpu.VMEM(shape, dtype)
     scratch = [
-        pltpu.SemaphoreType.DMA((83,)),
-        pltpu.SemaphoreType.DMA((87,)),
-        pltpu.SemaphoreType.DMA((15,)),
+        pltpu.SemaphoreType.DMA((3,)),
+        pltpu.SemaphoreType.DMA((97,)),
+        pltpu.SemaphoreType.DMA((21,)),
         pltpu.SemaphoreType.REGULAR,
         vmem((Wd, Cd), F32),
         vmem((9, Cd, C), F32),
@@ -1344,9 +1387,11 @@
         vmem((2, n_mp, R, C), BF16),
         vmem((2, R, M), BF16),
         vmem((2, R, M), BF16),
-        vmem((4, n_mp, 8, C), F32),
+        vmem((2, R, M), BF16),
         vmem((6, n_mp, 8, C), F32),
-        vmem((6, n_mp * n_dp, 8, C), F32),
+        vmem((6, 2 * n_mp, C), F32),
+        vmem((6, n_mp * n_dp, 2 * n_mp, C), F32),
+        vmem((6, 2 * n_mp, C), F32),
         vmem((12, n_dp, 8, Wd), F32),
         vmem((2, 3, 8, Wd), F32),
         vmem((2, R, C), F32),
@@ -1384,8 +1429,7 @@
         vmem((1, Cd, Wd), F32),
         vmem((8, Wd), F32),
         vmem((tasks, piece, Wd), F32),
-    ]
-    in_vmem = pl.BlockSpec(memory_space=pltpu.VMEM)
+    ] + [vmem(args[i].shape, args[i].dtype) for i in (1, 5, 6, 7, 8, 10)]
     in_any = pl.BlockSpec(memory_space=pl.ANY)
     whole = lambda shape, dtype=F32: jax.ShapeDtypeStruct(shape, dtype)
     out = pl.pallas_call(
@@ -1399,10 +1443,7 @@
             whole((8, Wd)),
             whole((tasks, piece, Wd)),
         ),
-        in_specs=[
-            in_any, in_vmem, in_any, in_any, in_any, in_vmem, in_vmem, in_vmem, in_vmem,
-            in_any, in_vmem, in_any,
-        ],
+        in_specs=[in_any] * len(args),
         out_specs=(in_any,) * 7,
         scratch_shapes=scratch,
         compiler_params=pltpu.CompilerParams(
@@ -1425,20 +1466,22 @@
     done = pl.pallas_call(
         hand_out,
         out_shape=shapes,
-        in_specs=[in_any] * 5 + [in_vmem, in_any],
-        out_specs=(in_any,) * 5 + (in_vmem,) * 4 + (in_any,),
-        scratch_shapes=[pltpu.VMEM(a.shape, a.dtype) for a in shapes[:5] + shapes[9:]]
-        + [pltpu.SemaphoreType.DMA((16,)), pltpu.SemaphoreType.DMA((16,))],
+        in_specs=[in_any] * 7,
+        out_specs=(in_any,) * 10,
+        scratch_shapes=[pltpu.VMEM(a.shape, a.dtype) for a in shapes]
+        + [vmem((8, Wd), F32), pltpu.SemaphoreType.DMA((9,)), pltpu.SemaphoreType.DMA((12,))],
     )(*out)
     return done[:9] + (jnp.transpose(done[9], (0, 2, 1)),)
 
 
 def hand_out(*refs):
-    given, outs, held, came, left = refs[:7], refs[7:17], refs[17:23], refs[23], refs[24]
-    vec, gains, shifts, gain_out, shift_out = given[5], *outs[5:9]
+    given, outs, held, vec, came, left = refs[:7], refs[7:17], refs[17:27], *refs[27:]
+    gains, shifts, gain_out, shift_out = held[5:9]
+    load_vec = pltpu.make_async_copy(given[5], vec, came.at[8])
+    load_vec.start()
     pieces = []
-    for src, mid, dst in zip(given[:5] + given[6:], held, outs[:5] + outs[9:]):
-        for i in range(src.shape[1]) if len(src.shape) == 4 else (None,):
+    for src, mid, dst in zip(given[:5] + given[6:], held[:5] + held[9:], outs[:5] + outs[9:]):
+        for i in range(src.shape[1]) if src.shape[1] == 2 else (None,):
             at = (lambda ref, i=i: ref) if i is None else (lambda ref, i=i: ref.at[0, i])
             n = len(pieces)
             pieces.append((
@@ -1450,6 +1493,7 @@
     d = lax.axis_index("dp")
     part, outer = gains.shape[3], gain_out.shape[2]
     lanes = part * lax.axis_size("dp")
+    load_vec.wait()
     rolled = pltpu.roll(vec[:, 0:lanes], lax.rem(lanes - d * part, lanes), 1)
     for i in range(2):
         gains[0, i] = rolled[i:i + 1, 0:part]
@@ -1457,10 +1501,15 @@
     mine = pl.ds(pl.multiple_of(d * outer, outer), outer)
     gain_out[0] = vec[4:5, mine]
     shift_out[0] = vec[5:6, mine]
+    stores = [
+        pltpu.make_async_copy(held[i], outs[i], left.at[len(pieces) + i - 5]) for i in range(5, 9)
+    ]
+    for store in stores:
+        store.start()
     for fetch, store in pieces:
         fetch.wait()
         store.start()
-    for _, store in pieces:
+    for store in stores + [store for _, store in pieces]:
         store.wait()
 
 

time: 179 us -> 174 us (0.972)
  Pallas kernels: 177 us -> 173 us
    pallas_call x1, Pallas kernels: 173 us -> 170 us  [fused_device(): pl.pallas_call(make_kernel(sizes), out_shape=(whole((1, 2, R, Wd), BF16),...]
where the time goes in v4:
time: 174 us
  Pallas kernels  173 us (99%)
    pallas_call x1, Pallas kernels, fused_device(): pl.pallas_call(make_kernel(sizes), out_shape=(whole((1, 2, R, Wd), BF16),...  170 us

profile of v4, /device:TPU:0, one launch (start us, length us, event | category | flops | bytes accessed | tf_op | source)
XLA Modules:
  0.0 174.2 jit_solution(17306144951209777398)
XLA Ops:
  0.6 170.2 %shard_map.195 = (bf16[1,2,384,512]{3,2,1,0:T(8,128)(2,1)}, f32[1,2,384,512]{3,2,1,0:T(8,128)}, f32[1,512,128]{2,1,0:T(8,128)}, f32[1,9,128,128]{3,2,1,0:T(8,128...) custom-call(bf16[2,384,512]{2,1,0:T(8,128)(2,1)} %refs_0_.1, s32[2,1,96]{2,1,0:T(1,128)} %refs_1_.1, ...), custom_call_target="tpu_custom_call" | custom-call | tf_op jit(solution)/shard_map/pallas_call | solution.py:1435
  170.9 3.1 %shard_map.196 = (bf16[1,2,384,512]{3,2,1,0:T(8,128)(2,1)}, f32[1,2,384,512]{3,2,1,0:T(8,128)}, f32[1,512,128]{2,1,0:T(8,128)}, f32[1,9,128,128]{3,2,1,0:T(8,128...) custom-call(bf16[1,2,384,512]{3,2,1,0:T(8,128)(2,1)} %get-tuple-elem, ...), custom_call_target="tpu_custom_call" | custom-call | tf_op jit(solution)/shard_map/pallas_call | solution.py:1466

commit v5 on v4

--- a/solution.py
+++ b/solution.py
@@ -733,7 +733,11 @@
             inv = lax.rsqrt(sqs / count + NORM_EPS)
             keep[j, i, :, 0:width] = rows_tile(mean, inv, count)
 
-        spans = [slice(r0, r0 + 128) for r0 in range(0, R, 128)]
+        def parted(*twelfths):
+            at = [max(32, R * n // 12 // 32 * 32) for n in twelfths]
+            return [slice(a, b) for a, b in zip([0] + at, at + [R])]
+
+        spans, halves = parted(2, 7), parted(6)
 
         def rows_out(buf, at, rows, values):
             buf[at, m, rows] = values.astype(BF16)
@@ -756,12 +760,13 @@
                 xhat = raw[j, c, rows].astype(F32) * tile[2:3] + tile[3:4]
                 sb[c] = sb[c] + fold(g)
                 sg[c] = sg[c] + fold(g * xhat)
-            if rows is spans[-1]:
+            last = rows.stop == R
+            if last:
                 sums = sums_out(p, sb + sg)
             group = Group("mp", lambda: rs_r.at[p, pl.ds(0, n_mp - 1), rows])
             group.put(lambda t: rs_s.at[p, t, rows], lambda src: rs_r.at[p, src, rows])
             groups.append(group.close())
-            return sums if rows is spans[-1] else None
+            return sums if last else None
 
         def sums_out(p, parts):
             place = lax.broadcasted_iota(jnp.int32, (2 * n_mp, C), 0)
@@ -840,14 +845,12 @@
             return tile[0:1], tile[1:2], tile[2:3], gain, shift
 
         def taps_sum(src, flip, put):
-            for r0 in range(0, R, 128):
-                put(r0, lambda idx_list, lanes: sum(
-                    masks[(len(MASKS) - 2 - (idx // 2) * 2 + idx % 2) if flip else idx, r0:r0 + 128]
-                    * src[
-                        PAD + r0 + (-1 if flip else 1) * MASKS[idx][4]:
-                        PAD + r0 + (-1 if flip else 1) * MASKS[idx][4] + 128,
-                        lanes,
-                    ]
+            way = -1 if flip else 1
+            for rows in spans:
+                first_row, last_row = PAD + rows.start, PAD + rows.stop
+                put(rows, lambda idx_list, lanes: sum(
+                    masks[(len(MASKS) - 2 - (idx // 2) * 2 + idx % 2) if flip else idx, rows]
+                    * src[first_row + way * MASKS[idx][4]:last_row + way * MASKS[idx][4], lanes]
                     for idx in idx_list
                 ))
 
@@ -884,8 +887,8 @@
 
             inner_norm(j, 0, first, ag_a, fulla, hooks[1], needs[0], conv)
 
-            def put(r0, summed):
-                second[j, r0:r0 + 128] = sum(
+            def put(rows, summed):
+                second[j, rows] = sum(
                     summed([2 * k, 2 * k + 1], slice(k * C, (k + 1) * C)) for k in range(9)
                 )
 
@@ -1031,7 +1034,7 @@
 
             none = lambda: ([jnp.zeros((8, C), F32)] * n_mp, [jnp.zeros((8, C), F32)] * n_mp)
             h, carry = rs_parts(), none()
-            for rows in spans:
+            for rows in halves:
                 for r0 in range(rows.start, rows.stop, 32):
                     d_third(slice(r0, r0 + 32), 0)
                 out = dot(dth[rows], we[j].reshape(M, Wd), NT)
@@ -1069,12 +1072,9 @@
             h, carry = rs_parts(), none()
             sums_a = []
 
-            def put(r0, summed):
+            def put(rows, summed):
                 for k in range(9):
-                    dbuf[r0:r0 + 128, k * C:(k + 1) * C] = summed(
-                        [2 * k, 2 * k + 1], slice(None)
-                    ).astype(BF16)
-                rows = spans[r0 // 128]
+                    dbuf[rows, k * C:(k + 1) * C] = summed([2 * k, 2 * k + 1], slice(None)).astype(BF16)
                 out = dot(dbuf[rows], wsp[j].reshape(M, W9), NT)
                 sums_a.append(rs_rows_sums(h, j, 0, rows, out, carry))
 
@@ -1133,10 +1133,10 @@
                     d_input(rows)
             if j == 0:
                 reduce_to_sib(j)
-                d_input(spans[0])
-                d_input(spans[1])
+                for rows in spans[:-1]:
+                    d_input(rows)
                 reduce_to_dp(j)
-                for rows in spans[2:]:
+                for rows in spans[-1:]:
                     d_input(rows)
             to_section(lambda: ig.at[j], ig_hbm, j)
 
@@ -1362,7 +1362,7 @@
     vmem = lambda shape, dtype: pltpu.VMEM(shape, dtype)
     scratch = [
         pltpu.SemaphoreType.DMA((3,)),
-        pltpu.SemaphoreType.DMA((97,)),
+        pltpu.SemaphoreType.DMA((95,)),
         pltpu.SemaphoreType.DMA((21,)),
         pltpu.SemaphoreType.REGULAR,
         vmem((Wd, Cd), F32),

time: 174 us -> 169 us (0.971)
  Pallas kernels: 173 us -> 168 us
    pallas_call x1, Pallas kernels: 170 us -> 165 us  [fused_device(): pl.pallas_call(make_kernel(sizes), out_shape=(whole((1, 2, R, Wd), BF16),...]
where the time goes in v5:
time: 169 us; the launch traced here: 168 us
  Pallas kernels  168 us (99%)
    pallas_call x1, Pallas kernels, fused_device(): pl.pallas_call(make_kernel(sizes), out_shape=(whole((1, 2, R, Wd), BF16),...  165 us

profile of v5, /device:TPU:0, one launch (start us, length us, event | category | flops | bytes accessed | tf_op | source)
XLA Modules:
  0.0 168.5 jit_solution(11618292078449868731)
XLA Ops:
  0.6 164.6 %shard_map.195 = (bf16[1,2,384,512]{3,2,1,0:T(8,128)(2,1)}, f32[1,2,384,512]{3,2,1,0:T(8,128)}, f32[1,512,128]{2,1,0:T(8,128)}, f32[1,9,128,128]{3,2,1,0:T(8,128...) custom-call(bf16[2,384,512]{2,1,0:T(8,128)(2,1)} %refs_0_.1, s32[2,1,96]{2,1,0:T(1,128)} %refs_1_.1, ...), custom_call_target="tpu_custom_call" | custom-call | tf_op jit(solution)/shard_map/pallas_call | solution.py:1435
  165.2 3.1 %shard_map.196 = (bf16[1,2,384,512]{3,2,1,0:T(8,128)(2,1)}, f32[1,2,384,512]{3,2,1,0:T(8,128)}, f32[1,512,128]{2,1,0:T(8,128)}, f32[1,9,128,128]{3,2,1,0:T(8,128...) custom-call(bf16[1,2,384,512]{3,2,1,0:T(8,128)(2,1)} %get-tuple-elem, ...), custom_call_target="tpu_custom_call" | custom-call | tf_op jit(solution)/shard_map/pallas_call | solution.py:1466

commit v6 on v5

--- a/solution.py
+++ b/solution.py
@@ -1133,10 +1133,8 @@
                     d_input(rows)
             if j == 0:
                 reduce_to_sib(j)
-                for rows in spans[:-1]:
-                    d_input(rows)
                 reduce_to_dp(j)
-                for rows in spans[-1:]:
+                for rows in spans:
                     d_input(rows)
             to_section(lambda: ig.at[j], ig_hbm, j)
 
@@ -1230,6 +1228,7 @@
         def heads_of(t):
             return hd[:, t].reshape(classes, Wd)
 
+        logit_group = Group("mp", lambda: lg_r.at[pl.ds(0, n_mp - 1)])
         for c in range(n_mp):
             act_c(slice(c * RM, (c + 1) * RM))
             rows = act1[c * RM:(c + 1) * RM]
@@ -1237,9 +1236,14 @@
                 lg_s[c, :, t * classes:(t + 1) * classes] = dot(rows, heads_of(t), NT).astype(
                     lg_s.dtype
                 )
-        base = spread(
-            "mp", lambda t: lg_s.at[t], lambda src: lg_r.at[src], lambda: lg_r.at[pl.ds(0, n_mp - 1)]
-        )
+
+            @pl.when(m != c)
+            def _():
+                put_to(
+                    lg_s.at[c], lg_r.at[m], logit_group.ssem, logit_group.rsem, mp_dev(c)
+                )
+
+        base = logit_group.close()
         to_section(lambda: act1, act_hbm, 1)
         settle(l_thr)
         prepare(1)

time: 169 us -> 168 us (level)
  no operation moved by 1% of the time
where the time goes in v6:
time: 168 us
  Pallas kernels  167 us (99%)
    pallas_call x1, Pallas kernels, fused_device(): pl.pallas_call(make_kernel(sizes), out_shape=(whole((1, 2, R, Wd), BF16),...  164 us

profile of v6, /device:TPU:0, one launch (start us, length us, event | category | flops | bytes accessed | tf_op | source)
XLA Modules:
  0.0 168.1 jit_solution(13187585872981059651)
XLA Ops:
  0.6 164.2 %shard_map.195 = (bf16[1,2,384,512]{3,2,1,0:T(8,128)(2,1)}, f32[1,2,384,512]{3,2,1,0:T(8,128)}, f32[1,512,128]{2,1,0:T(8,128)}, f32[1,9,128,128]{3,2,1,0:T(8,128...) custom-call(bf16[2,384,512]{2,1,0:T(8,128)(2,1)} %refs_0_.1, s32[2,1,96]{2,1,0:T(1,128)} %refs_1_.1, ...), custom_call_target="tpu_custom_call" | custom-call | tf_op jit(solution)/shard_map/pallas_call | solution.py:1439
  164.8 3.1 %shard_map.196 = (bf16[1,2,384,512]{3,2,1,0:T(8,128)(2,1)}, f32[1,2,384,512]{3,2,1,0:T(8,128)}, f32[1,512,128]{2,1,0:T(8,128)}, f32[1,9,128,128]{3,2,1,0:T(8,128...) custom-call(bf16[1,2,384,512]{3,2,1,0:T(8,128)(2,1)} %get-tuple-elem, ...), custom_call_target="tpu_custom_call" | custom-call | tf_op jit(solution)/shard_map/pallas_call | solution.py:1470

commit v7 on v6

--- a/solution.py
+++ b/solution.py
@@ -1250,6 +1250,9 @@
         settle(base)
         here = pl.ds(pl.multiple_of(m * RM, RM), RM)
         lv = wide(live[here], classes)
+        group = Group(
+            "mp", lambda: dl.at[pl.ds(0, n_mp - 1)], slot_of=lambda src: dl.at[src]
+        )
         for t in range(tasks):
             lanes = slice(t * classes, (t + 1) * classes)
             logit = lg_s[m, :, lanes].astype(F32)
@@ -1260,10 +1263,7 @@
             ids = lax.broadcasted_iota(jnp.int32, (RM, classes), 1).astype(F32)
             hot = (ids == labc[here, t:t + 1]).astype(F32)
             dl[m, :, lanes] = (LOSS_WEIGHT * lv * (soft - hot)).astype(BF16)
-        group = Group(
-            "mp", lambda: dl.at[pl.ds(0, n_mp - 1)], slot_of=lambda src: dl.at[src]
-        )
-        group.put(lambda t: dl.at[m], lambda src: dl.at[src])
+            group.put(lambda t: dl.at[m, :, lanes], lambda src: dl.at[src, :, lanes])
         group.close()
 
         def merge_block(c, sums):

time: 168 us -> 173 us (1.030)
  Pallas kernels: 167 us -> 172 us
    pallas_call x1, Pallas kernels: 164 us -> 169 us  [fused_device(): pl.pallas_call(make_kernel(sizes), out_shape=(whole((1, 2, R, Wd), BF16),...]
where the time goes in v7:
time: 173 us
  Pallas kernels  172 us (99%)
    pallas_call x1, Pallas kernels, fused_device(): pl.pallas_call(make_kernel(sizes), out_shape=(whole((1, 2, R, Wd), BF16),...  169 us

profile of v7, /device:TPU:0, one launch (start us, length us, event | category | flops | bytes accessed | tf_op | source)
XLA Modules:
  0.0 172.7 jit_solution(16043610332927024795)
XLA Ops:
  0.6 168.8 %shard_map.195 = (bf16[1,2,384,512]{3,2,1,0:T(8,128)(2,1)}, f32[1,2,384,512]{3,2,1,0:T(8,128)}, f32[1,512,128]{2,1,0:T(8,128)}, f32[1,9,128,128]{3,2,1,0:T(8,128...) custom-call(bf16[2,384,512]{2,1,0:T(8,128)(2,1)} %refs_0_.1, s32[2,1,96]{2,1,0:T(1,128)} %refs_1_.1, ...), custom_call_target="tpu_custom_call" | custom-call | tf_op jit(solution)/shard_map/pallas_call | solution.py:1439
  169.5 3.1 %shard_map.196 = (bf16[1,2,384,512]{3,2,1,0:T(8,128)(2,1)}, f32[1,2,384,512]{3,2,1,0:T(8,128)}, f32[1,512,128]{2,1,0:T(8,128)}, f32[1,9,128,128]{3,2,1,0:T(8,128...) custom-call(bf16[1,2,384,512]{3,2,1,0:T(8,128)(2,1)} %get-tuple-elem, ...), custom_call_target="tpu_custom_call" | custom-call | tf_op jit(solution)/shard_map/pallas_call | solution.py:1470
